TPU v7x, 32 devices: a whole 2x2x4 slice. The times are simulated.
32 devices in a mesh: groups: 2 (over y), sector: 4 (over z), op: 4 (over x, core).
Axes of the slice: x: 2, y: 2, z: 4, core: 2. Of those that a mesh axis runs over, the one named last changes fastest.
Arguments:
- start_vector: bfloat16 [256, 4096], P(('groups', 'sector')), parts along dimension 0, may hold values from -6 to 6
- extents: int32 [256, 2], P(('groups', 'sector')), parts along dimension 0, may hold values from 16 to 64, as said below
- offsets: int32 [64], P('groups'), parts along dimension 0, may hold values from 0 to 3, as said below
- env_left: bfloat16 [256, 28, 4096], P(('groups', 'sector'), 'op'), parts along dimension 0, may hold values from -0.75 to 0.75
- env_right: bfloat16 [256, 28, 4096], P(('groups', 'sector'), 'op'), parts along dimension 0, may hold values from -0.75 to 0.75
- channel_mask: int32 [256, 28], P(('groups', 'sector'), 'op'), parts along dimension 0, may hold values 0 or 1
Outputs:
- residual: float32 [256, 4096], P(('groups', 'sector')), parts along dimension 0
- projections: float32 [6, 3], P('groups'), parts along dimension 0
There are 2 independent parts, one for each index of `groups`. A program takes and returns all parts, laid end to end along the dimension named above; each array names one. Nothing has to cross between parts.
Inputs may be any that keep to these rules, and one draw needn't show every extreme that they name: `extents`: every block has at least 16 rows and columns, and block 0 has 64 rows. The environments of home slot j of sector device h are held by sector device (h + offsets[j]) mod (4), in its slot j. Each value occurs in offsets exactly 8 times or not at all.
All inputs are finite; a program needn't handle non-finite values. No bound on the sum of `channel_mask` on one device may be relied on, other than what follows from the above.
Results may differ from a plain program's by a relative error of at most 0.0077.
Values may be sent and summed in bfloat16 or wider, within the bound.
No kernel may reach another device: no remote copies, remote signals or barrier semaphores. Data moves between devices by JAX's collectives and lax.ppermute only.
A program may use at most 64 MiB of HBM per device.

v0:
```python
import jax
import jax.numpy as jnp
from jax import lax
from jax.sharding import PartitionSpec as P

B = 64
ITERS = 3


def pack_rows(data, index, nodes, cap):
    slots = data.shape[0]
    hit = jnp.arange(nodes * cap, dtype=jnp.int32)[:, None] == index[None, :]
    source = jnp.sum(jnp.where(hit, jnp.arange(slots, dtype=jnp.int32)[None, :], 0), axis=1)
    filled = jnp.any(hit, axis=1)
    rows = jnp.take(data, source, axis=0)
    rows = jnp.where(filled[:, None], rows, jnp.zeros_like(rows))
    return rows.reshape(nodes, cap, data.shape[1])


def unpack_rows(arrived, index):
    flat = arrived.reshape(arrived.shape[0] * arrived.shape[1], arrived.shape[2])
    return jnp.take(flat, index, axis=0)


def on_device(start_vector, extents, offsets, env_left, env_right, channel_mask):
    nodes = lax.axis_size("sector")
    here_index = lax.axis_index("sector")
    slots = start_vector.shape[0]
    cap = max(1, slots // nodes)
    chans = env_left.shape[1]
    count = float(slots * nodes * B * B)
    slot_ids = jnp.arange(slots, dtype=jnp.int32)
    same = offsets[:, None] == offsets[None, :]
    earlier = slot_ids[None, :] < slot_ids[:, None]
    rank = jnp.sum((same & earlier).astype(jnp.int32), axis=1)
    send_index = (here_index + offsets) % nodes * cap + rank
    recv_index = (here_index - offsets) % nodes * cap + rank
    position = jnp.arange(B * B, dtype=jnp.int32)
    inside = ((position // B)[None, :] < extents[:, 0:1]) & (
        (position % B)[None, :] < extents[:, 1:2]
    )
    mask = inside.astype(jnp.float32)
    left = env_left.reshape(slots, chans, B, B)
    right_wide = env_right.reshape(slots, chans, B, B).astype(jnp.float32)
    chan = channel_mask.astype(jnp.float32)

    def squares(vector):
        return lax.psum(jnp.sum(vector * vector), "sector") / count

    def correlation_table(basis, image):
        local = [jnp.sum(vector * image) for vector in basis]
        local = local + [jnp.zeros((), jnp.float32)] * (ITERS - len(basis))
        return lax.psum(jnp.stack(local), "sector") / count

    masked = mask * start_vector.astype(jnp.float32)
    basis = [masked / jnp.sqrt(squares(masked) + 1e-06)]
    projections = jnp.zeros((ITERS, ITERS), jnp.float32)
    residual = masked
    for step in range(ITERS):
        moving = pack_rows(basis[step].astype(jnp.bfloat16), send_index, nodes, cap)
        arrived = lax.all_to_all(moving, "sector", split_axis=0, concat_axis=0, tiled=True)
        blocks = unpack_rows(arrived, recv_index).reshape(slots, B, B)
        inner = jnp.einsum("swab,sbc->swac", left, blocks, preferred_element_type=jnp.float32)
        inner = inner * chan[:, :, None, None]
        partial_image = jnp.einsum(
            "swac,swdc->sad", inner, right_wide, precision=lax.Precision.HIGHEST
        )
        total = lax.psum(partial_image.reshape(slots, B * B), "op")
        going = pack_rows(total, recv_index, nodes, cap)
        returned = lax.all_to_all(going, "sector", split_axis=0, concat_axis=0, tiled=True)
        apply_image = unpack_rows(returned, send_index)
        image = apply_image * mask
        coeffs = correlation_table(basis, image)
        residual = image
        for index in range(step + 1):
            projections = projections.at[index, step].set(coeffs[index])
            residual = residual - coeffs[index] * basis[index]
        if step + 1 < ITERS:
            basis.append(residual / jnp.sqrt(squares(residual) + 1e-06))
    return (residual, projections)


def solution(mesh):
    return jax.shard_map(
        on_device,
        mesh=mesh,
        in_specs=(
            P(("groups", "sector"), None),
            P(("groups", "sector"), None),
            P("groups"),
            P(("groups", "sector"), "op", None),
            P(("groups", "sector"), "op", None),
            P(("groups", "sector"), "op"),
        ),
        out_specs=(P(("groups", "sector"), None), P("groups", None)),
        check_vma=False,
    )
```

profile of v0, /device:TPU:0, one launch (start us, length us, event | category | flops | bytes accessed | tf_op | source)
XLA Modules:
  0.0 336.1 jit_solution(11097717133061879836)
XLA Ops:
  7.2 1.0 convert_reduce_fusion
  9.7 1.8 multiply_reduce_fusion.8
  11.6 14.1 %psum.63 = f32[]{:T(128)} all-reduce(f32[]{:T(128)} %multiply_reduce_fusion.8), channel_id=1, replica_groups=mesh['groups'=2,'sector'=4,'op'=4] {'sector'}, use_global_device_ids=true, to_apply=%region_4.5 | all-reduce | flops 1 | bytes 8 | tf_op jit(solution)/shard_map/psum | solution.py:48
  26.4 1.1 fusion.63
  29.1 3.4 %all-to-all-start = ((bf16[4,8,4096]{2,1,0:T(8,128)(2,1)}), bf16[4,8,4096]{2,1,0:T(8,128)(2,1)S(1)}, u32[]{:S(2)}, u32[]{:S(2)}) async-start(bf16[4,8,4096]{2,1,0:T(8,128)(2,1)} %fusion.45), calls=%async_computation | async-start | bytes 524288 | tf_op jit(solution)/shard_map/all_to_all | solution.py:61
  32.7 5.0 %reshape.293 = bf16[32,7,64,64]{3,2,0,1:T(8,128)(2,1)} reshape(bf16[32,7,4096]{2,0,1:T(8,128)(2,1)S(1)} %copy-done.4) | data formatting | bytes 3670016 | tf_op jit(solution)/shard_map/reshape | solution.py:44
  37.6 6.3 %reshape.292 = bf16[32,7,64,64]{3,2,0,1:T(8,128)(2,1)} reshape(bf16[32,7,4096]{2,0,1:T(8,128)(2,1)} %param.25) | data formatting | bytes 3670016 | tf_op jit(solution)/shard_map/reshape | solution.py:43
  45.6 3.3 fusion.16
  48.9 4.4 %fusion.21 = f32[32,64,64]{2,1,0:T(8,128)S(1)} fusion(bf16[32,7,64,64]{3,2,0,1:T(8,128)(2,1)S(1)} %copy-done, f32[32,64,7,64]{1,3,2,0:T(8,128)S(1)} %fusion.16, f32[32,7]{1,0:T(8,128)S(1)} %copy.12), kind=kOutput, calls=%fused_computation.33 | convolution fusion | flops 705560576 | bytes 6030208 | tf_op jit(solution)/shard_map/swac,swdc->sad/dot_general | solution.py:65
  53.3 1.2 reshape.294
  54.5 34.7 %all-reduce.6.cloned.1.call-done = f32[32,4096]{1,0:T(8,128)} async-done(((f32[32,4096]{1,0:T(8,128)}), f32[32,4096]{1,0:T(8,128)}) %all-reduce.6.cloned.1.call-update) | async-done | bytes 524304 | tf_op jit(solution)/shard_map/psum | solution.py:68
  89.2 2.0 gather_fusion.2
  91.2 0.9 fusion.41
  92.1 4.6 %all-to-all-start.1 = ((f32[4,8,4096]{2,1,0:T(8,128)}), f32[4,8,4096]{2,1,0:T(8,128)S(1)}, u32[]{:S(2)}, u32[]{:S(2)}) async-start(f32[4,8,4096]{2,1,0:T(8,128)} %fusion.41), calls=%async_computation.1 | async-start | bytes 1048576 | tf_op jit(solution)/shard_map/all_to_all | solution.py:70
  96.7 13.5 %all-to-all-done.1 = f32[4,8,4096]{2,1,0:T(8,128)S(1)} async-done(((f32[4,8,4096]{2,1,0:T(8,128)}), f32[4,8,4096]{2,1,0:T(8,128)S(1)}, u32[]{:S(2)}, u32[]{:S(2)}) %all-to-all-start.1) | async-done | bytes 524320 | tf_op jit(solution)/shard_map/all_to_all | solution.py:70
  111.0 0.8 multiply_reduce_fusion.7
  112.5 9.8 %psum.65 = f32[3]{0:T(128)S(1)} all-reduce(f32[3]{0:T(128)S(1)} %stack.28), channel_id=1, replica_groups=mesh['groups'=2,'sector'=4,'op'=4] {'sector'}, use_global_device_ids=true, to_apply=%region_9.12 | all-reduce | flops 3 | bytes 24 | tf_op jit(solution)/shard_map/psum | solution.py:53
  122.3 0.9 multiply_reduce_fusion.6
  123.2 9.5 %psum.66 = f32[]{:T(128)} all-reduce(f32[]{:T(128)} %multiply_reduce_fusion.6), channel_id=1, replica_groups=mesh['groups'=2,'sector'=4,'op'=4] {'sector'}, use_global_device_ids=true, to_apply=%region_11.14 | all-reduce | flops 1 | bytes 8 | tf_op jit(solution)/shard_map/psum | solution.py:48
  134.6 9.7 %all_to_all.30 = bf16[4,8,4096]{2,1,0:T(8,128)(2,1)S(1)} all-to-all(bf16[4,8,4096]{2,1,0:T(8,128)(2,1)S(1)} %fusion.44), channel_id=1, replica_groups=mesh['groups'=2,'sector'=4,'op'=4] {'sector'}, dimensions={0} | all-to-all | bytes 524288 | tf_op jit(solution)/shard_map/all_to_all | solution.py:61
  145.6 3.3 fusion.14
  148.9 4.4 %fusion.26 = f32[32,64,64]{2,1,0:T(8,128)S(1)} fusion(bf16[32,7,64,64]{3,2,0,1:T(8,128)(2,1)S(1)} %copy-done.1, f32[32,64,7,64]{1,3,2,0:T(8,128)S(1)} %fusion.14, f32[32,7]{1,0:T(8,128)S(1)} %copy.12), kind=kOutput, calls=%fused_computation.34 | convolution fusion | flops 705560576 | bytes 6030208 | tf_op jit(solution)/shard_map/swac,swdc->sad/dot_general | solution.py:65
  153.3 1.2 reshape.300
  154.6 31.6 %all-reduce.8.cloned.1.call-done = f32[32,4096]{1,0:T(8,128)} async-done(((f32[32,4096]{1,0:T(8,128)}), f32[32,4096]{1,0:T(8,128)}) %all-reduce.8.cloned.1.call-update) | async-done | bytes 524304 | tf_op jit(solution)/shard_map/psum | solution.py:68
  186.1 2.0 gather_fusion.6
  188.3 18.0 %all_to_all.31 = f32[4,8,4096]{2,1,0:T(8,128)S(1)} all-to-all(f32[4,8,4096]{2,1,0:T(8,128)S(1)} %fusion.40), channel_id=1, replica_groups=mesh['groups'=2,'sector'=4,'op'=4] {'sector'}, dimensions={0} | all-to-all | bytes 1048576 | tf_op jit(solution)/shard_map/all_to_all | solution.py:70
  207.0 1.0 multiply_reduce_fusion.5
  207.9 1.4 pad_maximum_fusion
  209.3 9.8 %psum.68 = f32[3]{0:T(128)S(1)} all-reduce(f32[3]{0:T(128)S(1)} %pad_maximum_fusion), channel_id=1, replica_groups=mesh['groups'=2,'sector'=4,'op'=4] {'sector'}, use_global_device_ids=true, to_apply=%region_15.18 | all-reduce | flops 3 | bytes 24 | tf_op jit(solution)/shard_map/psum | solution.py:53
  219.8 2.2 multiply_reduce_fusion.3
  222.0 9.5 %psum.69 = f32[]{:T(128)} all-reduce(f32[]{:T(128)} %get-tuple-element.81), channel_id=1, replica_groups=mesh['groups'=2,'sector'=4,'op'=4] {'sector'}, use_global_device_ids=true, to_apply=%region_17.20 | all-reduce | flops 1 | bytes 8 | tf_op jit(solution)/shard_map/psum | solution.py:48
  233.1 9.7 %all_to_all.32 = bf16[4,8,4096]{2,1,0:T(8,128)(2,1)S(1)} all-to-all(bf16[4,8,4096]{2,1,0:T(8,128)(2,1)S(1)} %fusion.43), channel_id=1, replica_groups=mesh['groups'=2,'sector'=4,'op'=4] {'sector'}, dimensions={0} | all-to-all | bytes 524288 | tf_op jit(solution)/shard_map/all_to_all | solution.py:61
  244.1 3.3 fusion.12
  247.4 4.4 %fusion.31 = f32[32,64,64]{2,1,0:T(8,128)S(1)} fusion(bf16[32,7,64,64]{3,2,0,1:T(8,128)(2,1)S(1)} %copy-done.2, f32[32,64,7,64]{1,3,2,0:T(8,128)S(1)} %fusion.12, f32[32,7]{1,0:T(8,128)S(1)} %copy.12), kind=kOutput, calls=%fused_computation.35 | convolution fusion | flops 705560576 | bytes 6030208 | tf_op jit(solution)/shard_map/swac,swdc->sad/dot_general | solution.py:65
  251.8 1.2 reshape.306
  253.0 31.7 %all-reduce.10.cloned.1.call-done = f32[32,4096]{1,0:T(8,128)} async-done(((f32[32,4096]{1,0:T(8,128)}), f32[32,4096]{1,0:T(8,128)}) %all-reduce.10.cloned.1.call-update) | async-done | bytes 524304 | tf_op jit(solution)/shard_map/psum | solution.py:68
  284.7 2.0 gather_fusion.10
  286.7 0.9 fusion.39
  287.6 4.6 %all-to-all-start.5 = ((f32[4,8,4096]{2,1,0:T(8,128)}), f32[4,8,4096]{2,1,0:T(8,128)S(1)}, u32[]{:S(2)}, u32[]{:S(2)}) async-start(f32[4,8,4096]{2,1,0:T(8,128)} %fusion.39), calls=%async_computation.5 | async-start | bytes 1048576 | tf_op jit(solution)/shard_map/all_to_all | solution.py:70
  294.9 1.8 dynamic-slice.42
  298.5 1.3 scatter.21
  300.7 5.1 %all-to-all-done.5 = f32[4,8,4096]{2,1,0:T(8,128)S(1)} async-done(((f32[4,8,4096]{2,1,0:T(8,128)}), f32[4,8,4096]{2,1,0:T(8,128)S(1)}, u32[]{:S(2)}, u32[]{:S(2)}) %all-to-all-start.5) | async-done | bytes 524320 | tf_op jit(solution)/shard_map/all_to_all | solution.py:70
  306.5 1.1 multiply_reduce_fusion.2
  307.7 2.0 pad_maximum_fusion.1
  309.7 1.8 dynamic-slice.43
  311.4 9.8 %psum.71 = f32[3]{0:T(128)S(1)} all-reduce(f32[3]{0:T(128)S(1)} %pad_maximum_fusion.1), channel_id=1, replica_groups=mesh['groups'=2,'sector'=4,'op'=4] {'sector'}, use_global_device_ids=true, to_apply=%region_22.25 | all-reduce | flops 3 | bytes 24 | tf_op jit(solution)/shard_map/psum | solution.py:53
  323.8 1.3 scatter.25
  326.6 2.9 multiply_subtract_fusion
  (77 shorter events, 18.8 us)
Async XLA Ops:
  7.2 25.5 %copy-start.4 = (bf16[32,7,4096]{2,0,1:T(8,128)(2,1)S(1)}, bf16[32,7,4096]{2,0,1:T(8,128)(2,1)}, u32[]{:S(2)}) copy-start(bf16[32,7,4096]{2,0,1:T(8,128)(2,1)} %param.26) | copy-start | bytes 5505028
  29.1 15.1 %all-to-all-start = ((bf16[4,8,4096]{2,1,0:T(8,128)(2,1)}), bf16[4,8,4096]{2,1,0:T(8,128)(2,1)S(1)}, u32[]{:S(2)}, u32[]{:S(2)}) async-start(bf16[4,8,4096]{2,1,0:T(8,128)(2,1)} %fusion.45), calls=%async_computation | async-start | bytes 524288 | tf_op jit(solution)/shard_map/all_to_all | solution.py:61
  32.5 56.7 %all-reduce.6.cloned.1.call-start = ((), (), s32[]{:S(2)}) async-start(), calls=%async_computation.6 | async-start | bytes 1048576 | tf_op jit(solution)/shard_map/psum | solution.py:68
  37.6 6.3 %copy-start.6 = (s32[32,7]{0,1:T(8,128)S(1)}, s32[32,7]{0,1:T(8,128)}, u32[]{:S(2)}) copy-start(s32[32,7]{0,1:T(8,128)} %param.27) | copy-start | bytes 2692
  45.6 3.3 copy-start
  91.2 19.8 %copy-start.3 = (bf16[32,4096]{1,0:T(8,128)(2,1)S(1)}, bf16[32,4096]{1,0:T(8,128)(2,1)}, u32[]{:S(2)}) copy-start(bf16[32,4096]{1,0:T(8,128)(2,1)} %param.22) | copy-start | bytes 786436
  92.1 18.2 %all-to-all-start.1 = ((f32[4,8,4096]{2,1,0:T(8,128)}), f32[4,8,4096]{2,1,0:T(8,128)S(1)}, u32[]{:S(2)}, u32[]{:S(2)}) async-start(f32[4,8,4096]{2,1,0:T(8,128)} %fusion.41), calls=%async_computation.1 | async-start | bytes 1048576 | tf_op jit(solution)/shard_map/all_to_all | solution.py:70
  96.7 89.4 %all-reduce.8.cloned.1.call-start = ((), (), s32[]{:S(2)}) async-start(), calls=%async_computation.7 | async-start | bytes 1048576 | tf_op jit(solution)/shard_map/psum | solution.py:68
  145.6 3.3 copy-start.1
  154.5 130.2 %all-reduce.10.cloned.1.call-start = ((), (), s32[]{:S(2)}) async-start(), calls=%async_computation.8 | async-start | bytes 1048576 | tf_op jit(solution)/shard_map/psum | solution.py:68
  244.1 3.3 copy-start.2
  287.6 18.2 %all-to-all-start.5 = ((f32[4,8,4096]{2,1,0:T(8,128)}), f32[4,8,4096]{2,1,0:T(8,128)S(1)}, u32[]{:S(2)}, u32[]{:S(2)}) async-start(f32[4,8,4096]{2,1,0:T(8,128)} %fusion.39), calls=%async_computation.5 | async-start | bytes 1048576 | tf_op jit(solution)/shard_map/all_to_all | solution.py:70
  326.6 3.0 copy-start.5
Sparse Core Ops, SparseCore 0:
  54.6 34.5 all-reduce.5
  154.6 31.4 all-reduce.7
  253.1 31.5 all-reduce.9
where the time goes:
time: 337 us; the launch traced here: 336 us
  waiting for transfers between devices  117 us (35%)
  blocking collectives  99.9 us (30%)
  local copies, waits for them, and re-layouts  41.3 us (12%)
  matrix products  23.1 us (7%)
  other arithmetic  22.4 us (7%)
  between operations  20.1 us (6%)
  starting transfers between devices  12.7 us (4%)
    psum x3, waiting for transfers between devices, on_device(): total = lax.psum(partial_image.reshape(slots, B * B), 'op')  97.9 us
    psum x3, blocking collectives, squares(): return lax.psum(jnp.sum(vector * vector), 'sector') / count  33.1 us
    psum x3, blocking collectives, correlation_table(): return lax.psum(jnp.stack(local), 'sector') / count  29.4 us
    all_to_all x2, blocking collectives, on_device(): lax.all_to_all(moving, 'sector', split_axis=0, concat_axis=0, tiled=True)  19.4 us
    all_to_all x2, waiting for transfers between devices, on_device(): lax.all_to_all(going, 'sector', split_axis=0, concat_axis=0, tiled=True)  18.6 us
    all_to_all x1, blocking collectives, on_device(): lax.all_to_all(going, 'sector', split_axis=0, concat_axis=0, tiled=True)  18 us
    dot_general x3, matrix products, on_device(): jnp.einsum('swac,swdc->sad', inner, right_wide, precision=lax.Precision.H...  13.3 us
    dot_general x3, matrix products, on_device(): jnp.einsum('swab,sbc->swac', left, blocks, preferred_element_type=jnp.flo...  9.84 us
  transfers between devices with their start and end apart: 6, of which 5 were waited for; matrix products, arithmetic and copies ran while one was open for 5% of the time, Pallas kernels for 0%

commit v1 on v0

--- a/solution.py
+++ b/solution.py
@@ -1,10 +1,418 @@
 import jax
 import jax.numpy as jnp
 from jax import lax
+from jax.experimental import pallas as pl
+from jax.experimental.pallas import tpu as pltpu
 from jax.sharding import PartitionSpec as P
 
 B = 64
 ITERS = 3
+HALF = 32
+LANES = 128
+WIDE = 4 * LANES
+F32 = jnp.float32
+BF16 = jnp.bfloat16
+VMEM_LIMIT = 48 * 1024 * 1024
+
+
+def iota(shape, dim):
+    return lax.broadcasted_iota(jnp.int32, shape, dim)
+
+
+def sorted_column(c):
+    return (c % 2) * HALF + c // 2
+
+
+def lane_order(transposed):
+    row = iota((LANES, LANES), 1 if transposed else 0)
+    col = iota((LANES, LANES), 0 if transposed else 1)
+    to = row // B * B + sorted_column(row % B)
+    return (to == col).astype(F32).astype(BF16)
+
+
+def pair_order():
+    row = iota((2 * LANES, 2 * LANES), 0)
+    col = iota((2 * LANES, 2 * LANES), 1)
+    w, p, c = row // LANES, row // B % 2, row % B
+    return (p * LANES + w * B + sorted_column(c) == col).astype(F32).astype(BF16)
+
+
+def inside(rows, cols):
+    lane = iota((HALF, LANES), 1)
+    a = 2 * iota((HALF, LANES), 0) + lane // B
+    kept = lane % B
+    c = 2 * (kept % HALF) + kept // HALF
+    return jnp.where((a < rows) & (c < cols), 1.0, 0.0).astype(F32)
+
+
+def prepare_kernel(index_ref, chan_ref, left_ref, right_ref, out_ref, raw, turn, sems):
+    slots = out_ref.shape[1]
+    chans = raw.shape[2]
+
+    def fetch(s, t):
+        source = (left_ref, right_ref)[t]
+        return pltpu.make_async_copy(source.at[index_ref[s]], raw.at[t, s], sems.at[t, s])
+
+    for s in range(slots):
+        for t in range(2):
+            fetch(s, t).start()
+    order = pair_order()
+    blank = jnp.zeros((HALF, LANES), F32)
+
+    def body(s, carry):
+        for t in range(2):
+            fetch(s, t).wait()
+            rows = raw[t, s].astype(F32)
+            for i in range(HALF):
+                turn[t, pl.ds(8 * i, chans), :] = rows[:, i * LANES : (i + 1) * LANES]
+            parts = []
+            for w in range(8):
+                if w >= chans:
+                    parts.append(blank)
+                    continue
+                part = turn[t, pl.ds(w, HALF, stride=8), :]
+                if t == 0:
+                    part = part * chan_ref[index_ref[s], w].astype(F32)
+                parts.append(part)
+            pairs = [jnp.concatenate(parts[g : g + 2], axis=1) for g in range(0, 8, 2)]
+            mixed = jnp.dot(
+                jnp.concatenate(pairs, axis=0).astype(BF16), order, preferred_element_type=F32
+            ).astype(BF16)
+            for g in range(4):
+                for p in range(2):
+                    out_ref[t, s, p * HALF : (p + 1) * HALF, g * LANES : (g + 1) * LANES] = mixed[
+                        g * HALF : (g + 1) * HALF, p * LANES : (p + 1) * LANES
+                    ]
+        return carry
+
+    lax.fori_loop(0, slots, body, 0)
+
+
+def prepare(index, chan, left, right):
+    slots = index.shape[0]
+    chans = left.shape[1]
+    smem = pl.BlockSpec(memory_space=pltpu.SMEM)
+    hbm = pl.BlockSpec(memory_space=pl.ANY)
+    return pl.pallas_call(
+        prepare_kernel,
+        out_shape=jax.ShapeDtypeStruct((2, slots, B, WIDE), BF16),
+        in_specs=[smem, smem, hbm, hbm],
+        out_specs=pl.BlockSpec(memory_space=pltpu.VMEM),
+        scratch_shapes=[
+            pltpu.VMEM((2, slots, chans, B * B), BF16),
+            pltpu.VMEM((2, 8 * HALF, LANES), F32),
+            pltpu.SemaphoreType.DMA((2, slots)),
+        ],
+        compiler_params=pltpu.CompilerParams(vmem_limit_bytes=VMEM_LIMIT),
+        name="prepare",
+    )(index, chan, left, right)
+
+
+def block_diagonal(x):
+    low = iota((HALF, LANES), 1) < B
+    swapped = pltpu.roll(x, B, 1)
+    zero = jnp.zeros_like(x)
+    two = jnp.concatenate(
+        [
+            jnp.where(low, x, zero),
+            jnp.where(low, swapped, zero),
+            jnp.where(low, zero, swapped),
+            jnp.where(low, zero, x),
+        ],
+        axis=0,
+    )
+    blank = jnp.zeros_like(two)
+    return jnp.concatenate(
+        [jnp.concatenate([two, blank], axis=1), jnp.concatenate([blank, two], axis=1)], axis=0
+    )
+
+
+def split(x):
+    high = x.astype(BF16)
+    return high, (x - high.astype(F32)).astype(BF16)
+
+
+def dot_t(a, b):
+    return lax.dot_general(a, b, (((1,), (1,)), ((), ())), preferred_element_type=F32)
+
+
+def product_slot(x, s, env_refs, out_ref, exact):
+    diag_high, diag_low = split(block_diagonal(x))
+    total = None
+    for env in env_refs:
+        for g in range(2):
+            lanes = pl.ds(g * 2 * LANES, 2 * LANES)
+            left = env[0, s, :, lanes]
+            inner = jnp.dot(left, diag_high, preferred_element_type=F32)
+            if not exact:
+                inner = inner + jnp.dot(left, diag_low, preferred_element_type=F32)
+            high, low = split(inner)
+            right = env[1, s, :, lanes]
+            part = dot_t(high, right) + dot_t(low, right)
+            total = part if total is None else total + part
+    out_ref[s] = jnp.concatenate([total[:HALF], total[HALF:]], axis=1)
+
+
+def start_kernel(scale_ref, ext_ref, near_ref, far_ref, keep_ref, got_ref, q_ref, y_ref, turn):
+    slots = q_ref.shape[0]
+    half = slots // 2
+    for t, ref in enumerate((near_ref, far_ref)):
+        rows = ref[...].astype(F32)
+        for i in range(HALF):
+            turn[pl.ds(slots * i + half * t, half), :] = rows[:, i * LANES : (i + 1) * LANES]
+    order = lane_order(False)
+    for s in range(slots):
+        x = turn[pl.ds(s, HALF, stride=slots), :].astype(BF16)
+        x = jnp.dot(x, order, preferred_element_type=F32)
+        q_ref[s] = x * inside(ext_ref[s, 0], ext_ref[s, 1]) * scale_ref[0]
+
+    def body(s, carry):
+        product_slot(q_ref[s], s, (keep_ref, got_ref), y_ref, True)
+        return carry
+
+    lax.fori_loop(0, slots, body, 0)
+
+
+def total_of(x):
+    x = jnp.sum(x, axis=0)
+    return jnp.sum(jnp.sum(x, axis=0, keepdims=True), axis=1, keepdims=True)
+
+
+def ratio(a, b):
+    return jnp.where(b > 0, a / jnp.where(b > 0, b, 1.0), 0.0)
+
+
+def masked_sum(ext_ref, own_ref, other_ref, out_ref):
+    for s in range(out_ref.shape[0]):
+        out_ref[s] = (own_ref[s] + other_ref[s]) * inside(ext_ref[s, 0], ext_ref[s, 1])
+
+
+def step_kernel(count, *refs):
+    ext_ref, own_ref, other_ref = refs[:3]
+    basis = refs[3 : 3 + count]
+    keep_ref, got_ref, q_ref, y_ref, coeff_ref = refs[3 + count :]
+    slots = q_ref.shape[0]
+    masked_sum(ext_ref, own_ref, other_ref, q_ref)
+    image = q_ref[...]
+    rows = []
+    for ref in basis:
+        q = ref[...]
+        a = ratio(total_of(q * image), total_of(q * q))
+        rows.append(jnp.broadcast_to(a, (1, LANES)))
+    rest = image
+    for ref, row in zip(basis, rows):
+        rest = rest - row * ref[...]
+    q_ref[...] = rest
+    coeff_ref[...] = jnp.concatenate(rows + [jnp.zeros((8 - count, LANES), F32)], axis=0)
+
+    def body(s, carry):
+        product_slot(q_ref[s], s, (keep_ref, got_ref), y_ref, False)
+        return carry
+
+    lax.fori_loop(0, slots, body, 0)
+
+
+def vmem_call(kernel, out_shape, operands, smem, scratch=(), name=None):
+    specs = [pl.BlockSpec(memory_space=pltpu.SMEM)] * smem
+    specs += [pl.BlockSpec(memory_space=pltpu.VMEM)] * (len(operands) - smem)
+    outs = jax.tree.map(lambda _: pl.BlockSpec(memory_space=pltpu.VMEM), out_shape)
+    return pl.pallas_call(
+        kernel,
+        out_shape=out_shape,
+        in_specs=specs,
+        out_specs=outs,
+        scratch_shapes=list(scratch),
+        compiler_params=pltpu.CompilerParams(vmem_limit_bytes=VMEM_LIMIT),
+        name=name,
+    )(*operands)
+
+
+def gram_kernel(ext_ref, own_ref, other_ref, q0_ref, q1_ref, q2_ref, c1_ref, c2_ref, y_ref, table_ref):
+    masked_sum(ext_ref, own_ref, other_ref, y_ref)
+    vectors = [q0_ref[...], q1_ref[...], q2_ref[...], y_ref[...]]
+    rows = []
+    for i in range(4):
+        for j in range(i, 4):
+            rows.append(jnp.broadcast_to(total_of(vectors[i] * vectors[j]), (1, LANES)))
+    rows += [c1_ref[0:1], c2_ref[0:1], c2_ref[1:2]]
+    table_ref[...] = jnp.concatenate(rows + [jnp.zeros((3, LANES), F32)], axis=0)
+
+
+def combine(count, take):
+    gram = {}
+    row = 0
+    for i in range(4):
+        for j in range(i, 4):
+            gram[i, j] = gram[j, i] = take(row)
+            row += 1
+    a00, a01, a11 = take(10), take(11), take(12)
+    one = jnp.ones_like(a00)
+    zero = jnp.zeros_like(a00)
+
+    def mean(u, v):
+        acc = None
+        for i in range(4):
+            for j in range(4):
+                if u[i] is None or v[j] is None:
+                    continue
+                term = u[i] * v[j] * gram[i, j]
+                acc = term if acc is None else acc + term
+        return jnp.sum(acc, axis=0, keepdims=True) / count
+
+    images = [[a00, one, None, None], [a01, a11, one, None], [None, None, None, one]]
+    basis = [[one, None, None, None]]
+    projections = {}
+    for k in range(ITERS):
+        image = [None] * 4
+        for j, z in enumerate(basis[k]):
+            if z is None:
+                continue
+            for m, v in enumerate(images[j]):
+                if v is not None:
+                    image[m] = z * v if image[m] is None else image[m] + z * v
+        rest = list(image)
+        for i in range(k + 1):
+            p = mean(basis[i], image)
+            projections[i, k] = p
+            for m in range(4):
+                if basis[i][m] is not None:
+                    rest[m] = (zero if rest[m] is None else rest[m]) - p * basis[i][m]
+        if k + 1 < ITERS:
+            scale = 1.0 / jnp.sqrt(mean(rest, rest) + 1e-06)
+            basis.append([None if v is None else v * scale for v in rest])
+    return projections, rest
+
+
+def final_kernel(nodes, count, me_ref, t0_ref, t1_ref, t2_ref, t3_ref, q0_ref, q1_ref, q2_ref, y_ref,
+                 near_ref, far_ref, proj_ref, tables, turn):
+    node, core = me_ref[0], me_ref[1]
+    rows = t0_ref.shape[0]
+    for d, ref in enumerate((t0_ref, t1_ref, t2_ref, t3_ref)):
+        at = lax.rem(node + nodes - d, nodes) * rows
+        tables[pl.ds(pl.multiple_of(at, rows), rows), :] = ref[...]
+    devices = 2 * nodes
+    projections, rest = combine(count, lambda k: tables[pl.ds(k, devices, stride=16), :])
+    lines = []
+    for i in range(ITERS):
+        line = jnp.zeros((1, LANES), F32)
+        for k in range(i, ITERS):
+            line = jnp.where(iota((1, LANES), 1) == k, projections[i, k], line)
+        lines.append(line)
+    proj_ref[...] = jnp.concatenate(lines + [jnp.zeros((8 - ITERS, LANES), F32)], axis=0)
+    mine = iota((devices, LANES), 0) == 2 * node + core
+    coeff = [jnp.sum(jnp.where(mine, v, 0.0), axis=0, keepdims=True) for v in rest]
+    order = lane_order(True)
+    slots = y_ref.shape[0]
+    half = slots // 2
+    for s in range(slots):
+        x = coeff[0] * q0_ref[s] + coeff[1] * q1_ref[s] + coeff[2] * q2_ref[s] + coeff[3] * y_ref[s]
+        x = jnp.dot(x.astype(BF16), order, preferred_element_type=F32)
+        turn[pl.ds(s, HALF, stride=slots), :] = x
+    for t, ref in enumerate((near_ref, far_ref)):
+        for i in range(HALF):
+            ref[:, i * LANES : (i + 1) * LANES] = turn[pl.ds(slots * i + half * t, half), :].astype(BF16)
+
+
+def paired(start_vector, extents, offsets, env_left, env_right, channel_mask):
+    nodes = lax.axis_size("sector")
+    ops = lax.axis_size("op")
+    node = lax.axis_index("sector")
+    core = lax.axis_index("op") % 2
+    slots = start_vector.shape[0]
+    cap = slots // nodes
+    mine = slots // 2
+    count = float(slots * nodes * B * B)
+    swap_core = [(i, i ^ 1) for i in range(ops)]
+    swap_x = [(i, i ^ 2) for i in range(ops)]
+
+    slot_ids = jnp.arange(slots, dtype=jnp.int32)
+    same = offsets[:, None] == offsets[None, :]
+    earlier = slot_ids[None, :] < slot_ids[:, None]
+    place = offsets * cap + jnp.sum((same & earlier).astype(jnp.int32), axis=1)
+    order = jnp.sum(jnp.where(place[None, :] == slot_ids[:, None], slot_ids[None, :], 0), axis=1)
+    order = order.reshape(2, mine)
+    own = jnp.where(core == 0, order[0], order[1])
+    others = jnp.where(core == 0, order[1], order[0])
+
+    sent = prepare(others, channel_mask, env_left, env_right)
+    got = lax.ppermute(sent, "op", swap_core)
+    keep = prepare(own, channel_mask, env_left, env_right)
+
+    position = jnp.arange(B * B, dtype=jnp.int32)
+    mask = ((position // B)[None, :] < extents[:, 0:1]) & ((position % B)[None, :] < extents[:, 1:2])
+    masked = jnp.where(mask, start_vector.astype(F32), 0.0)
+    squares = jnp.sum(masked * masked)
+    high = lax.reduce_precision(squares, 8, 7)
+    middle = lax.reduce_precision(squares - high, 8, 7)
+    low = squares - high - middle
+
+    def route(t, back):
+        pairs = []
+        for h in range(nodes):
+            for q in range(ops):
+                to = (h + 2 * (q % 2) + t) % nodes
+                a, b = h * ops + q, to * ops + q
+                pairs.append((b, a) if back else (a, b))
+        return pairs
+
+    arrived = []
+    for t in range(2):
+        rows = lax.dynamic_slice_in_dim(own, t * cap, cap)
+        note = jnp.concatenate(
+            [jnp.take(extents, rows, axis=0).reshape(-1).astype(F32), jnp.stack([high, middle, low])]
+        )
+        note = jnp.pad(note, (0, B * B - note.shape[0])).astype(BF16)
+        payload = jnp.concatenate([jnp.take(start_vector, rows, axis=0), note[None]], axis=0)
+        arrived.append(lax.ppermute(payload, ("sector", "op"), route(t, False)))
+    notes = [a[cap].astype(F32) for a in arrived]
+    ext = jnp.concatenate([n[: 2 * cap].reshape(cap, 2) for n in notes]).astype(jnp.int32)
+    two = jnp.stack([jnp.sum(n[2 * cap : 2 * cap + 3]) for n in notes])
+    two_more = lax.ppermute(two, "op", swap_core)
+    four = jnp.where(core == 0, jnp.concatenate([two, two_more]), jnp.concatenate([two_more, two]))
+    by_node = jnp.take(four, (node - jnp.arange(nodes)) % nodes)
+    scale = (1.0 / jnp.sqrt(jnp.sum(by_node) / count + 1e-06)).reshape(1)
+
+    vector = jax.ShapeDtypeStruct((mine, HALF, LANES), F32)
+    coeffs = jax.ShapeDtypeStruct((8, LANES), F32)
+    q0, y0 = vmem_call(
+        start_kernel, (vector, vector), (scale, ext, arrived[0][:cap], arrived[1][:cap], keep, got), 2,
+        [pltpu.VMEM((mine * HALF, LANES), F32)], "start")
+    z0 = lax.ppermute(y0, "op", swap_x)
+
+    def step(*refs):
+        step_kernel(1, *refs)
+
+    def step_two(*refs):
+        step_kernel(2, *refs)
+
+    q1, y1, c1 = vmem_call(step, (vector, vector, coeffs), (ext, y0, z0, q0, keep, got), 1, name="second")
+    z1 = lax.ppermute(y1, "op", swap_x)
+    q2, y2, c2 = vmem_call(step_two, (vector, vector, coeffs), (ext, y1, z1, q0, q1, keep, got), 1, name="third")
+    z2 = lax.ppermute(y2, "op", swap_x)
+    image, table = vmem_call(
+        gram_kernel, (vector, jax.ShapeDtypeStruct((16, LANES), F32)),
+        (ext, y2, z2, q0, q1, q2, c1, c2), 1, name="gram")
+    other_table = lax.ppermute(table, "op", swap_core)
+    tables = jnp.where(
+        core == 0, jnp.concatenate([table, other_table]), jnp.concatenate([other_table, table]))
+    around = [tables] + [
+        lax.ppermute(tables, "sector", [(i, (i + d) % nodes) for i in range(nodes)]) for d in range(1, nodes)]
+    me = jnp.stack([node, core]).astype(jnp.int32)
+
+    def final(*refs):
+        final_kernel(nodes, count, *refs)
+
+    flat = jax.ShapeDtypeStruct((cap, B * B), BF16)
+    near, far, proj = vmem_call(
+        final, (flat, flat, coeffs), (me, *around, q0, q1, q2, image), 1,
+        [pltpu.VMEM((2 * nodes * 16, LANES), F32), pltpu.VMEM((mine * HALF, LANES), F32)], "final")
+    home = jnp.concatenate(
+        [lax.ppermute(part, ("sector", "op"), route(t, True)) for t, part in enumerate((near, far))])
+    home_other = lax.ppermute(home, "op", swap_core)
+    ordered = jnp.where(
+        core == 0, jnp.concatenate([home, home_other]), jnp.concatenate([home_other, home]))
+    residual = jnp.take(ordered, place, axis=0).astype(F32)
+    return residual, proj[:ITERS, :ITERS]
 
 
 def pack_rows(data, index, nodes, cap):
@@ -22,7 +430,7 @@
     return jnp.take(flat, index, axis=0)
 
 
-def on_device(start_vector, extents, offsets, env_left, env_right, channel_mask):
+def general(start_vector, extents, offsets, env_left, env_right, channel_mask):
     nodes = lax.axis_size("sector")
     here_index = lax.axis_index("sector")
     slots = start_vector.shape[0]
@@ -81,6 +489,13 @@
 
 
 def solution(mesh):
+    def on_device(start_vector, extents, offsets, env_left, env_right, channel_mask):
+        nodes, ops = mesh.shape["sector"], mesh.shape["op"]
+        slots, chans = env_left.shape[:2]
+        fits = nodes == 4 and ops == 4 and slots == 8 * nodes and chans <= 8
+        body = paired if fits else general
+        return body(start_vector, extents, offsets, env_left, env_right, channel_mask)
+
     return jax.shard_map(
         on_device,
         mesh=mesh,

time: 337 us -> 138 us (0.41)
  blocking collectives: 99.9 us -> 0 us
  waiting for transfers between devices: 117 us -> 24.1 us
  Pallas kernels: 0 us -> 59.3 us
  local copies, waits for them, and re-layouts: 41.3 us -> 14.7 us
  matrix products: 23.1 us -> 0 us
  between operations: 20.1 us -> 6.56 us
  other arithmetic: 22.4 us -> 10.1 us
  starting transfers between devices: 12.7 us -> 22.4 us
    psum x3 -> x0, waiting for transfers between devices: 97.9 us -> none  [on_device(): total = lax.psum(partial_image.reshape(slots, B * B), 'op')]
    psum x6 -> x0, blocking collectives: 62.6 us -> none  [the longest x3 33.1 us: squares(): return lax.psum(jnp.sum(vector * vector), 'sector') / count]
    pallas_call x0 -> x7, Pallas kernels: none -> 59.3 us  [the longest x5 40.6 us: vmem_call(): pl.pallas_call(kernel, out_shape=out_shape, in_specs=specs, out_specs=out...]
    all_to_all x3 -> x0, blocking collectives: 37.3 us -> none  [the longest x2 19.4 us: on_device(): lax.all_to_all(moving, 'sector', split_axis=0, concat_axis=0, tiled=True)]
    ppermute x0 -> x14, waiting for transfers between devices: none -> 24.1 us  [the longest x1 7.02 us: paired(): z0 = lax.ppermute(y0, 'op', swap_x)]
    dot_general x6 -> x0, matrix products: 23.1 us -> none  [the longest x3 13.3 us: on_device(): jnp.einsum('swac,swdc->sad', inner, right_wide, precision=lax.Precision.H...]
    ppermute x0 -> x14, starting transfers between devices: none -> 22.4 us  [the longest x2 4.51 us: paired(): lax.ppermute(part, ('sector', 'op'), route(t, True))]
    all_to_all x3 -> x0, waiting for transfers between devices: 18.6 us -> none  [the longest x2 18.6 us: on_device(): lax.all_to_all(going, 'sector', split_axis=0, concat_axis=0, tiled=True)]
  transfers between devices with their start and end apart: 6 -> 14, of which waited for: 5 -> 9; matrix products, arithmetic and copies ran while one was open for 5% -> 10% of each run, Pallas kernels for 0% -> 14%
where the time goes in v1:
time: 138 us; the launch traced here: 137 us
  Pallas kernels  59.3 us (43%)
  waiting for transfers between devices  24.1 us (17%)
  starting transfers between devices  22.4 us (16%)
  local copies, waits for them, and re-layouts  14.7 us (11%)
  other arithmetic  10.1 us (7%)
  between operations  6.56 us (5%)
    pallas_call x5, Pallas kernels, vmem_call(): pl.pallas_call(kernel, out_shape=out_shape, in_specs=specs, out_specs=out...  40.6 us
    pallas_call x2, Pallas kernels, prepare(): pl.pallas_call(prepare_kernel, out_shape=jax.ShapeDtypeStruct((2, slots,...  18.6 us
    unnamed x12, local copies, waits for them, and re-layouts  7.99 us
    ppermute x1, waiting for transfers between devices, paired(): z0 = lax.ppermute(y0, 'op', swap_x)  7.02 us
    ppermute x1, waiting for transfers between devices, paired(): z1 = lax.ppermute(y1, 'op', swap_x)  6.21 us
    ppermute x1, waiting for transfers between devices, paired(): z2 = lax.ppermute(y2, 'op', swap_x)  5.29 us
    ppermute x2, starting transfers between devices, paired(): lax.ppermute(part, ('sector', 'op'), route(t, True))  4.51 us
    ppermute x3, starting transfers between devices, paired(): lax.ppermute(tables, 'sector', [(i, (i + d) % nodes) for i in range(nodes)])  4.37 us
  transfers between devices with their start and end apart: 14, of which 9 were waited for; matrix products, arithmetic and copies ran while one was open for 10% of the time, Pallas kernels for 14%

profile of v1, /device:TPU:0, one launch (start us, length us, event | category | flops | bytes accessed | tf_op | source)
XLA Modules:
  0.0 137.2 jit_solution(6794017517776965963)
XLA Ops:
  0.7 0.8 copy.35
  1.4 0.8 slice_bitcast_fusion.1
  2.2 1.8 %multiply_reduce_fusion = f32[]{:T(128)} fusion(bf16[32,4096]{1,0:T(8,128)(2,1)} %param.10, s32[4096]{0:T(1024)S(1)} %fusion, s32[4096]{0:T(1024)S(1)} %add_select_fusion, s32[32]{0:T(128)S(1)} %get-tuple-element.37, s32[32]{0:T(128)S(1)} %get-tuple-element.36), kind=kLoop, calls=%fused_computation.6 | loop fusion | flops 917503 | bytes 295172 | tf_op jit(solution)/shard_map/reduce_sum | solution.py:344
  8.9 0.9 convert_reduce_fusion
  9.8 0.7 compare_and_fusion.2
  10.7 1.6 %gather_fusion.4 = bf16[8,4096]{1,0:T(8,128)(2,1)S(1)} fusion(bf16[32,4096]{1,0:T(8,128)(2,1)} %param.10, s32[1024]{0:T(1024)S(1)} %pad_clamp_fusion.2), kind=kCustom, calls=%fused_computation.2.clone | custom fusion | bytes 131104 | tf_op jit(solution)/shard_map/jit(_take)/gather | solution.py:365
  12.4 0.6 gather_fusion.5
  13.3 3.1 %collective-permute-start.1 = (bf16[9,4096]{1,0:T(8,128)(2,1)S(1)}, bf16[9,4096]{1,0:T(8,128)(2,1)S(1)}, u32[]{:S(2)}, u32[]{:S(2)}) collective-permute-start(bf16[9,4096]{1,0:T(8,128)(2,1)S(1)} %pad_maximum_fusion.1), channel_id=1, source_target_pairs={{0,4},{1,13},{2,6},{3,15},{4,8},{5,1},{6,10},{7,3},{8,12},{9,5},{1... | collective-permute-start | bytes 221192 | tf_op jit(solution)/shard_map/ppermute | solution.py:366
  16.4 0.8 copy.40.chan_ref
  17.2 2.5 %copy.41.left_ref = bf16[32,7,4096]{2,1,0:T(8,128)(2,1)S(1)} copy(bf16[32,7,4096]{2,0,1:T(8,128)(2,1)} %param.13) | data formatting | bytes 3670016 | tf_op args[3]
  19.7 2.4 %copy.42.right_ref = bf16[32,7,4096]{2,1,0:T(8,128)(2,1)} copy(bf16[32,7,4096]{2,0,1:T(8,128)(2,1)S(1)} %copy-done.3) | data formatting | bytes 3670016 | tf_op args[4]
  22.1 10.0 %prepare.3 = bf16[2,16,64,512]{3,2,1,0:T(8,128)(2,1)} custom-call(s32[16]{0:T(128)S(1)} %get-tuple-element.38.index_ref, s32[32,7]{1,0:T(8,128)S(1)} %copy.40.chan_ref, bf16[32,7,4096]{2,1,0:T(8,128)(2,1)S(1)} %copy.41.left_ref, bf16[32,7,4096]{2,1,0:T(8,128)(2,1)} %copy.42.right_ref), custom_call_target="tpu_custom_call" | custom-call | tf_op jit(solution)/shard_map/prepare/pallas_call | solution.py:96
  32.0 1.6 %collective-permute-start.3 = (bf16[2,16,64,512]{3,2,1,0:T(8,128)(2,1)}, bf16[2,16,64,512]{3,2,1,0:T(8,128)(2,1)}, u32[]{:S(2)}, u32[]{:S(2)}) collective-permute-start(bf16[2,16,64,512]{3,2,1,0:T(8,128)(2,1)} %prepare.3), channel_id=1, source_target_pairs={{0,1},{1,0},{2,3},{3,2},{4,5},{5,4},{6,7},{7,6},{8,9},{9,8},{10,11... | collective-permute-start | bytes 6291464 | tf_op jit(solution)/shard_map/ppermute | solution.py:338
  34.3 0.6 gather_fusion.2
  35.2 0.7 collective-permute-start
  35.9 1.6 %copy-done.1 = bf16[32,7,4096]{2,1,0:T(8,128)(2,1)S(1)} copy-done((bf16[32,7,4096]{2,1,0:T(8,128)(2,1)S(1)}, bf16[32,7,4096]{2,1,0:T(8,128)(2,1)}, u32[]{:S(2)}) %copy-start.1) | copy-done | bytes 1835032
  37.5 8.6 %prepare.2.keep_ref.refs_4_.refs_5_ = bf16[2,16,64,512]{3,2,1,0:T(8,128)(2,1)S(1)} custom-call(s32[16]{0:T(128)S(1)} %get-tuple-element.39.index_ref, s32[32,7]{1,0:T(8,128)S(1)} %copy.40.chan_ref, bf16[32,7,4096]{2,1,0:T(8,128)(2,1)S(1)} %copy-done.1, bf16[32,7,4096]{2,1,0:T(8,128)(2,1)} %copy.42.right_ref), custom_call_target="tpu_custom_call" | custom-call | tf_op jit(solution)/shard_map/prepare/pallas_call | solution.py:96
  46.8 0.7 fusion.13
  47.5 0.7 fusion.14
  48.2 1.4 pad_maximum_fusion.3
  49.6 2.5 %collective-permute-start.2 = (f32[2]{0:T(128)S(1)}, f32[2]{0:T(128)S(1)}, u32[]{:S(2)}, u32[]{:S(2)}) collective-permute-start(f32[2]{0:T(128)S(1)} %pad_maximum_fusion.3), channel_id=1, source_target_pairs={{0,1},{1,0},{2,3},{3,2},{4,5},{5,4},{6,7},{7,6},{8,9},{9,8},{10,11... | collective-permute-start | bytes 32 | tf_op jit(solution)/shard_map/ppermute | solution.py:370
  52.1 0.8 collective-permute-done.2
  52.9 1.4 broadcast_select_fusion.2
  54.2 0.6 gather_fusion
  54.9 0.7 fusion.15
  56.3 10.6 %start.1 = (f32[16,32,128]{2,1,0:T(8,128)S(1)}, f32[16,32,128]{2,1,0:T(8,128)S(1)}) custom-call(f32[1]{0:T(128)} %bitcast.10.scale_ref, s32[16,2]{1,0:T(8,128)S(1)} %convert_element_type.43.ext_ref.refs_0_, bf16[8,4096]{1,0:T(8,128)(2,1)S(1)} %slice.92.near_ref, bf16[8,4096]{1,0:T(8,128)(2,1)S(1)} %slice.93.far_ref, ...), custom_call_target="tpu_custom_call" | custom-call | tf_op jit(solution)/shard_map/start/pallas_call | solution.py:219
  66.9 1.6 %collective-permute-start.4 = (f32[16,32,128]{2,1,0:T(8,128)S(1)}, f32[16,32,128]{2,1,0:T(8,128)S(1)}, u32[]{:S(2)}, u32[]{:S(2)}) collective-permute-start(f32[16,32,128]{2,1,0:T(8,128)S(1)} %get-tuple-element.17.refs_1_), channel_id=1, source_target_pairs={{0,2},{1,3},{2,0},{3,1},{4,6},{5,7},{6,4},{7,5},{8,10},{9,11},{10,... | collective-permute-start | bytes 786440 | tf_op jit(solution)/shard_map/ppermute | solution.py:380
  68.4 7.0 %collective-permute-done.4.refs_2_ = f32[16,32,128]{2,1,0:T(8,128)S(1)} collective-permute-done((f32[16,32,128]{2,1,0:T(8,128)S(1)}, f32[16,32,128]{2,1,0:T(8,128)S(1)}, u32[]{:S(2)}, u32[]{:S(2)}) %collective-permute-start.4) | collective-permute-done | bytes 262176 | tf_op jit(solution)/shard_map/ppermute | solution.py:380
  75.5 14.0 %second.1 = (f32[16,32,128]{2,1,0:T(8,128)S(1)}, f32[16,32,128]{2,1,0:T(8,128)S(1)}, f32[8,128]{1,0:T(8,128)S(1)}) custom-call(s32[16,2]{1,0:T(8,128)S(1)} %convert_element_type.43.ext_ref.refs_0_, f32[16,32,128]{2,1,0:T(8,128)S(1)} %get-tuple-element.17.refs_1_, f32[16,32,128]{2,1,0:T(8,128)S(1)} %collective-permute-done.4.refs_2_, ...), custom_call_target="tpu_custom_call" | custom-call | tf_op jit(solution)/shard_map/second/pallas_call | solution.py:219
  89.5 1.6 %collective-permute-start.5 = (f32[16,32,128]{2,1,0:T(8,128)S(1)}, f32[16,32,128]{2,1,0:T(8,128)S(1)}, u32[]{:S(2)}, u32[]{:S(2)}) collective-permute-start(f32[16,32,128]{2,1,0:T(8,128)S(1)} %get-tuple-element.19.refs_1_), channel_id=1, source_target_pairs={{0,2},{1,3},{2,0},{3,1},{4,6},{5,7},{6,4},{7,5},{8,10},{9,11},{10,... | collective-permute-start | bytes 786440 | tf_op jit(solution)/shard_map/ppermute | solution.py:389
  91.0 6.2 %collective-permute-done.5.refs_2_ = f32[16,32,128]{2,1,0:T(8,128)S(1)} collective-permute-done((f32[16,32,128]{2,1,0:T(8,128)S(1)}, f32[16,32,128]{2,1,0:T(8,128)S(1)}, u32[]{:S(2)}, u32[]{:S(2)}) %collective-permute-start.5) | collective-permute-done | bytes 262176 | tf_op jit(solution)/shard_map/ppermute | solution.py:389
  97.2 14.1 %third.1 = (f32[16,32,128]{2,1,0:T(8,128)S(1)}, f32[16,32,128]{2,1,0:T(8,128)S(1)}, f32[8,128]{1,0:T(8,128)S(1)}) custom-call(s32[16,2]{1,0:T(8,128)S(1)} %convert_element_type.43.ext_ref.refs_0_, f32[16,32,128]{2,1,0:T(8,128)S(1)} %get-tuple-element.19.refs_1_, f32[16,32,128]{2,1,0:T(8,128)S(1)} %collective-permute-done.5.refs_2_, ...), custom_call_target="tpu_custom_call" | custom-call | tf_op jit(solution)/shard_map/third/pallas_call | solution.py:219
  111.3 1.6 %collective-permute-start.6 = (f32[16,32,128]{2,1,0:T(8,128)S(1)}, f32[16,32,128]{2,1,0:T(8,128)S(1)}, u32[]{:S(2)}, u32[]{:S(2)}) collective-permute-start(f32[16,32,128]{2,1,0:T(8,128)S(1)} %get-tuple-element.21.own_ref), channel_id=1, source_target_pairs={{0,2},{1,3},{2,0},{3,1},{4,6},{5,7},{6,4},{7,5},{8,10},{9,11},{10,... | collective-permute-start | bytes 786440 | tf_op jit(solution)/shard_map/ppermute | solution.py:391
  112.8 5.3 %collective-permute-done.6.other_ref = f32[16,32,128]{2,1,0:T(8,128)S(1)} collective-permute-done((f32[16,32,128]{2,1,0:T(8,128)S(1)}, f32[16,32,128]{2,1,0:T(8,128)S(1)}, u32[]{:S(2)}, u32[]{:S(2)}) %collective-permute-start.6) | collective-permute-done | bytes 262176 | tf_op jit(solution)/shard_map/ppermute | solution.py:391
  118.1 1.1 gram.1
  119.2 1.2 collective-permute-done.7
  120.5 1.8 %collective-permute-start.9 = (f32[32,128]{1,0:T(8,128)S(1)}, f32[32,128]{1,0:T(8,128)S(1)}, u32[]{:S(2)}, u32[]{:S(2)}) collective-permute-start(f32[32,128]{1,0:T(8,128)S(1)} %maximum_select_fusion.1.refs_1_), channel_id=1, source_target_pairs={{0,8},{4,12},{8,0},{12,4},{1,9},{5,13},{9,1},{13,5},{2,10},{6,14},... | collective-permute-start | bytes 49160 | tf_op jit(solution)/shard_map/ppermute | solution.py:399
  122.3 2.5 %collective-permute-start.10 = (f32[32,128]{1,0:T(8,128)S(1)}, f32[32,128]{1,0:T(8,128)S(1)}, u32[]{:S(2)}, u32[]{:S(2)}) collective-permute-start(f32[32,128]{1,0:T(8,128)S(1)} %maximum_select_fusion.1.refs_1_), channel_id=1, source_target_pairs={{0,12},{4,0},{8,4},{12,8},{1,13},{5,1},{9,5},{13,9},{2,14},{6,2},{... | collective-permute-start | bytes 49160 | tf_op jit(solution)/shard_map/ppermute | solution.py:399
  124.8 1.1 collective-permute-done.8.refs_2_
  125.9 0.6 collective-permute-done.10.refs_4_
  126.5 1.0 final.1
  127.5 3.9 %collective-permute-start.12 = (bf16[8,4096]{1,0:T(8,128)(2,1)S(1)}, bf16[8,4096]{1,0:T(8,128)(2,1)S(1)}, u32[]{:S(2)}, u32[]{:S(2)}) collective-permute-start(bf16[8,4096]{1,0:T(8,128)(2,1)S(1)} %get-tuple-element.28), channel_id=1, source_target_pairs={{4,0},{13,1},{6,2},{15,3},{8,4},{1,5},{10,6},{3,7},{12,8},{5,9},{1... | collective-permute-start | bytes 196616 | tf_op jit(solution)/shard_map/ppermute | solution.py:410
  131.3 0.7 collective-permute-start.11
  132.0 1.6 %collective-permute-done.12 = bf16[8,4096]{1,0:T(8,128)(2,1)S(1)} collective-permute-done((bf16[8,4096]{1,0:T(8,128)(2,1)S(1)}, bf16[8,4096]{1,0:T(8,128)(2,1)S(1)}, u32[]{:S(2)}, u32[]{:S(2)}) %collective-permute-start.12) | collective-permute-done | bytes 65568 | tf_op jit(solution)/shard_map/ppermute | solution.py:410
  133.6 1.0 collective-permute-start.13
  134.5 0.6 slice.75
  135.6 0.7 gather_fusion.1
  136.3 0.9 select_convert_fusion
  (55 shorter events, 2.9 us)
Async XLA Ops:
  13.3 6.4 %copy-start.3 = (bf16[32,7,4096]{2,0,1:T(8,128)(2,1)S(1)}, bf16[32,7,4096]{2,0,1:T(8,128)(2,1)}, u32[]{:S(2)}) copy-start(bf16[32,7,4096]{2,0,1:T(8,128)(2,1)} %param.14) | copy-start | bytes 5505028
  13.3 32.9 %collective-permute-start.1 = (bf16[9,4096]{1,0:T(8,128)(2,1)S(1)}, bf16[9,4096]{1,0:T(8,128)(2,1)S(1)}, u32[]{:S(2)}, u32[]{:S(2)}) collective-permute-start(bf16[9,4096]{1,0:T(8,128)(2,1)S(1)} %pad_maximum_fusion.1), channel_id=1, source_target_pairs={{0,4},{1,13},{2,6},{3,15},{4,8},{5,1},{6,10},{7,3},{8,12},{9,5},{1... | collective-permute-start | bytes 221192 | tf_op jit(solution)/shard_map/ppermute | solution.py:366
  19.7 12.3 %copy-start = (bf16[32,7,4096]{2,1,0:T(8,128)(2,1)}, bf16[32,7,4096]{2,1,0:T(8,128)(2,1)S(1)}, u32[]{:S(2)}) copy-start(bf16[32,7,4096]{2,1,0:T(8,128)(2,1)S(1)} %copy.41.left_ref) | copy-start | bytes 5505028
  22.1 12.2 %copy-start.2 = (bf16[32,4096]{1,0:T(8,128)(2,1)S(1)}, bf16[32,4096]{1,0:T(8,128)(2,1)}, u32[]{:S(2)}) copy-start(bf16[32,4096]{1,0:T(8,128)(2,1)} %param.10) | copy-start | bytes 786436
  32.0 24.2 %collective-permute-start.3 = (bf16[2,16,64,512]{3,2,1,0:T(8,128)(2,1)}, bf16[2,16,64,512]{3,2,1,0:T(8,128)(2,1)}, u32[]{:S(2)}, u32[]{:S(2)}) collective-permute-start(bf16[2,16,64,512]{3,2,1,0:T(8,128)(2,1)} %prepare.3), channel_id=1, source_target_pairs={{0,1},{1,0},{2,3},{3,2},{4,5},{5,4},{6,7},{7,6},{8,9},{9,8},{10,11... | collective-permute-start | bytes 6291464 | tf_op jit(solution)/shard_map/ppermute | solution.py:338
  35.2 11.0 %collective-permute-start = (bf16[9,4096]{1,0:T(8,128)(2,1)S(1)}, bf16[9,4096]{1,0:T(8,128)(2,1)S(1)}, u32[]{:S(2)}, u32[]{:S(2)}) collective-permute-start(bf16[9,4096]{1,0:T(8,128)(2,1)S(1)} %pad_maximum_fusion), channel_id=1, source_target_pairs={{0,0},{1,9},{2,2},{3,11},{4,4},{5,13},{6,6},{7,15},{8,8},{9,1},{10... | collective-permute-start | bytes 221192 | tf_op jit(solution)/shard_map/ppermute | solution.py:366
  35.9 1.6 %copy-start.1 = (bf16[32,7,4096]{2,1,0:T(8,128)(2,1)S(1)}, bf16[32,7,4096]{2,1,0:T(8,128)(2,1)}, u32[]{:S(2)}) copy-start(bf16[32,7,4096]{2,1,0:T(8,128)(2,1)} %copy-done) | copy-start | bytes 5505028
  49.6 3.3 %collective-permute-start.2 = (f32[2]{0:T(128)S(1)}, f32[2]{0:T(128)S(1)}, u32[]{:S(2)}, u32[]{:S(2)}) collective-permute-start(f32[2]{0:T(128)S(1)} %pad_maximum_fusion.3), channel_id=1, source_target_pairs={{0,1},{1,0},{2,3},{3,2},{4,5},{5,4},{6,7},{7,6},{8,9},{9,8},{10,11... | collective-permute-start | bytes 32 | tf_op jit(solution)/shard_map/ppermute | solution.py:370
  66.9 8.6 %collective-permute-start.4 = (f32[16,32,128]{2,1,0:T(8,128)S(1)}, f32[16,32,128]{2,1,0:T(8,128)S(1)}, u32[]{:S(2)}, u32[]{:S(2)}) collective-permute-start(f32[16,32,128]{2,1,0:T(8,128)S(1)} %get-tuple-element.17.refs_1_), channel_id=1, source_target_pairs={{0,2},{1,3},{2,0},{3,1},{4,6},{5,7},{6,4},{7,5},{8,10},{9,11},{10,... | collective-permute-start | bytes 786440 | tf_op jit(solution)/shard_map/ppermute | solution.py:380
  89.5 7.8 %collective-permute-start.5 = (f32[16,32,128]{2,1,0:T(8,128)S(1)}, f32[16,32,128]{2,1,0:T(8,128)S(1)}, u32[]{:S(2)}, u32[]{:S(2)}) collective-permute-start(f32[16,32,128]{2,1,0:T(8,128)S(1)} %get-tuple-element.19.refs_1_), channel_id=1, source_target_pairs={{0,2},{1,3},{2,0},{3,1},{4,6},{5,7},{6,4},{7,5},{8,10},{9,11},{10,... | collective-permute-start | bytes 786440 | tf_op jit(solution)/shard_map/ppermute | solution.py:389
  111.3 6.8 %collective-permute-start.6 = (f32[16,32,128]{2,1,0:T(8,128)S(1)}, f32[16,32,128]{2,1,0:T(8,128)S(1)}, u32[]{:S(2)}, u32[]{:S(2)}) collective-permute-start(f32[16,32,128]{2,1,0:T(8,128)S(1)} %get-tuple-element.21.own_ref), channel_id=1, source_target_pairs={{0,2},{1,3},{2,0},{3,1},{4,6},{5,7},{6,4},{7,5},{8,10},{9,11},{10,... | collective-permute-start | bytes 786440 | tf_op jit(solution)/shard_map/ppermute | solution.py:391
  119.2 1.2 collective-permute-start.7
  120.4 5.5 %collective-permute-start.8 = (f32[32,128]{1,0:T(8,128)S(1)}, f32[32,128]{1,0:T(8,128)S(1)}, u32[]{:S(2)}, u32[]{:S(2)}) collective-permute-start(f32[32,128]{1,0:T(8,128)S(1)} %maximum_select_fusion.1.refs_1_), channel_id=1, source_target_pairs={{0,4},{4,8},{8,12},{12,0},{1,5},{5,9},{9,13},{13,1},{2,6},{6,10},{... | collective-permute-start | bytes 49160 | tf_op jit(solution)/shard_map/ppermute | solution.py:399
  120.5 5.4 %collective-permute-start.9 = (f32[32,128]{1,0:T(8,128)S(1)}, f32[32,128]{1,0:T(8,128)S(1)}, u32[]{:S(2)}, u32[]{:S(2)}) collective-permute-start(f32[32,128]{1,0:T(8,128)S(1)} %maximum_select_fusion.1.refs_1_), channel_id=1, source_target_pairs={{0,8},{4,12},{8,0},{12,4},{1,9},{5,13},{9,1},{13,5},{2,10},{6,14},... | collective-permute-start | bytes 49160 | tf_op jit(solution)/shard_map/ppermute | solution.py:399
  122.3 4.2 %collective-permute-start.10 = (f32[32,128]{1,0:T(8,128)S(1)}, f32[32,128]{1,0:T(8,128)S(1)}, u32[]{:S(2)}, u32[]{:S(2)}) collective-permute-start(f32[32,128]{1,0:T(8,128)S(1)} %maximum_select_fusion.1.refs_1_), channel_id=1, source_target_pairs={{0,12},{4,0},{8,4},{12,8},{1,13},{5,1},{9,5},{13,9},{2,14},{6,2},{... | collective-permute-start | bytes 49160 | tf_op jit(solution)/shard_map/ppermute | solution.py:399
  127.5 6.1 %collective-permute-start.12 = (bf16[8,4096]{1,0:T(8,128)(2,1)S(1)}, bf16[8,4096]{1,0:T(8,128)(2,1)S(1)}, u32[]{:S(2)}, u32[]{:S(2)}) collective-permute-start(bf16[8,4096]{1,0:T(8,128)(2,1)S(1)} %get-tuple-element.28), channel_id=1, source_target_pairs={{4,0},{13,1},{6,2},{15,3},{8,4},{1,5},{10,6},{3,7},{12,8},{5,9},{1... | collective-permute-start | bytes 196616 | tf_op jit(solution)/shard_map/ppermute | solution.py:410
  131.3 2.2 %collective-permute-start.11 = (bf16[8,4096]{1,0:T(8,128)(2,1)S(1)}, bf16[8,4096]{1,0:T(8,128)(2,1)S(1)}, u32[]{:S(2)}, u32[]{:S(2)}) collective-permute-start(bf16[8,4096]{1,0:T(8,128)(2,1)S(1)} %get-tuple-element.27), channel_id=1, source_target_pairs={{0,0},{9,1},{2,2},{11,3},{4,4},{13,5},{6,6},{15,7},{8,8},{1,9},{10... | collective-permute-start | bytes 196616 | tf_op jit(solution)/shard_map/ppermute | solution.py:410
  133.6 2.0 %collective-permute-start.13 = (bf16[16,4096]{1,0:T(8,128)(2,1)S(1)}, bf16[16,4096]{1,0:T(8,128)(2,1)S(1)}, u32[]{:S(2)}, u32[]{:S(2)}) collective-permute-start(bf16[16,4096]{1,0:T(8,128)(2,1)S(1)} %pad_maximum_fusion.2), channel_id=1, source_target_pairs={{0,1},{1,0},{2,3},{3,2},{4,5},{5,4},{6,7},{7,6},{8,9},{9,8},{10,11... | collective-permute-start | bytes 393224 | tf_op jit(solution)/shard_map/ppermute | solution.py:411

commit v2 on v0

--- a/solution.py
+++ b/solution.py
@@ -1,10 +1,537 @@
 import jax
 import jax.numpy as jnp
 from jax import lax
+from jax.experimental import pallas as pl
+from jax.experimental.pallas import tpu as pltpu
 from jax.sharding import PartitionSpec as P
 
 B = 64
 ITERS = 3
+HALF = 32
+LANES = 128
+WIDE = 4 * LANES
+F32 = jnp.float32
+BF16 = jnp.bfloat16
+VMEM_LIMIT = 24 * 1024 * 1024
+
+
+def iota(shape, dim):
+    return lax.broadcasted_iota(jnp.int32, shape, dim)
+
+
+def one_hot(condition):
+    return jnp.where(condition, 1.0, 0.0).astype(BF16)
+
+
+def kept_column(c):
+    return (c % 2) * HALF + c // 2
+
+
+def to_kept():
+    row, col = iota((LANES, LANES), 0), iota((LANES, LANES), 1)
+    return one_hot(row // B * B + kept_column(row % B) == col)
+
+
+def from_kept_twice():
+    row, col = iota((2 * LANES, LANES), 0) % LANES, iota((2 * LANES, LANES), 1)
+    return one_hot(col // B * B + kept_column(col % B) == row)
+
+
+def pair_to_kept():
+    row, col = iota((2 * LANES, 2 * LANES), 0), iota((2 * LANES, 2 * LANES), 1)
+    w, p, c = row // LANES, row // B % 2, row % B
+    return one_hot(p * LANES + w * B + kept_column(c) == col)
+
+
+def blocks_first(order_ref, base, count, slots):
+    col, row = iota((8, 8 * slots), 1), iota((8, 8 * slots), 0)
+    same = col // slots == row
+    slot = col % slots
+    parts = [
+        jnp.where(same & (slot == order_ref[base + k]), 1.0, 0.0) for k in range(count)
+    ]
+    return jnp.concatenate(parts, axis=0).astype(BF16)
+
+
+def slots_last(order_ref, slots):
+    n = 8 * slots
+    place = iota((1, n), 1) // 8
+    slot = jnp.zeros((1, n), jnp.int32)
+    for k in range(slots):
+        slot = jnp.where(place == k, order_ref[k], slot)
+    row, col = iota((n, n), 0), iota((n, n), 1)
+    return one_hot((row // slots == col % 8) & (row % slots == slot))
+
+
+def inside(rows, cols):
+    lane = iota((HALF, LANES), 1)
+    a = 2 * iota((HALF, LANES), 0) + lane // B
+    kept = lane % B
+    c = 2 * (kept % HALF) + kept // HALF
+    return jnp.where((a.astype(F32) < rows) & (c.astype(F32) < cols), 1.0, 0.0)
+
+
+def total_of(x):
+    return jnp.sum(jnp.sum(x, axis=0, keepdims=True), axis=1, keepdims=True)
+
+
+def wide(x):
+    return jnp.broadcast_to(x, (1, LANES))
+
+
+def split(x):
+    high = x.astype(BF16)
+    return high, (x - high.astype(F32)).astype(BF16)
+
+
+def split_three(x):
+    high, _ = split(x)
+    rest = x - high.astype(F32)
+    middle, low = split(rest)
+    return high, middle, low
+
+
+def call(kernel, name, out_shape, operands, kinds, scratch=(), out_kinds=None, cost=2.0):
+    space = {"s": pltpu.SMEM, "v": pltpu.VMEM, "a": pl.ANY}
+    out_kinds = out_kinds or "v" * len(out_shape)
+    return pl.pallas_call(
+        kernel,
+        out_shape=out_shape,
+        in_specs=[pl.BlockSpec(memory_space=space[k]) for k in kinds],
+        out_specs=tuple(pl.BlockSpec(memory_space=space[k]) for k in out_kinds),
+        scratch_shapes=list(scratch),
+        compiler_params=pltpu.CompilerParams(vmem_limit_bytes=VMEM_LIMIT),
+        cost_estimate=pl.CostEstimate(flops=0, bytes_accessed=int(cost * 3.0e6), transcendentals=0),
+        name=name,
+    )(*operands)
+
+
+def sort_slots(core, offset_ref, order_ref, place_ref, seen):
+    slots = order_ref.shape[0]
+    nodes = seen.shape[0]
+    cap = slots // nodes
+    for o in range(nodes):
+        seen[o] = 0
+    for j in range(slots):
+        o = offset_ref[j]
+        rank = seen[o]
+        seen[o] = rank + 1
+        place = o * cap + rank + core * (slots // 2)
+        place = jnp.where(place >= slots, place - slots, place)
+        order_ref[place] = j
+        place_ref[j] = place
+
+
+def arrange(order_ref, base, chan_ref, raw, wait, outs):
+    chans, slots = raw.shape[1:3]
+    cap = outs[0].shape[1]
+    count = cap * len(outs)
+    first = blocks_first(order_ref, base, count, slots)
+    second = pair_to_kept()
+    low = iota((1, 2 * LANES), 1) % LANES < B
+    blank = jnp.zeros((slots, LANES), BF16)
+    for t in range(2):
+        for g in range(4):
+            used = [w for w in (2 * g, 2 * g + 1) if w < chans]
+            for w in used:
+                wait(t, w)
+            chunks = []
+            for c in range(4):
+                rows = []
+                for i in range(8 * c, 8 * c + 8):
+                    parts = [raw[t, w, :, i * LANES : (i + 1) * LANES] for w in used]
+                    rows.append(jnp.concatenate(parts + [blank] * (2 - len(used)), axis=1))
+                x = jnp.concatenate(rows, axis=0)
+                x = jnp.dot(first, x, preferred_element_type=F32).astype(BF16)
+                chunks.append(jnp.dot(x, second, preferred_element_type=F32))
+            for k in range(count):
+                x = jnp.concatenate([chunk[8 * k : 8 * k + 8] for chunk in chunks], axis=0)
+                if t == 0:
+                    slot = order_ref[base + k]
+                    kept = [chan_ref[w, slot].astype(F32) for w in used]
+                    x = x * jnp.where(low, kept[0], kept[-1])
+                x = x.astype(BF16)
+                for p in range(2):
+                    outs[k // cap][t, k % cap, p * HALF : (p + 1) * HALF, g * LANES : (g + 1) * LANES] = x[
+                        :, p * LANES : (p + 1) * LANES
+                    ]
+
+
+def fetcher(left_ref, right_ref, raw, sems):
+    def copy(t, w):
+        return pltpu.make_async_copy((left_ref, right_ref)[t].at[w], raw.at[t, w], sems.at[t, w])
+
+    for t in range(2):
+        for w in range(raw.shape[1]):
+            copy(t, w).start()
+    return lambda t, w: copy(t, w).wait()
+
+
+def send_kernel(me_ref, offset_ref, chan_ref, left_ref, right_ref, order_ref, place_ref, near_ref, far_ref,
+                raw, sems, seen):
+    wait = fetcher(left_ref, right_ref, raw, sems)
+    sort_slots(me_ref[1], offset_ref, order_ref, place_ref, seen)
+    arrange(order_ref, order_ref.shape[0] // 2, chan_ref, raw, wait, (near_ref, far_ref))
+
+
+def keep_kernel(order_ref, chan_ref, left_ref, right_ref, near_ref, far_ref, raw, sems):
+    wait = fetcher(left_ref, right_ref, raw, sems)
+    arrange(order_ref, 0, chan_ref, raw, wait, (near_ref, far_ref))
+
+
+def ship_kernel(order_ref, ext_ref, start_ref, near_ref, far_ref, home_ref):
+    slots = start_ref.shape[0]
+    cap = slots // 4
+    first = blocks_first(order_ref, 0, slots, slots)
+    second = to_kept()
+    chunks = []
+    for c in range(4):
+        rows = [start_ref[:, i * LANES : (i + 1) * LANES] for i in range(8 * c, 8 * c + 8)]
+        x = jnp.dot(first, jnp.concatenate(rows, axis=0), preferred_element_type=F32).astype(BF16)
+        chunks.append(jnp.dot(x, second, preferred_element_type=F32))
+    halves = []
+    for k in range(slots):
+        slot = order_ref[k]
+        x = jnp.concatenate([chunk[8 * k : 8 * k + 8] for chunk in chunks], axis=0)
+        x = x * inside(ext_ref[0, slot].astype(F32), ext_ref[1, slot].astype(F32))
+        home_ref[HALF * k : HALF * (k + 1), :] = x.astype(BF16)
+        if k < 2 * cap:
+            (near_ref, far_ref)[k // cap][HALF * (k % cap) : HALF * (k % cap + 1), :] = x.astype(BF16)
+        if k % (2 * cap) == 0:
+            halves.append(x * x)
+        else:
+            halves[-1] = halves[-1] + x * x
+    squares = wide(total_of(halves[0]) + total_of(halves[1]))
+    pieces = [v.astype(F32) for v in split_three(squares)]
+    blank = jnp.zeros((2 * 16 - 2 * cap - 3, LANES), F32)
+    for t, ref in enumerate((near_ref, far_ref)):
+        lines = []
+        for d in range(2):
+            for k in range(cap):
+                lines.append(jnp.full((1, LANES), ext_ref[d, order_ref[t * cap + k]].astype(F32)))
+        ref[HALF * cap :, :] = jnp.concatenate(lines + pieces + [blank], axis=0).astype(BF16)
+
+
+def note(ref):
+    return ref[ref.shape[0] - 32 :, :].astype(F32)
+
+
+def sums_kernel(near_ref, far_ref, out_ref):
+    lines = []
+    for ref in (near_ref, far_ref):
+        n = note(ref)
+        lines.append(n[16:17] + n[17:18] + n[18:19])
+    out_ref[...] = jnp.concatenate(lines + [jnp.zeros((6, LANES), F32)], axis=0)
+
+
+def block_diagonal(x):
+    low = iota((HALF, LANES), 1) < B
+    swapped = pltpu.roll(x, B, 1)
+    zero = jnp.zeros_like(x)
+    two = jnp.concatenate(
+        [
+            jnp.where(low, x, zero),
+            jnp.where(low, swapped, zero),
+            jnp.where(low, zero, swapped),
+            jnp.where(low, zero, x),
+        ],
+        axis=0,
+    )
+    blank = jnp.zeros_like(two)
+    return jnp.concatenate(
+        [jnp.concatenate([two, blank], axis=1), jnp.concatenate([blank, two], axis=1)], axis=0
+    )
+
+
+def product(q_ref, keep_ref, got_ref, y_ref, inner_ref, rounded):
+    count = q_ref.shape[0]
+    span = 2 * LANES
+    for s in range(count):
+        high, low = split(block_diagonal(q_ref[s]))
+        left = jnp.concatenate(
+            [ref[0, s, :, g * span : (g + 1) * span] for ref in (keep_ref, got_ref) for g in range(2)], axis=0
+        )
+        inner = jnp.dot(left, high, preferred_element_type=F32)
+        if not rounded:
+            inner = inner + jnp.dot(left, low, preferred_element_type=F32)
+        high, low = split(inner)
+        for k in range(4):
+            inner_ref[s, :B, k * span : (k + 1) * span] = high[k * B : (k + 1) * B]
+            inner_ref[s, B:, k * span : (k + 1) * span] = low[k * B : (k + 1) * B]
+    for s in range(count):
+        right = jnp.concatenate([keep_ref[1, s], got_ref[1, s]], axis=1)
+        both = lax.dot_general(inner_ref[s], right, (((1,), (1,)), ((), ())), preferred_element_type=F32)
+        image = both[:B] + both[B:]
+        y_ref[s] = jnp.concatenate([image[:HALF], image[HALF:]], axis=1)
+
+
+def start_kernel(count, nodes, me_ref, ship_ref, sums_ref, more_ref, keep_ref, got_ref, q_ref, y_ref, scale_ref,
+                 inner_ref):
+    node, core = me_ref[0], me_ref[1]
+    by_node = []
+    for e in range(nodes):
+        value = jnp.zeros((1, LANES), F32)
+        for ref, c in ((sums_ref, core), (more_ref, 1 - core)):
+            for t in range(2):
+                source = lax.rem(node + 2 * nodes - 2 * c - t, nodes)
+                value = value + jnp.where(source == e, ref[t : t + 1, :], 0.0)
+        by_node.append(value)
+    squares = (by_node[0] + by_node[1]) + (by_node[2] + by_node[3])
+    scale = 1.0 / jnp.sqrt(squares / count + 1e-06)
+    scale_ref[...] = jnp.broadcast_to(scale, scale_ref.shape)
+    for s in range(q_ref.shape[0]):
+        q_ref[s] = ship_ref[HALF * s : HALF * (s + 1), :].astype(F32) * scale
+    product(q_ref, keep_ref, got_ref, y_ref, inner_ref, True)
+
+
+def orthogonal(ship_ref, own_ref, other_ref, basis, q_ref):
+    n = note(ship_ref)
+    cap = q_ref.shape[0]
+    for s in range(cap):
+        q_ref[s] = (own_ref[s] + other_ref[s]) * inside(n[s : s + 1], n[cap + s : cap + s + 1])
+    image = q_ref[...].reshape(cap * HALF, LANES)
+    rows = []
+    rest = image
+    for ref in basis:
+        q = ref[...].reshape(cap * HALF, LANES)
+        length = total_of(q * q)
+        along = total_of(q * image)
+        row = wide(jnp.where(length > 0, along / jnp.where(length > 0, length, 1.0), 0.0))
+        rest = rest - row * q
+        rows.append(row)
+    q_ref[...] = rest.reshape(q_ref.shape)
+    return rows
+
+
+def step_kernel(count, *refs):
+    ship_ref, own_ref, other_ref = refs[:3]
+    basis = refs[3 : 3 + count]
+    keep_ref, got_ref, q_ref, y_ref, along_ref, inner_ref = refs[3 + count :]
+    rows = orthogonal(ship_ref, own_ref, other_ref, basis, q_ref)
+    along_ref[...] = jnp.concatenate(rows + [jnp.zeros((8 - count, LANES), F32)], axis=0)
+    product(q_ref, keep_ref, got_ref, y_ref, inner_ref, False)
+
+
+def table_kernel(*refs):
+    out_refs, table_ref = refs[16:18], refs[18]
+    rows = []
+    for t in range(2):
+        ship_ref, own_ref, other_ref, q0, q1, q2, c1, c2 = refs[8 * t : 8 * t + 8]
+        last = orthogonal(ship_ref, own_ref, other_ref, (q0, q1, q2), out_refs[t])
+        vectors = [ref[...].reshape(-1, LANES) for ref in (q0, q1, q2, out_refs[t])]
+        for i in range(4):
+            for j in range(i, 4):
+                rows.append(wide(total_of(vectors[i] * vectors[j])))
+        rows += [c1[0:1], c2[0:1], c2[1:2]] + last
+    table_ref[...] = jnp.concatenate(rows, axis=0)
+
+
+def pack_kernel(me_ref, table_ref, other_ref, *refs):
+    core = me_ref[1]
+    mine, other = table_ref[...], other_ref[...]
+    tables = jnp.concatenate(
+        [jnp.where(core == 0, mine, other), jnp.where(core == 0, other, mine)], axis=0
+    )
+    pieces = split_three(tables)
+    for t in range(2):
+        out_ref = refs[6 + t]
+        at = 0
+        for ref in refs[3 * t : 3 * t + 3]:
+            rows = ref.shape[0] * HALF
+            out_ref[at : at + rows, :] = ref[...].reshape(rows, LANES).astype(BF16)
+            at += rows
+        for piece in pieces:
+            out_ref[at : at + piece.shape[0], :] = piece
+            at += piece.shape[0]
+
+
+def combine(count, take):
+    gram = {}
+    row = 0
+    for i in range(4):
+        for j in range(i, 4):
+            gram[i, j] = gram[j, i] = take(row)
+            row += 1
+    one = jnp.ones_like(gram[0, 0])
+    images = [
+        [take(10), one, None, None],
+        [take(11), take(12), one, None],
+        [take(13), take(14), take(15), one],
+    ]
+
+    def mean(u, v):
+        acc = None
+        for i in range(4):
+            for j in range(4):
+                if u[i] is not None and v[j] is not None:
+                    term = u[i] * v[j] * gram[i, j]
+                    acc = term if acc is None else acc + term
+        return jnp.sum(acc, axis=0, keepdims=True) / count
+
+    basis = [[one, None, None, None]]
+    projections = {}
+    for k in range(ITERS):
+        image = [None] * 4
+        for z, parts in zip(basis[k], images):
+            for m, v in enumerate(parts):
+                if z is not None and v is not None:
+                    image[m] = z * v if image[m] is None else image[m] + z * v
+        rest = list(image)
+        for i in range(k + 1):
+            p = mean(basis[i], image)
+            projections[i, k] = p
+            for m, v in enumerate(basis[i]):
+                if v is not None:
+                    rest[m] = rest[m] - p * v
+        if k + 1 < ITERS:
+            scale = 1.0 / jnp.sqrt(mean(rest, rest) + 1e-06)
+            basis.append([None if v is None else v * scale for v in rest])
+    return projections, rest
+
+
+def finish_kernel(count, nodes, me_ref, order_ref, scale_ref, home_ref, near_ref, far_ref, near_more_ref,
+                  far_more_ref, out_ref, proj_ref, tables):
+    node, core = me_ref[0], me_ref[1]
+    slots = out_ref.shape[0]
+    rows = home_ref.shape[0] // 4
+    size = 4 * 16
+    sources = []
+    for k, ref in enumerate((near_ref, far_ref, near_more_ref, far_more_ref)):
+        c = core if k < 2 else 1 - core
+        hop = 2 * c + k % 2
+        host = lax.rem(node + hop, nodes)
+        pieces = [ref[3 * rows + d * size : 3 * rows + (d + 1) * size, :].astype(F32) for d in range(3)]
+        tables[pl.ds(pl.multiple_of(host * size, size), size), :] = pieces[0] + pieces[1] + pieces[2]
+        sources.append((ref, host * 4 + hop))
+    sets = 4 * nodes
+    projections, rest = combine(count, lambda k: tables[pl.ds(k, sets, stride=16), :])
+    lines = []
+    for i in range(ITERS):
+        line = jnp.zeros((1, LANES), F32)
+        for k in range(i, ITERS):
+            line = jnp.where(iota((1, LANES), 1) == k, projections[i, k], line)
+        lines.append(line)
+    proj_ref[...] = jnp.concatenate(lines + [jnp.zeros((8 - ITERS, LANES), F32)], axis=0)
+    scale = scale_ref[0:1, :]
+    blocks = []
+    for k, (ref, index) in enumerate(sources):
+        mine = iota((sets, LANES), 0) == index
+        coeff = [jnp.sum(jnp.where(mine, v, 0.0), axis=0, keepdims=True) for v in rest]
+        x = coeff[0] * (home_ref[rows * k : rows * (k + 1), :].astype(F32) * scale)
+        for d in range(3):
+            x = x + coeff[d + 1] * ref[rows * d : rows * (d + 1), :].astype(F32)
+        blocks.append(x)
+    first = slots_last(order_ref, slots)
+    second = from_kept_twice()
+    per = rows // HALF
+    for c in range(4):
+        x = jnp.concatenate(
+            [blocks[k // per][HALF * (k % per) + 8 * c : HALF * (k % per) + 8 * c + 8] for k in range(slots)],
+            axis=0,
+        )
+        x = jnp.dot(first, jnp.concatenate(split(x), axis=1), preferred_element_type=F32).astype(BF16)
+        x = jnp.dot(x, second, preferred_element_type=F32)
+        for i in range(8):
+            out_ref[:, (8 * c + i) * LANES : (8 * c + i + 1) * LANES] = x[i * slots : (i + 1) * slots]
+
+
+def paired(start_vector, extents, offsets, env_left, env_right, channel_mask):
+    nodes = lax.axis_size("sector")
+    ops = lax.axis_size("op")
+    node = lax.axis_index("sector")
+    core = lax.axis_index("op") % 2
+    slots = start_vector.shape[0]
+    chans = env_left.shape[1]
+    cap = slots // nodes
+    count = float(slots * nodes * B * B)
+    me = jnp.stack([node, core]).astype(jnp.int32)
+    swap_core = [(i, i ^ 1) for i in range(ops)]
+    swap_x = [(i, i ^ 2) for i in range(ops)]
+    left = jnp.transpose(env_left, (1, 0, 2))
+    right = jnp.transpose(env_right, (1, 0, 2))
+    chan = jnp.transpose(channel_mask)
+    ext = jnp.transpose(extents)
+
+    def route(t, back):
+        pairs = []
+        for h in range(nodes):
+            for q in range(ops):
+                to = (h + 2 * (q % 2) + t) % nodes
+                a, b = h * ops + q, to * ops + q
+                pairs.append((b, a) if back else (a, b))
+        return pairs
+
+    def across(x):
+        return lax.ppermute(x, "op", swap_core)
+
+    def shape(dims, dtype=F32):
+        return jax.ShapeDtypeStruct(dims, dtype)
+
+    environment = shape((2, cap, B, WIDE), BF16)
+    vector = shape((cap, HALF, LANES))
+    tile = shape((8, LANES))
+    raw = [pltpu.VMEM((2, chans, slots, B * B), BF16), pltpu.SemaphoreType.DMA((2, chans))]
+    inner = [pltpu.VMEM((cap, LANES, 2 * WIDE), BF16)]
+
+    order, _, *send = call(
+        send_kernel, "send", (shape((slots,), jnp.int32), shape((slots,), jnp.int32), environment, environment),
+        (me, offsets, chan, left, right), "sssaa", raw + [pltpu.SMEM((nodes,), jnp.int32)], "ssvv", 3.0)
+    got = [across(x) for x in send]
+    payload = shape((cap * HALF + 32, LANES), BF16)
+    *ships, home = call(
+        ship_kernel, "ship", (payload, payload, shape((slots * HALF, LANES), BF16)),
+        (order, ext, start_vector), "ssv", cost=1.0)
+    ships = [lax.ppermute(x, ("sector", "op"), route(t, False)) for t, x in enumerate(ships)]
+    keep = call(
+        keep_kernel, "keep", (environment, environment), (order, chan, left, right), "ssaa", raw, cost=3.0)
+    (sums,) = call(sums_kernel, "sums", (tile,), ships, "vv", cost=0.3)
+    more = across(sums)
+
+    def start(*refs):
+        start_kernel(count, nodes, *refs)
+
+    def step(k):
+        return lambda *refs: step_kernel(k, *refs)
+
+    basis = [[], []]
+    along = [[], []]
+    images = [None, None]
+    for t in range(2):
+        q, y, scale = call(
+            start, "first", (vector, vector, tile), (me, ships[t], sums, more, keep[t], got[t]), "svvvvv", inner)
+        basis[t].append(q)
+        images[t] = (y, lax.ppermute(y, "op", swap_x))
+    for k in range(1, ITERS):
+        for t in range(2):
+            q, y, a = call(
+                step(k), ("second", "third")[k - 1], (vector, vector, tile),
+                (ships[t], *images[t], *basis[t], keep[t], got[t]), "v" * (5 + k), inner)
+            basis[t].append(q)
+            along[t].append(a)
+            images[t] = (y, lax.ppermute(y, "op", swap_x))
+
+    operands = []
+    for t in range(2):
+        operands += [ships[t], *images[t], *basis[t], *along[t]]
+    *last, table = call(
+        table_kernel, "table", (vector, vector, shape((32, LANES))), operands, "v" * 16, cost=1.0)
+    other_table = across(table)
+    vectors = []
+    for t in range(2):
+        vectors += [basis[t][1], basis[t][2], last[t]]
+    parcel = shape((3 * cap * HALF + 3 * 64, LANES), BF16)
+    parcels = call(
+        pack_kernel, "pack", (parcel, parcel), (me, table, other_table, *vectors), "s" + "v" * 8, cost=0.7)
+    parcels = [lax.ppermute(x, ("sector", "op"), route(t, True)) for t, x in enumerate(parcels)]
+    parcels += [across(x) for x in parcels]
+
+    def finish(*refs):
+        finish_kernel(count, nodes, *refs)
+
+    residual, proj = call(
+        finish, "finish", (shape((slots, B * B)), tile), (me, order, scale, home, *parcels), "ssvvvvvv",
+        [pltpu.VMEM((4 * nodes * 16, LANES), F32)])
+    return residual, proj[:ITERS, :ITERS]
 
 
 def pack_rows(data, index, nodes, cap):
@@ -22,7 +549,7 @@
     return jnp.take(flat, index, axis=0)
 
 
-def on_device(start_vector, extents, offsets, env_left, env_right, channel_mask):
+def general(start_vector, extents, offsets, env_left, env_right, channel_mask):
     nodes = lax.axis_size("sector")
     here_index = lax.axis_index("sector")
     slots = start_vector.shape[0]
@@ -81,6 +608,13 @@
 
 
 def solution(mesh):
+    def on_device(start_vector, extents, offsets, env_left, env_right, channel_mask):
+        nodes, ops = mesh.shape["sector"], mesh.shape["op"]
+        slots, chans = env_left.shape[:2]
+        fits = nodes == 4 and ops == 4 and slots == 8 * nodes and chans <= 8
+        body = paired if fits else general
+        return body(start_vector, extents, offsets, env_left, env_right, channel_mask)
+
     return jax.shard_map(
         on_device,
         mesh=mesh,

time: 337 us -> 73.6 us (0.22)
  waiting for transfers between devices: 117 us -> 13.9 us
  blocking collectives: 99.9 us -> 0 us
  local copies, waits for them, and re-layouts: 41.3 us -> 5.88 us
  Pallas kernels: 0 us -> 23.6 us
  matrix products: 23.1 us -> 0 us
  other arithmetic: 22.4 us -> 0.08 us
  between operations: 20.1 us -> 0.75 us
  starting transfers between devices: 12.7 us -> 29.1 us
    psum x3 -> x0, waiting for transfers between devices: 97.9 us -> none  [on_device(): total = lax.psum(partial_image.reshape(slots, B * B), 'op')]
    psum x6 -> x0, blocking collectives: 62.6 us -> none  [the longest x3 33.1 us: squares(): return lax.psum(jnp.sum(vector * vector), 'sector') / count]
    all_to_all x3 -> x0, blocking collectives: 37.3 us -> none  [the longest x2 19.4 us: on_device(): lax.all_to_all(moving, 'sector', split_axis=0, concat_axis=0, tiled=True)]
    ppermute x0 -> x16, starting transfers between devices: none -> 29.1 us  [the longest x6 15.6 us: across(): return lax.ppermute(x, 'op', swap_core)]
    pallas_call x0 -> x13, Pallas kernels: none -> 23.6 us  [call(): pl.pallas_call(kernel, out_shape=out_shape, in_specs=[pl.BlockSpec(memory...]
    dot_general x6 -> x0, matrix products: 23.1 us -> none  [the longest x3 13.3 us: on_device(): jnp.einsum('swac,swdc->sad', inner, right_wide, precision=lax.Precision.H...]
    all_to_all x3 -> x0, waiting for transfers between devices: 18.6 us -> none  [the longest x2 18.6 us: on_device(): lax.all_to_all(going, 'sector', split_axis=0, concat_axis=0, tiled=True)]
    reshape x8 -> x0, local copies, waits for them, and re-layouts: 16.4 us -> none  [the longest x1 6.34 us: on_device(): left = env_left.reshape(slots, chans, B, B)]
  transfers between devices with their start and end apart: 6 -> 16, of which waited for: 5 -> 9; matrix products, arithmetic and copies ran while one was open for 5% -> 0% of each run, Pallas kernels for 0% -> 21%
where the time goes in v2:
time: 73.6 us; the launch traced here: 73.3 us
  starting transfers between devices  29.1 us (40%)
  Pallas kernels  23.6 us (32%)
  waiting for transfers between devices  13.9 us (19%)
  local copies, waits for them, and re-layouts  5.88 us (8%)
  between operations  0.75 us (1%)
    pallas_call x13, Pallas kernels, call(): pl.pallas_call(kernel, out_shape=out_shape, in_specs=[pl.BlockSpec(memory...  23.6 us
    ppermute x6, starting transfers between devices, across(): return lax.ppermute(x, 'op', swap_core)  15.6 us
    ppermute x6, starting transfers between devices, paired(): images[t] = (y, lax.ppermute(y, 'op', swap_x))  8.52 us
    ppermute x6, waiting for transfers between devices, paired(): images[t] = (y, lax.ppermute(y, 'op', swap_x))  7.33 us
    unnamed x18, local copies, waits for them, and re-layouts  5.3 us
    ppermute x2, starting transfers between devices, paired(): lax.ppermute(x, ('sector', 'op'), route(t, False))  3.87 us
    ppermute x2, waiting for transfers between devices, paired(): lax.ppermute(x, ('sector', 'op'), route(t, False))  3.86 us
    ppermute x6, waiting for transfers between devices, across(): return lax.ppermute(x, 'op', swap_core)  2.69 us
  transfers between devices with their start and end apart: 16, of which 9 were waited for; matrix products, arithmetic and copies ran while one was open for 0% of the time, Pallas kernels for 21%

profile of v2, /device:TPU:0, one launch (start us, length us, event | category | flops | bytes accessed | tf_op | source)
XLA Modules:
  0.0 73.3 jit_solution(11324729566426532458)
XLA Ops:
  0.6 0.1 pad_add_fusion.me_ref.refs_0_
  0.7 1.5 %copy-done = bf16[32,7,4096]{2,0,1:T(8,128)(2,1)S(1)} copy-done((bf16[32,7,4096]{2,0,1:T(8,128)(2,1)S(1)}, bf16[32,7,4096]{2,0,1:T(8,128)(2,1)}, u32[]{:S(2)}) %copy-start) | copy-done | bytes 1835032
  2.2 1.5 %copy-done.2 = bf16[32,7,4096]{2,0,1:T(8,128)(2,1)S(1)} copy-done((bf16[32,7,4096]{2,0,1:T(8,128)(2,1)S(1)}, bf16[32,7,4096]{2,0,1:T(8,128)(2,1)}, u32[]{:S(2)}) %copy-start.2) | copy-done | bytes 1835032
  3.7 0.7 copy-done.5
  4.4 0.7 copy-done.8
  5.1 4.6 %send.1 = (s32[32]{0:T(128)S(1)}, s32[32]{0:T(128)}, bf16[2,8,64,512]{3,2,1,0:T(8,128)(2,1)S(1)}, bf16[2,8,64,512]{3,2,1,0:T(8,128)(2,1)S(1)}) custom-call(s32[2]{0:T(128)S(1)} %pad_add_fusion.me_ref.refs_0_, s32[32]{0:T(128)S(1)} %copy-done.8, s32[7,32]{1,0:T(8,128)S(1)} %bitcast.10, bf16[7,32,4096]{2,1,0:T(8,128)(2,1)S(1)} %bitcast.6, ...), custom_call_target="tpu_custom_call" | custom-call | bytes 9000000 | tf_op jit(solution)/shard_map/send/pallas_call | solution.py:97
  9.7 0.5 collective-permute-start.3
  10.2 0.1 collective-permute-start.4
  10.3 0.9 %copy-done.4 = bf16[32,4096]{1,0:T(8,128)(2,1)S(1)} copy-done((bf16[32,4096]{1,0:T(8,128)(2,1)S(1)}, bf16[32,4096]{1,0:T(8,128)(2,1)}, u32[]{:S(2)}) %copy-start.4) | copy-done | bytes 262168
  11.3 1.5 %ship.1 = (bf16[288,128]{1,0:T(8,128)(2,1)S(1)}, bf16[288,128]{1,0:T(8,128)(2,1)S(1)}, bf16[1024,128]{1,0:T(8,128)(2,1)S(1)}) custom-call(s32[32]{0:T(128)S(1)} %get-tuple-element.34.order_ref.refs_1_, s32[2,32]{1,0:T(2,128)S(1)} %bitcast.12, bf16[32,4096]{1,0:T(8,128)(2,1)S(1)} %copy-done.4), custom_call_target="tpu_custom_call" | custom-call | bytes 3000000 | tf_op jit(solution)/shard_map/ship/pallas_call | solution.py:97
  12.8 3.0 %collective-permute-start = (bf16[288,128]{1,0:T(8,128)(2,1)S(1)}, bf16[288,128]{1,0:T(8,128)(2,1)S(1)}, u32[]{:S(2)}, u32[]{:S(2)}) collective-permute-start(bf16[288,128]{1,0:T(8,128)(2,1)S(1)} %get-tuple-element.35), channel_id=1, source_target_pairs={{0,4},{1,13},{2,6},{3,15},{4,8},{5,1},{6,10},{7,3},{8,12},{9,5},{1... | collective-permute-start | bytes 221192 | tf_op jit(solution)/shard_map/ppermute | solution.py:484
  15.8 0.8 %collective-permute-start.1 = (bf16[288,128]{1,0:T(8,128)(2,1)S(1)}, bf16[288,128]{1,0:T(8,128)(2,1)S(1)}, u32[]{:S(2)}, u32[]{:S(2)}) collective-permute-start(bf16[288,128]{1,0:T(8,128)(2,1)S(1)} %get-tuple-element.36), channel_id=1, source_target_pairs={{0,0},{1,9},{2,2},{3,11},{4,4},{5,13},{6,6},{7,15},{8,8},{9,1},{10... | collective-permute-start | bytes 221192 | tf_op jit(solution)/shard_map/ppermute | solution.py:484
  16.6 3.9 %collective-permute-done.far_ref.refs_1_.refs_0_.refs_8_ = bf16[288,128]{1,0:T(8,128)(2,1)S(1)} collective-permute-done((bf16[288,128]{1,0:T(8,128)(2,1)S(1)}, bf16[288,128]{1,0:T(8,128)(2,1)S(1)}, u32[]{:S(2)}, u32[]{:S(2)}) %collective-permute-start) | collective-permute-done | bytes 73760 | tf_op jit(solution)/shard_map/ppermute | solution.py:484
  20.5 0.0 collective-permute-done.1.near_ref.refs_1_.refs_0_
  20.5 3.2 %collective-permute-start.2 = (f32[8,128]{1,0:T(8,128)S(1)}, f32[8,128]{1,0:T(8,128)S(1)}, u32[]{:S(2)}, u32[]{:S(2)}) collective-permute-start(f32[8,128]{1,0:T(8,128)S(1)} %sums.1.refs_2_), channel_id=1, source_target_pairs={{0,1},{1,0},{2,3},{3,2},{4,5},{5,4},{6,7},{7,6},{8,9},{9,8},{10,11... | collective-permute-start | bytes 12296 | tf_op jit(solution)/shard_map/ppermute | solution.py:465
  23.7 4.3 %keep.1 = (bf16[2,8,64,512]{3,2,1,0:T(8,128)(2,1)S(1)}, bf16[2,8,64,512]{3,2,1,0:T(8,128)(2,1)S(1)}) custom-call(s32[32]{0:T(128)S(1)} %get-tuple-element.34.order_ref.refs_1_, s32[7,32]{1,0:T(8,128)S(1)} %bitcast.11, bf16[7,32,4096]{2,1,0:T(8,128)(2,1)S(1)} %bitcast.7, bf16[7,32,4096]{2,1,0:T(8,128)(2,1)S(1)} %bitcast.9), custom_call_target="tpu_custom_call" | custom-call | bytes 9000000 | tf_op jit(solution)/shard_map/keep/pallas_call | solution.py:97
  28.0 0.0 collective-permute-done.2.refs_3_
  28.0 1.7 %first.2 = (f32[8,32,128]{2,1,0:T(8,128)S(1)}, f32[8,32,128]{2,1,0:T(8,128)S(1)}, f32[8,128]{1,0:T(8,128)S(1)}) custom-call(s32[2]{0:T(128)S(1)} %pad_add_fusion.me_ref.refs_0_, bf16[288,128]{1,0:T(8,128)(2,1)S(1)} %collective-permute-done.far_ref.refs_1_.refs_0_.refs_8_, f32[8,128]{1,0:T(8,128)S(1)} %sums.1.refs_2_, ...), custom_call_target="tpu_custom_call" | custom-call | bytes 6000000 | tf_op jit(solution)/shard_map/first/pallas_call | solution.py:97
  29.7 1.6 %collective-permute-start.8 = (f32[8,32,128]{2,1,0:T(8,128)S(1)}, f32[8,32,128]{2,1,0:T(8,128)S(1)}, u32[]{:S(2)}, u32[]{:S(2)}) collective-permute-start(f32[8,32,128]{2,1,0:T(8,128)S(1)} %get-tuple-element.51.refs_1_), channel_id=1, source_target_pairs={{0,2},{1,3},{2,0},{3,1},{4,6},{5,7},{6,4},{7,5},{8,10},{9,11},{10,... | collective-permute-start | bytes 393224 | tf_op jit(solution)/shard_map/ppermute | solution.py:503
  31.3 1.7 %first.3 = (f32[8,32,128]{2,1,0:T(8,128)S(1)}, f32[8,32,128]{2,1,0:T(8,128)S(1)}, f32[8,128]{1,0:T(8,128)}) custom-call(s32[2]{0:T(128)S(1)} %pad_add_fusion.me_ref.refs_0_, bf16[288,128]{1,0:T(8,128)(2,1)S(1)} %collective-permute-done.1.near_ref.refs_1_.refs_0_, f32[8,128]{1,0:T(8,128)S(1)} %sums.1.refs_2_, f32[8,128]{1,0:T(8,128)S(1)} %collective-permute-done.2.refs_3_, ...), custom_call_target="tpu_custom_call" | custom-call | bytes 6000000 | tf_op jit(solution)/shard_map/first/pallas_call | solution.py:97
  33.0 0.6 collective-permute-start.5
  33.6 1.6 %collective-permute-done.8.refs_2_ = f32[8,32,128]{2,1,0:T(8,128)S(1)} collective-permute-done((f32[8,32,128]{2,1,0:T(8,128)S(1)}, f32[8,32,128]{2,1,0:T(8,128)S(1)}, u32[]{:S(2)}, u32[]{:S(2)}) %collective-permute-start.8) | collective-permute-done | bytes 131104 | tf_op jit(solution)/shard_map/ppermute | solution.py:503
  35.2 1.6 %second.3 = (f32[8,32,128]{2,1,0:T(8,128)S(1)}, f32[8,32,128]{2,1,0:T(8,128)S(1)}, f32[8,128]{1,0:T(8,128)S(1)}) custom-call(bf16[288,128]{1,0:T(8,128)(2,1)S(1)} %collective-permute-done.far_ref.refs_1_.refs_0_.refs_8_, f32[8,32,128]{2,1,0:T(8,128)S(1)} %get-tuple-element.51.refs_1_, f32[8,32,128]{2,1,0:T(8,128)S(1)} %collective-permute-done.8.refs_2_, ...), custom_call_target="tpu_custom_call" | custom-call | bytes 6000000 | tf_op jit(solution)/shard_map/second/pallas_call | solution.py:97
  36.8 2.3 %collective-permute-start.9 = (f32[8,32,128]{2,1,0:T(8,128)S(1)}, f32[8,32,128]{2,1,0:T(8,128)S(1)}, u32[]{:S(2)}, u32[]{:S(2)}) collective-permute-start(f32[8,32,128]{2,1,0:T(8,128)S(1)} %get-tuple-element.53.refs_1_), channel_id=1, source_target_pairs={{0,2},{1,3},{2,0},{3,1},{4,6},{5,7},{6,4},{7,5},{8,10},{9,11},{10,... | collective-permute-start | bytes 393224 | tf_op jit(solution)/shard_map/ppermute | solution.py:511
  39.1 0.0 collective-permute-done.5.refs_2_
  39.1 1.6 %second.2 = (f32[8,32,128]{2,1,0:T(8,128)S(1)}, f32[8,32,128]{2,1,0:T(8,128)S(1)}, f32[8,128]{1,0:T(8,128)S(1)}) custom-call(bf16[288,128]{1,0:T(8,128)(2,1)S(1)} %collective-permute-done.1.near_ref.refs_1_.refs_0_, f32[8,32,128]{2,1,0:T(8,128)S(1)} %get-tuple-element.43.refs_1_, f32[8,32,128]{2,1,0:T(8,128)S(1)} %collective-permute-done.5.refs_2_, ...), custom_call_target="tpu_custom_call" | custom-call | bytes 6000000 | tf_op jit(solution)/shard_map/second/pallas_call | solution.py:97
  40.7 0.5 collective-permute-start.6
  41.2 1.5 %collective-permute-done.9.refs_2_ = f32[8,32,128]{2,1,0:T(8,128)S(1)} collective-permute-done((f32[8,32,128]{2,1,0:T(8,128)S(1)}, f32[8,32,128]{2,1,0:T(8,128)S(1)}, u32[]{:S(2)}, u32[]{:S(2)}) %collective-permute-start.9) | collective-permute-done | bytes 131104 | tf_op jit(solution)/shard_map/ppermute | solution.py:511
  42.7 1.6 %third.3 = (f32[8,32,128]{2,1,0:T(8,128)S(1)}, f32[8,32,128]{2,1,0:T(8,128)S(1)}, f32[8,128]{1,0:T(8,128)S(1)}) custom-call(bf16[288,128]{1,0:T(8,128)(2,1)S(1)} %collective-permute-done.far_ref.refs_1_.refs_0_.refs_8_, f32[8,32,128]{2,1,0:T(8,128)S(1)} %get-tuple-element.53.refs_1_, f32[8,32,128]{2,1,0:T(8,128)S(1)} %collective-permute-done.9.refs_2_, ...), custom_call_target="tpu_custom_call" | custom-call | bytes 6000000 | tf_op jit(solution)/shard_map/third/pallas_call | solution.py:97
  44.3 2.5 %collective-permute-start.10 = (f32[8,32,128]{2,1,0:T(8,128)S(1)}, f32[8,32,128]{2,1,0:T(8,128)S(1)}, u32[]{:S(2)}, u32[]{:S(2)}) collective-permute-start(f32[8,32,128]{2,1,0:T(8,128)S(1)} %get-tuple-element.55.refs_9_), channel_id=1, source_target_pairs={{0,2},{1,3},{2,0},{3,1},{4,6},{5,7},{6,4},{7,5},{8,10},{9,11},{10,... | collective-permute-start | bytes 393224 | tf_op jit(solution)/shard_map/ppermute | solution.py:511
  46.8 0.2 collective-permute-done.6.refs_2_
  47.0 1.6 %third.2 = (f32[8,32,128]{2,1,0:T(8,128)S(1)}, f32[8,32,128]{2,1,0:T(8,128)S(1)}, f32[8,128]{1,0:T(8,128)S(1)}) custom-call(bf16[288,128]{1,0:T(8,128)(2,1)S(1)} %collective-permute-done.1.near_ref.refs_1_.refs_0_, f32[8,32,128]{2,1,0:T(8,128)S(1)} %get-tuple-element.45.refs_1_, f32[8,32,128]{2,1,0:T(8,128)S(1)} %collective-permute-done.6.refs_2_, ...), custom_call_target="tpu_custom_call" | custom-call | bytes 6000000 | tf_op jit(solution)/shard_map/third/pallas_call | solution.py:97
  48.6 1.0 %collective-permute-start.7 = (f32[8,32,128]{2,1,0:T(8,128)S(1)}, f32[8,32,128]{2,1,0:T(8,128)S(1)}, u32[]{:S(2)}, u32[]{:S(2)}) collective-permute-start(f32[8,32,128]{2,1,0:T(8,128)S(1)} %get-tuple-element.47.refs_1_), channel_id=1, source_target_pairs={{0,2},{1,3},{2,0},{3,1},{4,6},{5,7},{6,4},{7,5},{8,10},{9,11},{10,... | collective-permute-start | bytes 393224 | tf_op jit(solution)/shard_map/ppermute | solution.py:511
  49.6 1.4 %collective-permute-done.10.refs_10_ = f32[8,32,128]{2,1,0:T(8,128)S(1)} collective-permute-done((f32[8,32,128]{2,1,0:T(8,128)S(1)}, f32[8,32,128]{2,1,0:T(8,128)S(1)}, u32[]{:S(2)}, u32[]{:S(2)}) %collective-permute-start.10) | collective-permute-done | bytes 131104 | tf_op jit(solution)/shard_map/ppermute | solution.py:511
  51.0 2.6 %collective-permute-done.7.refs_2_ = f32[8,32,128]{2,1,0:T(8,128)S(1)} collective-permute-done((f32[8,32,128]{2,1,0:T(8,128)S(1)}, f32[8,32,128]{2,1,0:T(8,128)S(1)}, u32[]{:S(2)}, u32[]{:S(2)}) %collective-permute-start.7) | collective-permute-done | bytes 131104 | tf_op jit(solution)/shard_map/ppermute | solution.py:511
  53.6 0.6 table.1
  54.2 0.0 collective-permute-start.11
  54.3 1.2 %collective-permute-done.11.other_ref = f32[32,128]{1,0:T(8,128)S(1)} collective-permute-done((f32[32,128]{1,0:T(8,128)S(1)}, f32[32,128]{1,0:T(8,128)S(1)}, u32[]{:S(2)}, u32[]{:S(2)}) %collective-permute-start.11) | collective-permute-done | bytes 16416 | tf_op jit(solution)/shard_map/ppermute | solution.py:465
  55.4 0.6 pack.1
  56.0 0.7 collective-permute-start.12
  56.7 0.5 collective-permute-start.13
  57.2 11.8 %collective-permute-start.14 = (bf16[960,128]{1,0:T(8,128)(2,1)S(1)}, bf16[960,128]{1,0:T(8,128)(2,1)S(1)}, u32[]{:S(2)}, u32[]{:S(2)}) collective-permute-start(bf16[960,128]{1,0:T(8,128)(2,1)S(1)} %collective-permute-done.12.refs_4_), channel_id=1, source_target_pairs={{0,1},{1,0},{2,3},{3,2},{4,5},{5,4},{6,7},{7,6},{8,9},{9,8},{10,11... | collective-permute-start | bytes 737288 | tf_op jit(solution)/shard_map/ppermute | solution.py:465
  69.0 0.0 collective-permute-done.13.refs_5_
  69.0 0.0 collective-permute-start.15
  69.0 1.1 %collective-permute-done.14.refs_6_ = bf16[960,128]{1,0:T(8,128)(2,1)S(1)} collective-permute-done((bf16[960,128]{1,0:T(8,128)(2,1)S(1)}, bf16[960,128]{1,0:T(8,128)(2,1)S(1)}, u32[]{:S(2)}, u32[]{:S(2)}) %collective-permute-start.14) | collective-permute-done | bytes 245792 | tf_op jit(solution)/shard_map/ppermute | solution.py:465
  70.1 0.4 collective-permute-done.15.refs_7_
  70.5 2.3 %finish.1 = (f32[32,4096]{1,0:T(8,128)}, f32[8,128]{1,0:T(8,128)S(1)}) custom-call(s32[2]{0:T(128)S(1)} %pad_add_fusion.me_ref.refs_0_, s32[32]{0:T(128)S(1)} %get-tuple-element.34.order_ref.refs_1_, f32[8,128]{1,0:T(8,128)S(1)} %get-tuple-element.39.refs_2_, bf16[1024,128]{1,0:T(8,128)(2,1)S(1)} %get-tuple-element.40.refs_3_, ...), custom_call_target="tpu_custom_call" | custom-call | bytes 6000000 | tf_op jit(solution)/shard_map/finish/pallas_call | solution.py:97
  72.7 0.6 slice.3
  (17 shorter events, 0.0 us)
Async XLA Ops:
  0.7 1.5 %copy-start = (bf16[32,7,4096]{2,0,1:T(8,128)(2,1)S(1)}, bf16[32,7,4096]{2,0,1:T(8,128)(2,1)}, u32[]{:S(2)}) copy-start(bf16[32,7,4096]{2,0,1:T(8,128)(2,1)} %param.9) | copy-start | bytes 5505028
  2.2 1.5 %copy-start.2 = (bf16[32,7,4096]{2,0,1:T(8,128)(2,1)S(1)}, bf16[32,7,4096]{2,0,1:T(8,128)(2,1)}, u32[]{:S(2)}) copy-start(bf16[32,7,4096]{2,0,1:T(8,128)(2,1)} %param.10) | copy-start | bytes 5505028
  3.7 0.7 copy-start.5
  4.4 0.7 copy-start.8
  5.1 5.3 %copy-start.7 = (s32[32,2]{0,1:T(2,128)S(1)}, s32[32,2]{0,1:T(2,128)}, u32[]{:S(2)}) copy-start(s32[32,2]{0,1:T(2,128)} %param.7) | copy-start | bytes 772
  5.1 18.6 %copy-start.1 = (bf16[32,7,4096]{2,0,1:T(8,128)(2,1)S(1)}, bf16[32,7,4096]{2,0,1:T(8,128)(2,1)}, u32[]{:S(2)}) copy-start(bf16[32,7,4096]{2,0,1:T(8,128)(2,1)} %param.9) | copy-start | bytes 5505028
  5.1 18.6 %copy-start.3 = (bf16[32,7,4096]{2,0,1:T(8,128)(2,1)S(1)}, bf16[32,7,4096]{2,0,1:T(8,128)(2,1)}, u32[]{:S(2)}) copy-start(bf16[32,7,4096]{2,0,1:T(8,128)(2,1)} %param.10) | copy-start | bytes 5505028
  5.1 18.6 %copy-start.6 = (s32[32,7]{0,1:T(8,128)S(1)}, s32[32,7]{0,1:T(8,128)}, u32[]{:S(2)}) copy-start(s32[32,7]{0,1:T(8,128)} %param.11) | copy-start | bytes 2692
  9.7 18.3 %collective-permute-start.3 = (bf16[2,8,64,512]{3,2,1,0:T(8,128)(2,1)S(1)}, bf16[2,8,64,512]{3,2,1,0:T(8,128)(2,1)S(1)}, u32[]{:S(2)}, u32[]{:S(2)}) collective-permute-start(bf16[2,8,64,512]{3,2,1,0:T(8,128)(2,1)S(1)} %get-tuple-element.38), channel_id=1, source_target_pairs={{0,1},{1,0},{2,3},{3,2},{4,5},{5,4},{6,7},{7,6},{8,9},{9,8},{10,11... | collective-permute-start | bytes 3145736 | tf_op jit(solution)/shard_map/ppermute | solution.py:465
  10.2 21.1 %collective-permute-start.4 = (bf16[2,8,64,512]{3,2,1,0:T(8,128)(2,1)S(1)}, bf16[2,8,64,512]{3,2,1,0:T(8,128)(2,1)S(1)}, u32[]{:S(2)}, u32[]{:S(2)}) collective-permute-start(bf16[2,8,64,512]{3,2,1,0:T(8,128)(2,1)S(1)} %get-tuple-element.42), channel_id=1, source_target_pairs={{0,1},{1,0},{2,3},{3,2},{4,5},{5,4},{6,7},{7,6},{8,9},{9,8},{10,11... | collective-permute-start | bytes 3145736 | tf_op jit(solution)/shard_map/ppermute | solution.py:465
  10.3 1.0 %copy-start.4 = (bf16[32,4096]{1,0:T(8,128)(2,1)S(1)}, bf16[32,4096]{1,0:T(8,128)(2,1)}, u32[]{:S(2)}) copy-start(bf16[32,4096]{1,0:T(8,128)(2,1)} %start_ref.1) | copy-start | bytes 786436
  12.8 7.7 %collective-permute-start = (bf16[288,128]{1,0:T(8,128)(2,1)S(1)}, bf16[288,128]{1,0:T(8,128)(2,1)S(1)}, u32[]{:S(2)}, u32[]{:S(2)}) collective-permute-start(bf16[288,128]{1,0:T(8,128)(2,1)S(1)} %get-tuple-element.35), channel_id=1, source_target_pairs={{0,4},{1,13},{2,6},{3,15},{4,8},{5,1},{6,10},{7,3},{8,12},{9,5},{1... | collective-permute-start | bytes 221192 | tf_op jit(solution)/shard_map/ppermute | solution.py:484
  15.8 4.7 %collective-permute-start.1 = (bf16[288,128]{1,0:T(8,128)(2,1)S(1)}, bf16[288,128]{1,0:T(8,128)(2,1)S(1)}, u32[]{:S(2)}, u32[]{:S(2)}) collective-permute-start(bf16[288,128]{1,0:T(8,128)(2,1)S(1)} %get-tuple-element.36), channel_id=1, source_target_pairs={{0,0},{1,9},{2,2},{3,11},{4,4},{5,13},{6,6},{7,15},{8,8},{9,1},{10... | collective-permute-start | bytes 221192 | tf_op jit(solution)/shard_map/ppermute | solution.py:484
  20.5 7.5 %collective-permute-start.2 = (f32[8,128]{1,0:T(8,128)S(1)}, f32[8,128]{1,0:T(8,128)S(1)}, u32[]{:S(2)}, u32[]{:S(2)}) collective-permute-start(f32[8,128]{1,0:T(8,128)S(1)} %sums.1.refs_2_), channel_id=1, source_target_pairs={{0,1},{1,0},{2,3},{3,2},{4,5},{5,4},{6,7},{7,6},{8,9},{9,8},{10,11... | collective-permute-start | bytes 12296 | tf_op jit(solution)/shard_map/ppermute | solution.py:465
  29.7 5.5 %collective-permute-start.8 = (f32[8,32,128]{2,1,0:T(8,128)S(1)}, f32[8,32,128]{2,1,0:T(8,128)S(1)}, u32[]{:S(2)}, u32[]{:S(2)}) collective-permute-start(f32[8,32,128]{2,1,0:T(8,128)S(1)} %get-tuple-element.51.refs_1_), channel_id=1, source_target_pairs={{0,2},{1,3},{2,0},{3,1},{4,6},{5,7},{6,4},{7,5},{8,10},{9,11},{10,... | collective-permute-start | bytes 393224 | tf_op jit(solution)/shard_map/ppermute | solution.py:503
  33.0 6.1 %collective-permute-start.5 = (f32[8,32,128]{2,1,0:T(8,128)S(1)}, f32[8,32,128]{2,1,0:T(8,128)S(1)}, u32[]{:S(2)}, u32[]{:S(2)}) collective-permute-start(f32[8,32,128]{2,1,0:T(8,128)S(1)} %get-tuple-element.43.refs_1_), channel_id=1, source_target_pairs={{0,2},{1,3},{2,0},{3,1},{4,6},{5,7},{6,4},{7,5},{8,10},{9,11},{10,... | collective-permute-start | bytes 393224 | tf_op jit(solution)/shard_map/ppermute | solution.py:503
  36.8 5.9 %collective-permute-start.9 = (f32[8,32,128]{2,1,0:T(8,128)S(1)}, f32[8,32,128]{2,1,0:T(8,128)S(1)}, u32[]{:S(2)}, u32[]{:S(2)}) collective-permute-start(f32[8,32,128]{2,1,0:T(8,128)S(1)} %get-tuple-element.53.refs_1_), channel_id=1, source_target_pairs={{0,2},{1,3},{2,0},{3,1},{4,6},{5,7},{6,4},{7,5},{8,10},{9,11},{10,... | collective-permute-start | bytes 393224 | tf_op jit(solution)/shard_map/ppermute | solution.py:511
  40.7 6.3 %collective-permute-start.6 = (f32[8,32,128]{2,1,0:T(8,128)S(1)}, f32[8,32,128]{2,1,0:T(8,128)S(1)}, u32[]{:S(2)}, u32[]{:S(2)}) collective-permute-start(f32[8,32,128]{2,1,0:T(8,128)S(1)} %get-tuple-element.45.refs_1_), channel_id=1, source_target_pairs={{0,2},{1,3},{2,0},{3,1},{4,6},{5,7},{6,4},{7,5},{8,10},{9,11},{10,... | collective-permute-start | bytes 393224 | tf_op jit(solution)/shard_map/ppermute | solution.py:511
  44.3 6.8 %collective-permute-start.10 = (f32[8,32,128]{2,1,0:T(8,128)S(1)}, f32[8,32,128]{2,1,0:T(8,128)S(1)}, u32[]{:S(2)}, u32[]{:S(2)}) collective-permute-start(f32[8,32,128]{2,1,0:T(8,128)S(1)} %get-tuple-element.55.refs_9_), channel_id=1, source_target_pairs={{0,2},{1,3},{2,0},{3,1},{4,6},{5,7},{6,4},{7,5},{8,10},{9,11},{10,... | collective-permute-start | bytes 393224 | tf_op jit(solution)/shard_map/ppermute | solution.py:511
  48.6 5.0 %collective-permute-start.7 = (f32[8,32,128]{2,1,0:T(8,128)S(1)}, f32[8,32,128]{2,1,0:T(8,128)S(1)}, u32[]{:S(2)}, u32[]{:S(2)}) collective-permute-start(f32[8,32,128]{2,1,0:T(8,128)S(1)} %get-tuple-element.47.refs_1_), channel_id=1, source_target_pairs={{0,2},{1,3},{2,0},{3,1},{4,6},{5,7},{6,4},{7,5},{8,10},{9,11},{10,... | collective-permute-start | bytes 393224 | tf_op jit(solution)/shard_map/ppermute | solution.py:511
  54.2 1.2 %collective-permute-start.11 = (f32[32,128]{1,0:T(8,128)S(1)}, f32[32,128]{1,0:T(8,128)S(1)}, u32[]{:S(2)}, u32[]{:S(2)}) collective-permute-start(f32[32,128]{1,0:T(8,128)S(1)} %get-tuple-element.59.table_ref), channel_id=1, source_target_pairs={{0,1},{1,0},{2,3},{3,2},{4,5},{5,4},{6,7},{7,6},{8,9},{9,8},{10,11... | collective-permute-start | bytes 49160 | tf_op jit(solution)/shard_map/ppermute | solution.py:465
  56.0 1.2 %collective-permute-start.12 = (bf16[960,128]{1,0:T(8,128)(2,1)S(1)}, bf16[960,128]{1,0:T(8,128)(2,1)S(1)}, u32[]{:S(2)}, u32[]{:S(2)}) collective-permute-start(bf16[960,128]{1,0:T(8,128)(2,1)S(1)} %get-tuple-element.62), channel_id=1, source_target_pairs={{0,0},{9,1},{2,2},{11,3},{4,4},{13,5},{6,6},{15,7},{8,8},{1,9},{10... | collective-permute-start | bytes 737288 | tf_op jit(solution)/shard_map/ppermute | solution.py:525
  56.7 12.3 %collective-permute-start.13 = (bf16[960,128]{1,0:T(8,128)(2,1)S(1)}, bf16[960,128]{1,0:T(8,128)(2,1)S(1)}, u32[]{:S(2)}, u32[]{:S(2)}) collective-permute-start(bf16[960,128]{1,0:T(8,128)(2,1)S(1)} %get-tuple-element.63), channel_id=1, source_target_pairs={{4,0},{13,1},{6,2},{15,3},{8,4},{1,5},{10,6},{3,7},{12,8},{5,9},{1... | collective-permute-start | bytes 737288 | tf_op jit(solution)/shard_map/ppermute | solution.py:525
  57.2 12.9 %collective-permute-start.14 = (bf16[960,128]{1,0:T(8,128)(2,1)S(1)}, bf16[960,128]{1,0:T(8,128)(2,1)S(1)}, u32[]{:S(2)}, u32[]{:S(2)}) collective-permute-start(bf16[960,128]{1,0:T(8,128)(2,1)S(1)} %collective-permute-done.12.refs_4_), channel_id=1, source_target_pairs={{0,1},{1,0},{2,3},{3,2},{4,5},{5,4},{6,7},{7,6},{8,9},{9,8},{10,11... | collective-permute-start | bytes 737288 | tf_op jit(solution)/shard_map/ppermute | solution.py:465
  69.0 1.5 %collective-permute-start.15 = (bf16[960,128]{1,0:T(8,128)(2,1)S(1)}, bf16[960,128]{1,0:T(8,128)(2,1)S(1)}, u32[]{:S(2)}, u32[]{:S(2)}) collective-permute-start(bf16[960,128]{1,0:T(8,128)(2,1)S(1)} %collective-permute-done.13.refs_5_), channel_id=1, source_target_pairs={{0,1},{1,0},{2,3},{3,2},{4,5},{5,4},{6,7},{7,6},{8,9},{9,8},{10,11... | collective-permute-start | bytes 737288 | tf_op jit(solution)/shard_map/ppermute | solution.py:465

commit v3 on v2

--- a/solution.py
+++ b/solution.py
@@ -13,6 +13,12 @@
 F32 = jnp.float32
 BF16 = jnp.bfloat16
 VMEM_LIMIT = 24 * 1024 * 1024
+ROOMY = 32 * 1024 * 1024
+ARRANGE = 32 * 1024 * 1024
+
+
+def position():
+    return lax.axis_index("sector"), lax.axis_index("op") % 2
 
 
 def iota(shape, dim):
@@ -91,8 +97,9 @@
     return high, middle, low
 
 
-def call(kernel, name, out_shape, operands, kinds, scratch=(), out_kinds=None, cost=2.0):
-    space = {"s": pltpu.SMEM, "v": pltpu.VMEM, "a": pl.ANY}
+def call(kernel, name, out_shape, operands, kinds, scratch=(), out_kinds=None, cost=2.0, limit=VMEM_LIMIT,
+         compute=False):
+    space = {"s": pltpu.SMEM, "v": pltpu.VMEM, "h": pltpu.HBM, "a": pl.ANY}
     out_kinds = out_kinds or "v" * len(out_shape)
     return pl.pallas_call(
         kernel,
@@ -100,86 +107,63 @@
         in_specs=[pl.BlockSpec(memory_space=space[k]) for k in kinds],
         out_specs=tuple(pl.BlockSpec(memory_space=space[k]) for k in out_kinds),
         scratch_shapes=list(scratch),
-        compiler_params=pltpu.CompilerParams(vmem_limit_bytes=VMEM_LIMIT),
-        cost_estimate=pl.CostEstimate(flops=0, bytes_accessed=int(cost * 3.0e6), transcendentals=0),
+        compiler_params=pltpu.CompilerParams(vmem_limit_bytes=limit),
+        cost_estimate=pl.CostEstimate(
+            flops=int(cost * 1.0e9) if compute else 0,
+            bytes_accessed=1024 if compute else int(cost * 3.0e6),
+            transcendentals=0,
+        ),
         name=name,
     )(*operands)
 
 
-def sort_slots(core, offset_ref, order_ref, place_ref, seen):
+def sort_slots(core, meta_ref, order_ref, seen):
     slots = order_ref.shape[0]
     nodes = seen.shape[0]
     cap = slots // nodes
     for o in range(nodes):
         seen[o] = 0
     for j in range(slots):
-        o = offset_ref[j]
+        o = meta_ref[0, j]
         rank = seen[o]
         seen[o] = rank + 1
         place = o * cap + rank + core * (slots // 2)
-        place = jnp.where(place >= slots, place - slots, place)
-        order_ref[place] = j
-        place_ref[j] = place
-
-
-def arrange(order_ref, base, chan_ref, raw, wait, outs):
-    chans, slots = raw.shape[1:3]
-    cap = outs[0].shape[1]
-    count = cap * len(outs)
-    first = blocks_first(order_ref, base, count, slots)
+        order_ref[jnp.where(place >= slots, place - slots, place)] = j
+
+
+def arrange_kernel(masked, order_ref, meta_ref, env_ref, _, *outs):
+    chans, slots = env_ref.shape[:2]
+    cap = outs[0].shape[0]
+    first = blocks_first(order_ref, 0, slots, slots)
     second = pair_to_kept()
     low = iota((1, 2 * LANES), 1) % LANES < B
     blank = jnp.zeros((slots, LANES), BF16)
-    for t in range(2):
-        for g in range(4):
-            used = [w for w in (2 * g, 2 * g + 1) if w < chans]
-            for w in used:
-                wait(t, w)
-            chunks = []
-            for c in range(4):
-                rows = []
-                for i in range(8 * c, 8 * c + 8):
-                    parts = [raw[t, w, :, i * LANES : (i + 1) * LANES] for w in used]
-                    rows.append(jnp.concatenate(parts + [blank] * (2 - len(used)), axis=1))
-                x = jnp.concatenate(rows, axis=0)
-                x = jnp.dot(first, x, preferred_element_type=F32).astype(BF16)
-                chunks.append(jnp.dot(x, second, preferred_element_type=F32))
-            for k in range(count):
-                x = jnp.concatenate([chunk[8 * k : 8 * k + 8] for chunk in chunks], axis=0)
-                if t == 0:
-                    slot = order_ref[base + k]
-                    kept = [chan_ref[w, slot].astype(F32) for w in used]
-                    x = x * jnp.where(low, kept[0], kept[-1])
-                x = x.astype(BF16)
-                for p in range(2):
-                    outs[k // cap][t, k % cap, p * HALF : (p + 1) * HALF, g * LANES : (g + 1) * LANES] = x[
-                        :, p * LANES : (p + 1) * LANES
-                    ]
-
-
-def fetcher(left_ref, right_ref, raw, sems):
-    def copy(t, w):
-        return pltpu.make_async_copy((left_ref, right_ref)[t].at[w], raw.at[t, w], sems.at[t, w])
-
-    for t in range(2):
-        for w in range(raw.shape[1]):
-            copy(t, w).start()
-    return lambda t, w: copy(t, w).wait()
-
-
-def send_kernel(me_ref, offset_ref, chan_ref, left_ref, right_ref, order_ref, place_ref, near_ref, far_ref,
-                raw, sems, seen):
-    wait = fetcher(left_ref, right_ref, raw, sems)
-    sort_slots(me_ref[1], offset_ref, order_ref, place_ref, seen)
-    arrange(order_ref, order_ref.shape[0] // 2, chan_ref, raw, wait, (near_ref, far_ref))
-
-
-def keep_kernel(order_ref, chan_ref, left_ref, right_ref, near_ref, far_ref, raw, sems):
-    wait = fetcher(left_ref, right_ref, raw, sems)
-    arrange(order_ref, 0, chan_ref, raw, wait, (near_ref, far_ref))
-
-
-def ship_kernel(order_ref, ext_ref, start_ref, near_ref, far_ref, home_ref):
+    for g in range(4):
+        used = [w for w in (2 * g, 2 * g + 1) if w < chans]
+        chunks = []
+        for c in range(4):
+            rows = []
+            for i in range(8 * c, 8 * c + 8):
+                parts = [env_ref[w, :, i * LANES : (i + 1) * LANES] for w in used]
+                rows.append(jnp.concatenate(parts + [blank] * (2 - len(used)), axis=1))
+            x = jnp.concatenate(rows, axis=0)
+            x = jnp.dot(first, x, preferred_element_type=F32).astype(BF16)
+            chunks.append(jnp.dot(x, second, preferred_element_type=F32))
+        for k in range(slots):
+            x = jnp.concatenate([chunk[8 * k : 8 * k + 8] for chunk in chunks], axis=0)
+            if masked:
+                slot = order_ref[k]
+                kept = [meta_ref[3 + w, slot].astype(F32) for w in used]
+                x = x * jnp.where(low, kept[0], kept[-1])
+            x = x.astype(BF16)
+            for p in range(2):
+                outs[k // cap][k % cap, p * HALF : (p + 1) * HALF, g * LANES : (g + 1) * LANES] = x[
+                    :, p * LANES : (p + 1) * LANES
+                ]
+
+
+def ship_kernel(meta_ref, start_ref, order_ref, near_ref, far_ref, home_ref, seen):
+    sort_slots(position()[1], meta_ref, order_ref, seen)
     slots = start_ref.shape[0]
     cap = slots // 4
     first = blocks_first(order_ref, 0, slots, slots)
@@ -193,7 +177,7 @@
     for k in range(slots):
         slot = order_ref[k]
         x = jnp.concatenate([chunk[8 * k : 8 * k + 8] for chunk in chunks], axis=0)
-        x = x * inside(ext_ref[0, slot].astype(F32), ext_ref[1, slot].astype(F32))
+        x = x * inside(meta_ref[1, slot].astype(F32), meta_ref[2, slot].astype(F32))
         home_ref[HALF * k : HALF * (k + 1), :] = x.astype(BF16)
         if k < 2 * cap:
             (near_ref, far_ref)[k // cap][HALF * (k % cap) : HALF * (k % cap + 1), :] = x.astype(BF16)
@@ -208,7 +192,7 @@
         lines = []
         for d in range(2):
             for k in range(cap):
-                lines.append(jnp.full((1, LANES), ext_ref[d, order_ref[t * cap + k]].astype(F32)))
+                lines.append(jnp.full((1, LANES), meta_ref[1 + d, order_ref[t * cap + k]].astype(F32)))
         ref[HALF * cap :, :] = jnp.concatenate(lines + pieces + [blank], axis=0).astype(BF16)
 
 
@@ -216,7 +200,7 @@
     return ref[ref.shape[0] - 32 :, :].astype(F32)
 
 
-def sums_kernel(near_ref, far_ref, out_ref):
+def sums_kernel(near_ref, far_ref, _, out_ref):
     lines = []
     for ref in (near_ref, far_ref):
         n = note(ref)
@@ -243,13 +227,14 @@
     )
 
 
-def product(q_ref, keep_ref, got_ref, y_ref, inner_ref, rounded):
+def product(q_ref, envs, y_ref, inner_ref, rounded):
     count = q_ref.shape[0]
     span = 2 * LANES
+    keep_left, keep_right, got_left, got_right = envs
     for s in range(count):
         high, low = split(block_diagonal(q_ref[s]))
         left = jnp.concatenate(
-            [ref[0, s, :, g * span : (g + 1) * span] for ref in (keep_ref, got_ref) for g in range(2)], axis=0
+            [ref[s, :, g * span : (g + 1) * span] for ref in (keep_left, got_left) for g in range(2)], axis=0
         )
         inner = jnp.dot(left, high, preferred_element_type=F32)
         if not rounded:
@@ -259,15 +244,15 @@
             inner_ref[s, :B, k * span : (k + 1) * span] = high[k * B : (k + 1) * B]
             inner_ref[s, B:, k * span : (k + 1) * span] = low[k * B : (k + 1) * B]
     for s in range(count):
-        right = jnp.concatenate([keep_ref[1, s], got_ref[1, s]], axis=1)
+        right = jnp.concatenate([keep_right[s], got_right[s]], axis=1)
         both = lax.dot_general(inner_ref[s], right, (((1,), (1,)), ((), ())), preferred_element_type=F32)
         image = both[:B] + both[B:]
         y_ref[s] = jnp.concatenate([image[:HALF], image[HALF:]], axis=1)
 
 
-def start_kernel(count, nodes, me_ref, ship_ref, sums_ref, more_ref, keep_ref, got_ref, q_ref, y_ref, scale_ref,
-                 inner_ref):
-    node, core = me_ref[0], me_ref[1]
+def start_kernel(count, nodes, ship_ref, sums_ref, more_ref, *refs):
+    envs, (q_ref, y_ref, scale_ref, inner_ref) = refs[:4], refs[4:]
+    node, core = position()
     by_node = []
     for e in range(nodes):
         value = jnp.zeros((1, LANES), F32)
@@ -281,7 +266,7 @@
     scale_ref[...] = jnp.broadcast_to(scale, scale_ref.shape)
     for s in range(q_ref.shape[0]):
         q_ref[s] = ship_ref[HALF * s : HALF * (s + 1), :].astype(F32) * scale
-    product(q_ref, keep_ref, got_ref, y_ref, inner_ref, True)
+    product(q_ref, envs, y_ref, inner_ref, True)
 
 
 def orthogonal(ship_ref, own_ref, other_ref, basis, q_ref):
@@ -306,43 +291,46 @@
 def step_kernel(count, *refs):
     ship_ref, own_ref, other_ref = refs[:3]
     basis = refs[3 : 3 + count]
-    keep_ref, got_ref, q_ref, y_ref, along_ref, inner_ref = refs[3 + count :]
+    envs = refs[3 + count : 7 + count]
+    q_ref, y_ref, along_ref, *parcel_ref, inner_ref = refs[7 + count :]
     rows = orthogonal(ship_ref, own_ref, other_ref, basis, q_ref)
     along_ref[...] = jnp.concatenate(rows + [jnp.zeros((8 - count, LANES), F32)], axis=0)
-    product(q_ref, keep_ref, got_ref, y_ref, inner_ref, False)
+    for ref in parcel_ref:
+        vectors = [r[...].reshape(-1, LANES) for r in (*basis[1:], q_ref)]
+        ref[...] = jnp.concatenate(vectors, axis=0).astype(BF16)
+    product(q_ref, envs, y_ref, inner_ref, False)
+
+
+def line_of(values):
+    lane = iota((1, LANES), 1)
+    line = jnp.zeros((1, LANES), F32)
+    for k, value in enumerate(values):
+        line = jnp.where(lane == k, value, line)
+    return line
 
 
 def table_kernel(*refs):
     out_refs, table_ref = refs[16:18], refs[18]
-    rows = []
+    lines = []
     for t in range(2):
         ship_ref, own_ref, other_ref, q0, q1, q2, c1, c2 = refs[8 * t : 8 * t + 8]
         last = orthogonal(ship_ref, own_ref, other_ref, (q0, q1, q2), out_refs[t])
         vectors = [ref[...].reshape(-1, LANES) for ref in (q0, q1, q2, out_refs[t])]
-        for i in range(4):
-            for j in range(i, 4):
-                rows.append(wide(total_of(vectors[i] * vectors[j])))
-        rows += [c1[0:1], c2[0:1], c2[1:2]] + last
-    table_ref[...] = jnp.concatenate(rows, axis=0)
-
-
-def pack_kernel(me_ref, table_ref, other_ref, *refs):
-    core = me_ref[1]
-    mine, other = table_ref[...], other_ref[...]
-    tables = jnp.concatenate(
-        [jnp.where(core == 0, mine, other), jnp.where(core == 0, other, mine)], axis=0
-    )
-    pieces = split_three(tables)
-    for t in range(2):
-        out_ref = refs[6 + t]
-        at = 0
-        for ref in refs[3 * t : 3 * t + 3]:
-            rows = ref.shape[0] * HALF
-            out_ref[at : at + rows, :] = ref[...].reshape(rows, LANES).astype(BF16)
-            at += rows
-        for piece in pieces:
-            out_ref[at : at + piece.shape[0], :] = piece
-            at += piece.shape[0]
+        values = [total_of(vectors[i] * vectors[j]) for i in range(4) for j in range(i, 4)]
+        lines.append(line_of(values + [c1[0:1], c2[0:1], c2[1:2]] + last))
+    table_ref[...] = jnp.concatenate(lines + [jnp.zeros((6, LANES), F32)], axis=0)
+
+
+def pack_kernel(table_ref, other_ref, *refs):
+    core = position()[1]
+    mine, other = table_ref[0:2, :], other_ref[0:2, :]
+    lines = jnp.concatenate([jnp.where(core == 0, mine, other), jnp.where(core == 0, other, mine)], axis=0)
+    pieces = [v.astype(F32) for v in split_three(lines)]
+    tail = jnp.concatenate(pieces + [jnp.zeros((4, LANES), F32)], axis=0).astype(BF16)
+    for ref, out_ref in zip(refs[:2], refs[2:]):
+        rows = ref.shape[0] * HALF
+        out_ref[:rows, :] = ref[...].reshape(rows, LANES).astype(BF16)
+        out_ref[rows:, :] = tail
 
 
 def combine(count, take):
@@ -389,37 +377,34 @@
     return projections, rest
 
 
-def finish_kernel(count, nodes, me_ref, order_ref, scale_ref, home_ref, near_ref, far_ref, near_more_ref,
-                  far_more_ref, out_ref, proj_ref, tables):
-    node, core = me_ref[0], me_ref[1]
+def finish_kernel(count, nodes, order_ref, scale_ref, home_ref, *refs):
+    early, late, (out_ref, proj_ref) = refs[:4], refs[4:8], refs[8:]
+    node, core = position()
     slots = out_ref.shape[0]
     rows = home_ref.shape[0] // 4
-    size = 4 * 16
     sources = []
-    for k, ref in enumerate((near_ref, far_ref, near_more_ref, far_more_ref)):
-        c = core if k < 2 else 1 - core
-        hop = 2 * c + k % 2
+    lines = [jnp.zeros((4, LANES), F32) for _ in range(nodes)]
+    for k, ref in enumerate(late):
+        hop = 2 * (core if k < 2 else 1 - core) + k % 2
         host = lax.rem(node + hop, nodes)
-        pieces = [ref[3 * rows + d * size : 3 * rows + (d + 1) * size, :].astype(F32) for d in range(3)]
-        tables[pl.ds(pl.multiple_of(host * size, size), size), :] = pieces[0] + pieces[1] + pieces[2]
-        sources.append((ref, host * 4 + hop))
+        tail = ref[rows:, :].astype(F32)
+        four = tail[0:4] + tail[4:8] + tail[8:12]
+        lines = [jnp.where(host == e, four, v) for e, v in enumerate(lines)]
+        sources.append((early[k], ref, host * 4 + hop))
+    table = jnp.concatenate(lines, axis=0)
     sets = 4 * nodes
-    projections, rest = combine(count, lambda k: tables[pl.ds(k, sets, stride=16), :])
-    lines = []
-    for i in range(ITERS):
-        line = jnp.zeros((1, LANES), F32)
-        for k in range(i, ITERS):
-            line = jnp.where(iota((1, LANES), 1) == k, projections[i, k], line)
-        lines.append(line)
-    proj_ref[...] = jnp.concatenate(lines + [jnp.zeros((8 - ITERS, LANES), F32)], axis=0)
+    projections, rest = combine(
+        count, lambda k: jnp.broadcast_to(table[:, k : k + 1], (sets, LANES)))
+    lines = [line_of([projections.get((i, k), 0.0) for k in range(ITERS)]) for i in range(ITERS)]
+    proj_ref[...] = jnp.concatenate(lines, axis=0)[:, :ITERS]
     scale = scale_ref[0:1, :]
     blocks = []
-    for k, (ref, index) in enumerate(sources):
+    for k, (two, one, index) in enumerate(sources):
         mine = iota((sets, LANES), 0) == index
         coeff = [jnp.sum(jnp.where(mine, v, 0.0), axis=0, keepdims=True) for v in rest]
         x = coeff[0] * (home_ref[rows * k : rows * (k + 1), :].astype(F32) * scale)
-        for d in range(3):
-            x = x + coeff[d + 1] * ref[rows * d : rows * (d + 1), :].astype(F32)
+        x = x + coeff[1] * two[:rows, :].astype(F32) + coeff[2] * two[rows:, :].astype(F32)
+        x = x + coeff[3] * one[:rows, :].astype(F32)
         blocks.append(x)
     first = slots_last(order_ref, slots)
     second = from_kept_twice()
@@ -438,19 +423,14 @@
 def paired(start_vector, extents, offsets, env_left, env_right, channel_mask):
     nodes = lax.axis_size("sector")
     ops = lax.axis_size("op")
-    node = lax.axis_index("sector")
-    core = lax.axis_index("op") % 2
     slots = start_vector.shape[0]
-    chans = env_left.shape[1]
     cap = slots // nodes
     count = float(slots * nodes * B * B)
-    me = jnp.stack([node, core]).astype(jnp.int32)
     swap_core = [(i, i ^ 1) for i in range(ops)]
     swap_x = [(i, i ^ 2) for i in range(ops)]
     left = jnp.transpose(env_left, (1, 0, 2))
     right = jnp.transpose(env_right, (1, 0, 2))
-    chan = jnp.transpose(channel_mask)
-    ext = jnp.transpose(extents)
+    meta = jnp.concatenate([offsets[None], jnp.transpose(extents), jnp.transpose(channel_mask)], axis=0)
 
     def route(t, back):
         pairs = []
@@ -467,24 +447,26 @@
     def shape(dims, dtype=F32):
         return jax.ShapeDtypeStruct(dims, dtype)
 
-    environment = shape((2, cap, B, WIDE), BF16)
+    environment = shape((cap, B, WIDE), BF16)
     vector = shape((cap, HALF, LANES))
     tile = shape((8, LANES))
-    raw = [pltpu.VMEM((2, chans, slots, B * B), BF16), pltpu.SemaphoreType.DMA((2, chans))]
-    inner = [pltpu.VMEM((cap, LANES, 2 * WIDE), BF16)]
-
-    order, _, *send = call(
-        send_kernel, "send", (shape((slots,), jnp.int32), shape((slots,), jnp.int32), environment, environment),
-        (me, offsets, chan, left, right), "sssaa", raw + [pltpu.SMEM((nodes,), jnp.int32)], "ssvv", 3.0)
-    got = [across(x) for x in send]
     payload = shape((cap * HALF + 32, LANES), BF16)
-    *ships, home = call(
-        ship_kernel, "ship", (payload, payload, shape((slots * HALF, LANES), BF16)),
-        (order, ext, start_vector), "ssv", cost=1.0)
+    order, *ships, home = call(
+        ship_kernel, "ship",
+        (shape((slots,), jnp.int32), payload, payload, shape((slots * HALF, LANES), BF16)),
+        (meta, start_vector), "sv", [pltpu.SMEM((nodes,), jnp.int32)], "svvv", 2.0, ROOMY, True)
     ships = [lax.ppermute(x, ("sector", "op"), route(t, False)) for t, x in enumerate(ships)]
-    keep = call(
-        keep_kernel, "keep", (environment, environment), (order, chan, left, right), "ssaa", raw, cost=3.0)
-    (sums,) = call(sums_kernel, "sums", (tile,), ships, "vv", cost=0.3)
+
+    def arrange(masked, env, after):
+        sets = call(
+            lambda *refs: arrange_kernel(masked, *refs), "arrange", (environment,) * 4, (order, meta, env, after),
+            "ssva", cost=3.0, limit=ARRANGE, compute=True)
+        return sets[:2], [across(x) for x in sets[2:]]
+
+    keep_left, got_left = arrange(True, left, order)
+    (sums,) = call(sums_kernel, "sums", (tile,), (*ships, keep_left[0]), "vva", cost=0.3)
+    keep_right, got_right = arrange(False, right, sums)
+    envs = [(keep_left[t], keep_right[t], got_left[t], got_right[t]) for t in range(2)]
     more = across(sums)
 
     def start(*refs):
@@ -493,45 +475,46 @@
     def step(k):
         return lambda *refs: step_kernel(k, *refs)
 
+    inner = [pltpu.VMEM((cap, LANES, 2 * WIDE), BF16)]
     basis = [[], []]
     along = [[], []]
     images = [None, None]
+    early = []
     for t in range(2):
         q, y, scale = call(
-            start, "first", (vector, vector, tile), (me, ships[t], sums, more, keep[t], got[t]), "svvvvv", inner)
+            start, "first", (vector, vector, tile), (ships[t], sums, more, *envs[t]), "v" * 7, inner)
         basis[t].append(q)
         images[t] = (y, lax.ppermute(y, "op", swap_x))
     for k in range(1, ITERS):
         for t in range(2):
-            q, y, a = call(
-                step(k), ("second", "third")[k - 1], (vector, vector, tile),
-                (ships[t], *images[t], *basis[t], keep[t], got[t]), "v" * (5 + k), inner)
+            outs = [vector, vector, tile]
+            if k == ITERS - 1:
+                outs.append(shape((2 * cap * HALF, LANES), BF16))
+            q, y, a, *parcel = call(
+                step(k), ("second", "third")[k - 1], tuple(outs),
+                (ships[t], *images[t], *basis[t], *envs[t]), "v" * (7 + k), inner)
             basis[t].append(q)
             along[t].append(a)
             images[t] = (y, lax.ppermute(y, "op", swap_x))
+            early += [lax.ppermute(x, ("sector", "op"), route(t, True)) for x in parcel]
+    early += [across(x) for x in early]
 
     operands = []
     for t in range(2):
         operands += [ships[t], *images[t], *basis[t], *along[t]]
-    *last, table = call(
-        table_kernel, "table", (vector, vector, shape((32, LANES))), operands, "v" * 16, cost=1.0)
-    other_table = across(table)
-    vectors = []
-    for t in range(2):
-        vectors += [basis[t][1], basis[t][2], last[t]]
-    parcel = shape((3 * cap * HALF + 3 * 64, LANES), BF16)
-    parcels = call(
-        pack_kernel, "pack", (parcel, parcel), (me, table, other_table, *vectors), "s" + "v" * 8, cost=0.7)
-    parcels = [lax.ppermute(x, ("sector", "op"), route(t, True)) for t, x in enumerate(parcels)]
-    parcels += [across(x) for x in parcels]
+    *last, table = call(table_kernel, "table", (vector, vector, tile), operands, "v" * 16, cost=1.0)
+    parcel = shape((cap * HALF + 16, LANES), BF16)
+    late = call(
+        pack_kernel, "pack", (parcel, parcel), (table, across(table), *last), "vvvv", cost=0.7)
+    late = [lax.ppermute(x, ("sector", "op"), route(t, True)) for t, x in enumerate(late)]
+    late += [across(x) for x in late]
 
     def finish(*refs):
         finish_kernel(count, nodes, *refs)
 
-    residual, proj = call(
-        finish, "finish", (shape((slots, B * B)), tile), (me, order, scale, home, *parcels), "ssvvvvvv",
-        [pltpu.VMEM((4 * nodes * 16, LANES), F32)])
-    return residual, proj[:ITERS, :ITERS]
+    return call(
+        finish, "finish", (shape((slots, B * B)), shape((ITERS, ITERS))),
+        (order, scale, home, *early, *late), "s" + "v" * 10)
 
 
 def pack_rows(data, index, nodes, cap):

time: 73.6 us -> 59 us (0.80)
  Pallas kernels: 23.6 us -> 18.1 us
  local copies, waits for them, and re-layouts: 5.88 us -> 0.96 us
  starting transfers between devices: 29.1 us -> 26.6 us
  waiting for transfers between devices: 13.9 us -> 11.6 us
    pallas_call x13, Pallas kernels: 23.6 us -> 18.1 us  [call(): pl.pallas_call(kernel, out_shape=out_shape, in_specs=[pl.BlockSpec(memory...]
    unnamed x18 -> x6, local copies, waits for them, and re-layouts: 5.3 us -> 0.96 us
    ppermute x2, waiting for transfers between devices: 3.86 us -> 0.01 us  [paired(): lax.ppermute(x, ('sector', 'op'), route(t, False))]
    ppermute x6 -> x10, starting transfers between devices: 15.6 us -> 12.7 us  [across(): return lax.ppermute(x, 'op', swap_core)]
    ppermute x6 -> x10, waiting for transfers between devices: 2.69 us -> 4.52 us  [across(): return lax.ppermute(x, 'op', swap_core)]
    ppermute x0 -> x2, starting transfers between devices: none -> 1.13 us  [paired(): early += [lax.ppermute(x, ('sector', 'op'), route(t, True)) for x in parcel]]
  transfers between devices with their start and end apart: 16 -> 22, of which waited for: 9 -> 7; matrix products, arithmetic and copies ran while one was open for 0% -> 0% of each run, Pallas kernels for 21% -> 23%
where the time goes in v3:
time: 59 us; the launch traced here: 58.8 us
  starting transfers between devices  26.6 us (45%)
  Pallas kernels  18.1 us (31%)
  waiting for transfers between devices  11.6 us (20%)
  local copies, waits for them, and re-layouts  0.96 us (2%)
  between operations  0.76 us (1%)
  other arithmetic  0.71 us (1%)
    pallas_call x13, Pallas kernels, call(): pl.pallas_call(kernel, out_shape=out_shape, in_specs=[pl.BlockSpec(memory...  18.1 us
    ppermute x10, starting transfers between devices, across(): return lax.ppermute(x, 'op', swap_core)  12.7 us
    ppermute x6, starting transfers between devices, paired(): images[t] = (y, lax.ppermute(y, 'op', swap_x))  7.9 us
    ppermute x6, waiting for transfers between devices, paired(): images[t] = (y, lax.ppermute(y, 'op', swap_x))  7.07 us
    ppermute x10, waiting for transfers between devices, across(): return lax.ppermute(x, 'op', swap_core)  4.52 us
    ppermute x2, starting transfers between devices, paired(): lax.ppermute(x, ('sector', 'op'), route(t, False))  3.73 us
  transfers between devices with their start and end apart: 22, of which 7 were waited for; matrix products, arithmetic and copies ran while one was open for 0% of the time, Pallas kernels for 23%

profile of v3, /device:TPU:0, one launch (start us, length us, event | category | flops | bytes accessed | tf_op | source)
XLA Modules:
  0.0 58.8 jit_solution(9790958089351228867)
XLA Ops:
  0.6 0.7 %pad_add_fusion.meta_ref.refs_1_ = s32[10,32]{1,0:T(8,128)S(1)} fusion(s32[7,32]{1,0:T(8,128)} %bitcast.7, s32[2,32]{1,0:T(2,128)} %bitcast.8, s32[1,32]{1,0:T(1,128)} %bitcast.9), kind=kLoop, calls=%fused_computation | loop fusion | flops 640 | bytes 2560 | tf_op jit(solution)/shard_map/concatenate | solution.py:433
  1.4 0.9 %copy-done.2 = bf16[32,4096]{1,0:T(8,128)(2,1)S(1)} copy-done((bf16[32,4096]{1,0:T(8,128)(2,1)S(1)}, bf16[32,4096]{1,0:T(8,128)(2,1)}, u32[]{:S(2)}) %copy-start.2) | copy-done | bytes 262168
  2.3 2.3 %ship.1 = (s32[32]{0:T(128)S(1)}, bf16[288,128]{1,0:T(8,128)(2,1)S(1)}, bf16[288,128]{1,0:T(8,128)(2,1)S(1)}, bf16[1024,128]{1,0:T(8,128)(2,1)S(1)}) custom-call(s32[10,32]{1,0:T(8,128)S(1)} %pad_add_fusion.meta_ref.refs_1_, bf16[32,4096]{1,0:T(8,128)(2,1)S(1)} %copy-done.2), custom_call_target="tpu_custom_call" | custom-call | flops 2000000000 | bytes 1024 | tf_op jit(solution)/shard_map/ship/pallas_call | solution.py:104
  4.6 3.1 %collective-permute-start = (bf16[288,128]{1,0:T(8,128)(2,1)S(1)}, bf16[288,128]{1,0:T(8,128)(2,1)S(1)}, u32[]{:S(2)}, u32[]{:S(2)}) collective-permute-start(bf16[288,128]{1,0:T(8,128)(2,1)S(1)} %get-tuple-element.39), channel_id=1, source_target_pairs={{0,4},{1,13},{2,6},{3,15},{4,8},{5,1},{6,10},{7,3},{8,12},{9,5},{1... | collective-permute-start | bytes 221192 | tf_op jit(solution)/shard_map/ppermute | solution.py:458
  7.7 0.7 %collective-permute-start.1 = (bf16[288,128]{1,0:T(8,128)(2,1)S(1)}, bf16[288,128]{1,0:T(8,128)(2,1)S(1)}, u32[]{:S(2)}, u32[]{:S(2)}) collective-permute-start(bf16[288,128]{1,0:T(8,128)(2,1)S(1)} %get-tuple-element.40), channel_id=1, source_target_pairs={{0,0},{1,9},{2,2},{3,11},{4,4},{5,13},{6,6},{7,15},{8,8},{9,1},{10... | collective-permute-start | bytes 221192 | tf_op jit(solution)/shard_map/ppermute | solution.py:458
  8.4 0.0 copy-start.1
  8.4 2.1 %arrange.2 = (bf16[8,64,512]{2,1,0:T(8,128)(2,1)S(1)}, bf16[8,64,512]{2,1,0:T(8,128)(2,1)S(1)}, bf16[8,64,512]{2,1,0:T(8,128)(2,1)S(1)}, bf16[8,64,512]{2,1,0:T(8,128)(2,1)S(1)}) custom-call(s32[32]{0:T(128)S(1)} %get-tuple-element.38.refs_0_.refs_3_, s32[10,32]{1,0:T(8,128)S(1)} %pad_add_fusion.meta_ref.refs_1_, bf16[7,32,4096]{2,1,0:T(8,128)(2,1)S(1)} %bitcast.5, ...), custom_call_target="tpu_custom_call" | custom-call | flops 3000000000 | bytes 1024 | tf_op jit(solution)/shard_map/arrange/pallas_call | solution.py:104
  10.5 2.9 %collective-permute-start.3 = (bf16[8,64,512]{2,1,0:T(8,128)(2,1)S(1)}, bf16[8,64,512]{2,1,0:T(8,128)(2,1)S(1)}, u32[]{:S(2)}, u32[]{:S(2)}) collective-permute-start(bf16[8,64,512]{2,1,0:T(8,128)(2,1)S(1)} %get-tuple-element.44), channel_id=1, source_target_pairs={{0,1},{1,0},{2,3},{3,2},{4,5},{5,4},{6,7},{7,6},{8,9},{9,8},{10,11... | collective-permute-start | bytes 1572872 | tf_op jit(solution)/shard_map/ppermute | solution.py:445
  13.4 0.0 collective-permute-done.far_ref.refs_0_.refs_8_
  13.4 0.0 collective-permute-done.1.near_ref.refs_0_
  13.4 2.0 %arrange.3 = (bf16[8,64,512]{2,1,0:T(8,128)(2,1)S(1)}, bf16[8,64,512]{2,1,0:T(8,128)(2,1)S(1)}, bf16[8,64,512]{2,1,0:T(8,128)(2,1)S(1)}, bf16[8,64,512]{2,1,0:T(8,128)(2,1)S(1)}) custom-call(s32[32]{0:T(128)S(1)} %get-tuple-element.38.refs_0_.refs_3_, s32[10,32]{1,0:T(8,128)S(1)} %pad_add_fusion.meta_ref.refs_1_, bf16[7,32,4096]{2,1,0:T(8,128)(2,1)S(1)} %bitcast.6, ...), custom_call_target="tpu_custom_call" | custom-call | flops 3000000000 | bytes 1024 | tf_op jit(solution)/shard_map/arrange/pallas_call | solution.py:104
  15.5 1.9 %collective-permute-start.4 = (bf16[8,64,512]{2,1,0:T(8,128)(2,1)S(1)}, bf16[8,64,512]{2,1,0:T(8,128)(2,1)S(1)}, u32[]{:S(2)}, u32[]{:S(2)}) collective-permute-start(bf16[8,64,512]{2,1,0:T(8,128)(2,1)S(1)} %get-tuple-element.45), channel_id=1, source_target_pairs={{0,1},{1,0},{2,3},{3,2},{4,5},{5,4},{6,7},{7,6},{8,9},{9,8},{10,11... | collective-permute-start | bytes 1572872 | tf_op jit(solution)/shard_map/ppermute | solution.py:445
  17.4 0.1 collective-permute-start.5
  17.5 0.4 collective-permute-start.6
  17.9 0.1 collective-permute-start.2
  18.0 2.5 %collective-permute-done.2.refs_2_ = f32[8,128]{1,0:T(8,128)S(1)} collective-permute-done((f32[8,128]{1,0:T(8,128)S(1)}, f32[8,128]{1,0:T(8,128)S(1)}, u32[]{:S(2)}, u32[]{:S(2)}) %collective-permute-start.2) | collective-permute-done | bytes 4128 | tf_op jit(solution)/shard_map/ppermute | solution.py:445
  20.4 1.2 %first.2 = (f32[8,32,128]{2,1,0:T(8,128)S(1)}, f32[8,32,128]{2,1,0:T(8,128)S(1)}, f32[8,128]{1,0:T(8,128)S(1)}) custom-call(bf16[288,128]{1,0:T(8,128)(2,1)S(1)} %collective-permute-done.far_ref.refs_0_.refs_8_, f32[8,128]{1,0:T(8,128)S(1)} %sums.1.refs_3_.refs_1_, f32[8,128]{1,0:T(8,128)S(1)} %collective-permute-done.2.refs_2_, ...), custom_call_target="tpu_custom_call" | custom-call | bytes 6000000 | tf_op jit(solution)/shard_map/first/pallas_call | solution.py:104
  21.6 1.6 %collective-permute-start.10 = (f32[8,32,128]{2,1,0:T(8,128)S(1)}, f32[8,32,128]{2,1,0:T(8,128)S(1)}, u32[]{:S(2)}, u32[]{:S(2)}) collective-permute-start(f32[8,32,128]{2,1,0:T(8,128)S(1)} %get-tuple-element.56.refs_1_), channel_id=1, source_target_pairs={{0,2},{1,3},{2,0},{3,1},{4,6},{5,7},{6,4},{7,5},{8,10},{9,11},{10,... | collective-permute-start | bytes 393224 | tf_op jit(solution)/shard_map/ppermute | solution.py:487
  23.2 0.0 collective-permute-done.5.refs_5_.refs_6_.refs_7_
  23.2 0.0 collective-permute-done.6.refs_6_.refs_7_.refs_8_
  23.2 1.2 %first.3 = (f32[8,32,128]{2,1,0:T(8,128)S(1)}, f32[8,32,128]{2,1,0:T(8,128)S(1)}, f32[8,128]{1,0:T(8,128)}) custom-call(bf16[288,128]{1,0:T(8,128)(2,1)S(1)} %collective-permute-done.1.near_ref.refs_0_, f32[8,128]{1,0:T(8,128)S(1)} %sums.1.refs_3_.refs_1_, f32[8,128]{1,0:T(8,128)S(1)} %collective-permute-done.2.refs_2_, ...), custom_call_target="tpu_custom_call" | custom-call | bytes 6000000 | tf_op jit(solution)/shard_map/first/pallas_call | solution.py:104
  24.4 0.6 %collective-permute-start.7 = (f32[8,32,128]{2,1,0:T(8,128)S(1)}, f32[8,32,128]{2,1,0:T(8,128)S(1)}, u32[]{:S(2)}, u32[]{:S(2)}) collective-permute-start(f32[8,32,128]{2,1,0:T(8,128)S(1)} %get-tuple-element.51.refs_1_), channel_id=1, source_target_pairs={{0,2},{1,3},{2,0},{3,1},{4,6},{5,7},{6,4},{7,5},{8,10},{9,11},{10,... | collective-permute-start | bytes 393224 | tf_op jit(solution)/shard_map/ppermute | solution.py:487
  25.0 2.8 %collective-permute-done.10.refs_2_ = f32[8,32,128]{2,1,0:T(8,128)S(1)} collective-permute-done((f32[8,32,128]{2,1,0:T(8,128)S(1)}, f32[8,32,128]{2,1,0:T(8,128)S(1)}, u32[]{:S(2)}, u32[]{:S(2)}) %collective-permute-start.10) | collective-permute-done | bytes 131104 | tf_op jit(solution)/shard_map/ppermute | solution.py:487
  27.7 1.6 %second.3 = (f32[8,32,128]{2,1,0:T(8,128)S(1)}, f32[8,32,128]{2,1,0:T(8,128)S(1)}, f32[8,128]{1,0:T(8,128)S(1)}) custom-call(bf16[288,128]{1,0:T(8,128)(2,1)S(1)} %collective-permute-done.far_ref.refs_0_.refs_8_, f32[8,32,128]{2,1,0:T(8,128)S(1)} %get-tuple-element.56.refs_1_, f32[8,32,128]{2,1,0:T(8,128)S(1)} %collective-permute-done.10.refs_2_, ...), custom_call_target="tpu_custom_call" | custom-call | bytes 6000000 | tf_op jit(solution)/shard_map/second/pallas_call | solution.py:104
  29.3 1.8 %collective-permute-start.11 = (f32[8,32,128]{2,1,0:T(8,128)S(1)}, f32[8,32,128]{2,1,0:T(8,128)S(1)}, u32[]{:S(2)}, u32[]{:S(2)}) collective-permute-start(f32[8,32,128]{2,1,0:T(8,128)S(1)} %get-tuple-element.58.refs_1_), channel_id=1, source_target_pairs={{0,2},{1,3},{2,0},{3,1},{4,6},{5,7},{6,4},{7,5},{8,10},{9,11},{10,... | collective-permute-start | bytes 393224 | tf_op jit(solution)/shard_map/ppermute | solution.py:498
  31.1 1.6 %second.2 = (f32[8,32,128]{2,1,0:T(8,128)S(1)}, f32[8,32,128]{2,1,0:T(8,128)S(1)}, f32[8,128]{1,0:T(8,128)S(1)}) custom-call(bf16[288,128]{1,0:T(8,128)(2,1)S(1)} %collective-permute-done.1.near_ref.refs_0_, f32[8,32,128]{2,1,0:T(8,128)S(1)} %get-tuple-element.51.refs_1_, f32[8,32,128]{2,1,0:T(8,128)S(1)} %collective-permute-done.7.refs_2_, ...), custom_call_target="tpu_custom_call" | custom-call | bytes 6000000 | tf_op jit(solution)/shard_map/second/pallas_call | solution.py:104
  32.7 0.7 %collective-permute-start.8 = (f32[8,32,128]{2,1,0:T(8,128)S(1)}, f32[8,32,128]{2,1,0:T(8,128)S(1)}, u32[]{:S(2)}, u32[]{:S(2)}) collective-permute-start(f32[8,32,128]{2,1,0:T(8,128)S(1)} %get-tuple-element.53.refs_1_), channel_id=1, source_target_pairs={{0,2},{1,3},{2,0},{3,1},{4,6},{5,7},{6,4},{7,5},{8,10},{9,11},{10,... | collective-permute-start | bytes 393224 | tf_op jit(solution)/shard_map/ppermute | solution.py:498
  33.4 1.2 %collective-permute-done.11.refs_2_ = f32[8,32,128]{2,1,0:T(8,128)S(1)} collective-permute-done((f32[8,32,128]{2,1,0:T(8,128)S(1)}, f32[8,32,128]{2,1,0:T(8,128)S(1)}, u32[]{:S(2)}, u32[]{:S(2)}) %collective-permute-start.11) | collective-permute-done | bytes 131104 | tf_op jit(solution)/shard_map/ppermute | solution.py:498
  34.6 1.6 %third.3 = (f32[8,32,128]{2,1,0:T(8,128)S(1)}, f32[8,32,128]{2,1,0:T(8,128)S(1)}, f32[8,128]{1,0:T(8,128)S(1)}, bf16[512,128]{1,0:T(8,128)(2,1)S(1)}) custom-call(bf16[288,128]{1,0:T(8,128)(2,1)S(1)} %collective-permute-done.far_ref.refs_0_.refs_8_, f32[8,32,128]{2,1,0:T(8,128)S(1)} %get-tuple-element.58.refs_1_, ...), custom_call_target="tpu_custom_call" | custom-call | bytes 6000000 | tf_op jit(solution)/shard_map/third/pallas_call | solution.py:104
  36.2 2.2 %collective-permute-start.16 = (f32[8,32,128]{2,1,0:T(8,128)S(1)}, f32[8,32,128]{2,1,0:T(8,128)S(1)}, u32[]{:S(2)}, u32[]{:S(2)}) collective-permute-start(f32[8,32,128]{2,1,0:T(8,128)S(1)} %get-tuple-element.65.refs_9_), channel_id=1, source_target_pairs={{0,2},{1,3},{2,0},{3,1},{4,6},{5,7},{6,4},{7,5},{8,10},{9,11},{10,... | collective-permute-start | bytes 393224 | tf_op jit(solution)/shard_map/ppermute | solution.py:498
  38.3 0.3 collective-permute-done.8.refs_2_
  38.6 1.6 %third.2 = (f32[8,32,128]{2,1,0:T(8,128)S(1)}, f32[8,32,128]{2,1,0:T(8,128)S(1)}, f32[8,128]{1,0:T(8,128)S(1)}, bf16[512,128]{1,0:T(8,128)(2,1)S(1)}) custom-call(bf16[288,128]{1,0:T(8,128)(2,1)S(1)} %collective-permute-done.1.near_ref.refs_0_, f32[8,32,128]{2,1,0:T(8,128)S(1)} %get-tuple-element.53.refs_1_, ...), custom_call_target="tpu_custom_call" | custom-call | bytes 6000000 | tf_op jit(solution)/shard_map/third/pallas_call | solution.py:104
  40.2 1.0 %collective-permute-start.15 = (f32[8,32,128]{2,1,0:T(8,128)S(1)}, f32[8,32,128]{2,1,0:T(8,128)S(1)}, u32[]{:S(2)}, u32[]{:S(2)}) collective-permute-start(f32[8,32,128]{2,1,0:T(8,128)S(1)} %get-tuple-element.61.refs_1_), channel_id=1, source_target_pairs={{0,2},{1,3},{2,0},{3,1},{4,6},{5,7},{6,4},{7,5},{8,10},{9,11},{10,... | collective-permute-start | bytes 393224 | tf_op jit(solution)/shard_map/ppermute | solution.py:498
  41.2 0.5 collective-permute-start.12
  41.7 0.7 %collective-permute-start.9 = (bf16[512,128]{1,0:T(8,128)(2,1)S(1)}, bf16[512,128]{1,0:T(8,128)(2,1)S(1)}, u32[]{:S(2)}, u32[]{:S(2)}) collective-permute-start(bf16[512,128]{1,0:T(8,128)(2,1)S(1)} %get-tuple-element.55), channel_id=1, source_target_pairs={{0,0},{9,1},{2,2},{11,3},{4,4},{13,5},{6,6},{15,7},{8,8},{1,9},{10... | collective-permute-start | bytes 393224 | tf_op jit(solution)/shard_map/ppermute | solution.py:499
  42.4 0.0 collective-permute-done.16.refs_10_
  42.4 2.9 %collective-permute-done.15.refs_2_ = f32[8,32,128]{2,1,0:T(8,128)S(1)} collective-permute-done((f32[8,32,128]{2,1,0:T(8,128)S(1)}, f32[8,32,128]{2,1,0:T(8,128)S(1)}, u32[]{:S(2)}, u32[]{:S(2)}) %collective-permute-start.15) | collective-permute-done | bytes 131104 | tf_op jit(solution)/shard_map/ppermute | solution.py:498
  45.2 0.6 %table.1 = (f32[8,32,128]{2,1,0:T(8,128)S(1)}, f32[8,32,128]{2,1,0:T(8,128)S(1)}, f32[8,128]{1,0:T(8,128)S(1)}) custom-call(bf16[288,128]{1,0:T(8,128)(2,1)S(1)} %collective-permute-done.1.near_ref.refs_0_, f32[8,32,128]{2,1,0:T(8,128)S(1)} %get-tuple-element.61.refs_1_, f32[8,32,128]{2,1,0:T(8,128)S(1)} %collective-permute-done.15.refs_2_, ...), custom_call_target="tpu_custom_call" | custom-call | bytes 3000000 | tf_op jit(solution)/shard_map/table/pallas_call | solution.py:104
  45.9 0.1 collective-permute-start.17
  45.9 1.2 %collective-permute-done.17.other_ref = f32[8,128]{1,0:T(8,128)S(1)} collective-permute-done((f32[8,128]{1,0:T(8,128)S(1)}, f32[8,128]{1,0:T(8,128)S(1)}, u32[]{:S(2)}, u32[]{:S(2)}) %collective-permute-start.17) | collective-permute-done | bytes 4128 | tf_op jit(solution)/shard_map/ppermute | solution.py:445
  47.1 0.7 %collective-permute-start.18 = (bf16[272,128]{1,0:T(8,128)(2,1)S(1)}, bf16[272,128]{1,0:T(8,128)(2,1)S(1)}, u32[]{:S(2)}, u32[]{:S(2)}) collective-permute-start(bf16[272,128]{1,0:T(8,128)(2,1)S(1)} %get-tuple-element.72), channel_id=1, source_target_pairs={{0,0},{9,1},{2,2},{11,3},{4,4},{13,5},{6,6},{15,7},{8,8},{1,9},{10... | collective-permute-start | bytes 208904 | tf_op jit(solution)/shard_map/ppermute | solution.py:509
  47.8 0.5 collective-permute-start.19
  48.3 2.3 %collective-permute-start.14 = (bf16[512,128]{1,0:T(8,128)(2,1)S(1)}, bf16[512,128]{1,0:T(8,128)(2,1)S(1)}, u32[]{:S(2)}, u32[]{:S(2)}) collective-permute-start(bf16[512,128]{1,0:T(8,128)(2,1)S(1)} %collective-permute-done.12.refs_4_), channel_id=1, source_target_pairs={{0,1},{1,0},{2,3},{3,2},{4,5},{5,4},{6,7},{7,6},{8,9},{9,8},{10,11... | collective-permute-start | bytes 393224 | tf_op jit(solution)/shard_map/ppermute | solution.py:445
  50.7 0.1 collective-permute-start.13
  50.7 2.7 %collective-permute-start.20 = (bf16[272,128]{1,0:T(8,128)(2,1)S(1)}, bf16[272,128]{1,0:T(8,128)(2,1)S(1)}, u32[]{:S(2)}, u32[]{:S(2)}) collective-permute-start(bf16[272,128]{1,0:T(8,128)(2,1)S(1)} %collective-permute-done.18.refs_7_), channel_id=1, source_target_pairs={{0,1},{1,0},{2,3},{3,2},{4,5},{5,4},{6,7},{7,6},{8,9},{9,8},{10,11... | collective-permute-start | bytes 208904 | tf_op jit(solution)/shard_map/ppermute | solution.py:445
  53.4 2.1 %collective-permute-start.21 = (bf16[272,128]{1,0:T(8,128)(2,1)S(1)}, bf16[272,128]{1,0:T(8,128)(2,1)S(1)}, u32[]{:S(2)}, u32[]{:S(2)}) collective-permute-start(bf16[272,128]{1,0:T(8,128)(2,1)S(1)} %collective-permute-done.19.refs_8_), channel_id=1, source_target_pairs={{0,1},{1,0},{2,3},{3,2},{4,5},{5,4},{6,7},{7,6},{8,9},{9,8},{10,11... | collective-permute-start | bytes 208904 | tf_op jit(solution)/shard_map/ppermute | solution.py:445
  55.5 0.9 %collective-permute-done.21.refs_10_ = bf16[272,128]{1,0:T(8,128)(2,1)S(1)} collective-permute-done((bf16[272,128]{1,0:T(8,128)(2,1)S(1)}, bf16[272,128]{1,0:T(8,128)(2,1)S(1)}, u32[]{:S(2)}, u32[]{:S(2)}) %collective-permute-start.21) | collective-permute-done | bytes 69664 | tf_op jit(solution)/shard_map/ppermute | solution.py:445
  56.4 2.3 %finish.1 = (f32[32,4096]{1,0:T(8,128)}, f32[3,3]{1,0:T(4,128)}) custom-call(s32[32]{0:T(128)S(1)} %get-tuple-element.38.refs_0_.refs_3_, f32[8,128]{1,0:T(8,128)S(1)} %get-tuple-element.46.refs_1_, bf16[1024,128]{1,0:T(8,128)(2,1)S(1)} %get-tuple-element.47.refs_2_, bf16[512,128]{1,0:T(8,128)(2,1)S(1)} %collective-permute-done.9.refs_3_, ...), custom_call_target="tpu_custom_call" | custom-call | bytes 6000000 | tf_op jit(solution)/shard_map/finish/pallas_call | solution.py:104
  (16 shorter events, 0.1 us)
Async XLA Ops:
  1.3 1.0 %copy-start.2 = (bf16[32,4096]{1,0:T(8,128)(2,1)S(1)}, bf16[32,4096]{1,0:T(8,128)(2,1)}, u32[]{:S(2)}) copy-start(bf16[32,4096]{1,0:T(8,128)(2,1)} %start_ref.1) | copy-start | bytes 786436
  2.3 6.1 %copy-start = (bf16[32,7,4096]{2,0,1:T(8,128)(2,1)S(1)}, bf16[32,7,4096]{2,0,1:T(8,128)(2,1)}, u32[]{:S(2)}) copy-start(bf16[32,7,4096]{2,0,1:T(8,128)(2,1)} %param.9) | copy-start | bytes 5505028
  4.6 8.8 %collective-permute-start = (bf16[288,128]{1,0:T(8,128)(2,1)S(1)}, bf16[288,128]{1,0:T(8,128)(2,1)S(1)}, u32[]{:S(2)}, u32[]{:S(2)}) collective-permute-start(bf16[288,128]{1,0:T(8,128)(2,1)S(1)} %get-tuple-element.39), channel_id=1, source_target_pairs={{0,4},{1,13},{2,6},{3,15},{4,8},{5,1},{6,10},{7,3},{8,12},{9,5},{1... | collective-permute-start | bytes 221192 | tf_op jit(solution)/shard_map/ppermute | solution.py:458
  7.7 5.7 %collective-permute-start.1 = (bf16[288,128]{1,0:T(8,128)(2,1)S(1)}, bf16[288,128]{1,0:T(8,128)(2,1)S(1)}, u32[]{:S(2)}, u32[]{:S(2)}) collective-permute-start(bf16[288,128]{1,0:T(8,128)(2,1)S(1)} %get-tuple-element.40), channel_id=1, source_target_pairs={{0,0},{1,9},{2,2},{3,11},{4,4},{5,13},{6,6},{7,15},{8,8},{9,1},{10... | collective-permute-start | bytes 221192 | tf_op jit(solution)/shard_map/ppermute | solution.py:458
  8.4 5.1 %copy-start.1 = (bf16[32,7,4096]{2,0,1:T(8,128)(2,1)S(1)}, bf16[32,7,4096]{2,0,1:T(8,128)(2,1)}, u32[]{:S(2)}) copy-start(bf16[32,7,4096]{2,0,1:T(8,128)(2,1)} %param.10) | copy-start | bytes 5505028
  10.5 9.9 %collective-permute-start.3 = (bf16[8,64,512]{2,1,0:T(8,128)(2,1)S(1)}, bf16[8,64,512]{2,1,0:T(8,128)(2,1)S(1)}, u32[]{:S(2)}, u32[]{:S(2)}) collective-permute-start(bf16[8,64,512]{2,1,0:T(8,128)(2,1)S(1)} %get-tuple-element.44), channel_id=1, source_target_pairs={{0,1},{1,0},{2,3},{3,2},{4,5},{5,4},{6,7},{7,6},{8,9},{9,8},{10,11... | collective-permute-start | bytes 1572872 | tf_op jit(solution)/shard_map/ppermute | solution.py:445
  15.5 5.0 %collective-permute-start.4 = (bf16[8,64,512]{2,1,0:T(8,128)(2,1)S(1)}, bf16[8,64,512]{2,1,0:T(8,128)(2,1)S(1)}, u32[]{:S(2)}, u32[]{:S(2)}) collective-permute-start(bf16[8,64,512]{2,1,0:T(8,128)(2,1)S(1)} %get-tuple-element.45), channel_id=1, source_target_pairs={{0,1},{1,0},{2,3},{3,2},{4,5},{5,4},{6,7},{7,6},{8,9},{9,8},{10,11... | collective-permute-start | bytes 1572872 | tf_op jit(solution)/shard_map/ppermute | solution.py:445
  17.4 5.8 %collective-permute-start.5 = (bf16[8,64,512]{2,1,0:T(8,128)(2,1)S(1)}, bf16[8,64,512]{2,1,0:T(8,128)(2,1)S(1)}, u32[]{:S(2)}, u32[]{:S(2)}) collective-permute-start(bf16[8,64,512]{2,1,0:T(8,128)(2,1)S(1)} %get-tuple-element.49), channel_id=1, source_target_pairs={{0,1},{1,0},{2,3},{3,2},{4,5},{5,4},{6,7},{7,6},{8,9},{9,8},{10,11... | collective-permute-start | bytes 1572872 | tf_op jit(solution)/shard_map/ppermute | solution.py:445
  17.5 5.7 %collective-permute-start.6 = (bf16[8,64,512]{2,1,0:T(8,128)(2,1)S(1)}, bf16[8,64,512]{2,1,0:T(8,128)(2,1)S(1)}, u32[]{:S(2)}, u32[]{:S(2)}) collective-permute-start(bf16[8,64,512]{2,1,0:T(8,128)(2,1)S(1)} %get-tuple-element.50), channel_id=1, source_target_pairs={{0,1},{1,0},{2,3},{3,2},{4,5},{5,4},{6,7},{7,6},{8,9},{9,8},{10,11... | collective-permute-start | bytes 1572872 | tf_op jit(solution)/shard_map/ppermute | solution.py:445
  17.9 2.5 %collective-permute-start.2 = (f32[8,128]{1,0:T(8,128)S(1)}, f32[8,128]{1,0:T(8,128)S(1)}, u32[]{:S(2)}, u32[]{:S(2)}) collective-permute-start(f32[8,128]{1,0:T(8,128)S(1)} %sums.1.refs_3_.refs_1_), channel_id=1, source_target_pairs={{0,1},{1,0},{2,3},{3,2},{4,5},{5,4},{6,7},{7,6},{8,9},{9,8},{10,11... | collective-permute-start | bytes 12296 | tf_op jit(solution)/shard_map/ppermute | solution.py:445
  21.6 6.1 %collective-permute-start.10 = (f32[8,32,128]{2,1,0:T(8,128)S(1)}, f32[8,32,128]{2,1,0:T(8,128)S(1)}, u32[]{:S(2)}, u32[]{:S(2)}) collective-permute-start(f32[8,32,128]{2,1,0:T(8,128)S(1)} %get-tuple-element.56.refs_1_), channel_id=1, source_target_pairs={{0,2},{1,3},{2,0},{3,1},{4,6},{5,7},{6,4},{7,5},{8,10},{9,11},{10,... | collective-permute-start | bytes 393224 | tf_op jit(solution)/shard_map/ppermute | solution.py:487
  24.4 6.8 %collective-permute-start.7 = (f32[8,32,128]{2,1,0:T(8,128)S(1)}, f32[8,32,128]{2,1,0:T(8,128)S(1)}, u32[]{:S(2)}, u32[]{:S(2)}) collective-permute-start(f32[8,32,128]{2,1,0:T(8,128)S(1)} %get-tuple-element.51.refs_1_), channel_id=1, source_target_pairs={{0,2},{1,3},{2,0},{3,1},{4,6},{5,7},{6,4},{7,5},{8,10},{9,11},{10,... | collective-permute-start | bytes 393224 | tf_op jit(solution)/shard_map/ppermute | solution.py:487
  29.3 5.3 %collective-permute-start.11 = (f32[8,32,128]{2,1,0:T(8,128)S(1)}, f32[8,32,128]{2,1,0:T(8,128)S(1)}, u32[]{:S(2)}, u32[]{:S(2)}) collective-permute-start(f32[8,32,128]{2,1,0:T(8,128)S(1)} %get-tuple-element.58.refs_1_), channel_id=1, source_target_pairs={{0,2},{1,3},{2,0},{3,1},{4,6},{5,7},{6,4},{7,5},{8,10},{9,11},{10,... | collective-permute-start | bytes 393224 | tf_op jit(solution)/shard_map/ppermute | solution.py:498
  32.7 5.9 %collective-permute-start.8 = (f32[8,32,128]{2,1,0:T(8,128)S(1)}, f32[8,32,128]{2,1,0:T(8,128)S(1)}, u32[]{:S(2)}, u32[]{:S(2)}) collective-permute-start(f32[8,32,128]{2,1,0:T(8,128)S(1)} %get-tuple-element.53.refs_1_), channel_id=1, source_target_pairs={{0,2},{1,3},{2,0},{3,1},{4,6},{5,7},{6,4},{7,5},{8,10},{9,11},{10,... | collective-permute-start | bytes 393224 | tf_op jit(solution)/shard_map/ppermute | solution.py:498
  36.2 6.2 %collective-permute-start.16 = (f32[8,32,128]{2,1,0:T(8,128)S(1)}, f32[8,32,128]{2,1,0:T(8,128)S(1)}, u32[]{:S(2)}, u32[]{:S(2)}) collective-permute-start(f32[8,32,128]{2,1,0:T(8,128)S(1)} %get-tuple-element.65.refs_9_), channel_id=1, source_target_pairs={{0,2},{1,3},{2,0},{3,1},{4,6},{5,7},{6,4},{7,5},{8,10},{9,11},{10,... | collective-permute-start | bytes 393224 | tf_op jit(solution)/shard_map/ppermute | solution.py:498
  40.2 5.0 %collective-permute-start.15 = (f32[8,32,128]{2,1,0:T(8,128)S(1)}, f32[8,32,128]{2,1,0:T(8,128)S(1)}, u32[]{:S(2)}, u32[]{:S(2)}) collective-permute-start(f32[8,32,128]{2,1,0:T(8,128)S(1)} %get-tuple-element.61.refs_1_), channel_id=1, source_target_pairs={{0,2},{1,3},{2,0},{3,1},{4,6},{5,7},{6,4},{7,5},{8,10},{9,11},{10,... | collective-permute-start | bytes 393224 | tf_op jit(solution)/shard_map/ppermute | solution.py:498
  41.2 7.1 %collective-permute-start.12 = (bf16[512,128]{1,0:T(8,128)(2,1)S(1)}, bf16[512,128]{1,0:T(8,128)(2,1)S(1)}, u32[]{:S(2)}, u32[]{:S(2)}) collective-permute-start(bf16[512,128]{1,0:T(8,128)(2,1)S(1)} %get-tuple-element.60), channel_id=1, source_target_pairs={{4,0},{13,1},{6,2},{15,3},{8,4},{1,5},{10,6},{3,7},{12,8},{5,9},{1... | collective-permute-start | bytes 393224 | tf_op jit(solution)/shard_map/ppermute | solution.py:499
  41.7 9.0 %collective-permute-start.9 = (bf16[512,128]{1,0:T(8,128)(2,1)S(1)}, bf16[512,128]{1,0:T(8,128)(2,1)S(1)}, u32[]{:S(2)}, u32[]{:S(2)}) collective-permute-start(bf16[512,128]{1,0:T(8,128)(2,1)S(1)} %get-tuple-element.55), channel_id=1, source_target_pairs={{0,0},{9,1},{2,2},{11,3},{4,4},{13,5},{6,6},{15,7},{8,8},{1,9},{10... | collective-permute-start | bytes 393224 | tf_op jit(solution)/shard_map/ppermute | solution.py:499
  45.9 1.2 %collective-permute-start.17 = (f32[8,128]{1,0:T(8,128)S(1)}, f32[8,128]{1,0:T(8,128)S(1)}, u32[]{:S(2)}, u32[]{:S(2)}) collective-permute-start(f32[8,128]{1,0:T(8,128)S(1)} %get-tuple-element.69.table_ref), channel_id=1, source_target_pairs={{0,1},{1,0},{2,3},{3,2},{4,5},{5,4},{6,7},{7,6},{8,9},{9,8},{10,11... | collective-permute-start | bytes 12296 | tf_op jit(solution)/shard_map/ppermute | solution.py:445
  47.1 3.6 %collective-permute-start.18 = (bf16[272,128]{1,0:T(8,128)(2,1)S(1)}, bf16[272,128]{1,0:T(8,128)(2,1)S(1)}, u32[]{:S(2)}, u32[]{:S(2)}) collective-permute-start(bf16[272,128]{1,0:T(8,128)(2,1)S(1)} %get-tuple-element.72), channel_id=1, source_target_pairs={{0,0},{9,1},{2,2},{11,3},{4,4},{13,5},{6,6},{15,7},{8,8},{1,9},{10... | collective-permute-start | bytes 208904 | tf_op jit(solution)/shard_map/ppermute | solution.py:509
  47.8 5.6 %collective-permute-start.19 = (bf16[272,128]{1,0:T(8,128)(2,1)S(1)}, bf16[272,128]{1,0:T(8,128)(2,1)S(1)}, u32[]{:S(2)}, u32[]{:S(2)}) collective-permute-start(bf16[272,128]{1,0:T(8,128)(2,1)S(1)} %get-tuple-element.73), channel_id=1, source_target_pairs={{4,0},{13,1},{6,2},{15,3},{8,4},{1,5},{10,6},{3,7},{12,8},{5,9},{1... | collective-permute-start | bytes 208904 | tf_op jit(solution)/shard_map/ppermute | solution.py:509
  48.3 7.2 %collective-permute-start.14 = (bf16[512,128]{1,0:T(8,128)(2,1)S(1)}, bf16[512,128]{1,0:T(8,128)(2,1)S(1)}, u32[]{:S(2)}, u32[]{:S(2)}) collective-permute-start(bf16[512,128]{1,0:T(8,128)(2,1)S(1)} %collective-permute-done.12.refs_4_), channel_id=1, source_target_pairs={{0,1},{1,0},{2,3},{3,2},{4,5},{5,4},{6,7},{7,6},{8,9},{9,8},{10,11... | collective-permute-start | bytes 393224 | tf_op jit(solution)/shard_map/ppermute | solution.py:445
  50.7 4.9 %collective-permute-start.13 = (bf16[512,128]{1,0:T(8,128)(2,1)S(1)}, bf16[512,128]{1,0:T(8,128)(2,1)S(1)}, u32[]{:S(2)}, u32[]{:S(2)}) collective-permute-start(bf16[512,128]{1,0:T(8,128)(2,1)S(1)} %collective-permute-done.9.refs_3_), channel_id=1, source_target_pairs={{0,1},{1,0},{2,3},{3,2},{4,5},{5,4},{6,7},{7,6},{8,9},{9,8},{10,11... | collective-permute-start | bytes 393224 | tf_op jit(solution)/shard_map/ppermute | solution.py:445
  50.7 4.8 %collective-permute-start.20 = (bf16[272,128]{1,0:T(8,128)(2,1)S(1)}, bf16[272,128]{1,0:T(8,128)(2,1)S(1)}, u32[]{:S(2)}, u32[]{:S(2)}) collective-permute-start(bf16[272,128]{1,0:T(8,128)(2,1)S(1)} %collective-permute-done.18.refs_7_), channel_id=1, source_target_pairs={{0,1},{1,0},{2,3},{3,2},{4,5},{5,4},{6,7},{7,6},{8,9},{9,8},{10,11... | collective-permute-start | bytes 208904 | tf_op jit(solution)/shard_map/ppermute | solution.py:445
  53.4 3.0 %collective-permute-start.21 = (bf16[272,128]{1,0:T(8,128)(2,1)S(1)}, bf16[272,128]{1,0:T(8,128)(2,1)S(1)}, u32[]{:S(2)}, u32[]{:S(2)}) collective-permute-start(bf16[272,128]{1,0:T(8,128)(2,1)S(1)} %collective-permute-done.19.refs_8_), channel_id=1, source_target_pairs={{0,1},{1,0},{2,3},{3,2},{4,5},{5,4},{6,7},{7,6},{8,9},{9,8},{10,11... | collective-permute-start | bytes 208904 | tf_op jit(solution)/shard_map/ppermute | solution.py:445

commit v4 on v3

--- a/solution.py
+++ b/solution.py
@@ -208,6 +208,31 @@
     out_ref[...] = jnp.concatenate(lines + [jnp.zeros((6, LANES), F32)], axis=0)
 
 
+BITS = 14
+
+
+def encode(s, x, out_ref):
+    largest = jnp.max(jnp.max(jnp.abs(x), axis=0, keepdims=True), axis=1, keepdims=True)
+    power = wide(jnp.ceil(jnp.log2(jnp.maximum(largest, 1e-30))))
+    code = jnp.floor(x * jnp.exp2(BITS - power) + 0.5)
+    out_ref[HALF * s : HALF * (s + 1), :] = code.astype(jnp.int32).astype(jnp.int16)
+    return power
+
+
+def encode_end(powers, out_ref):
+    cap = len(powers)
+    tail = jnp.concatenate(powers + [jnp.zeros((16 - cap, LANES), F32)], axis=0)
+    out_ref[HALF * cap :, :] = tail.astype(jnp.int32).astype(jnp.int16)
+
+
+def decode(ref, s, scales):
+    return ref[HALF * s : HALF * (s + 1), :].astype(jnp.int32).astype(F32) * scales[s : s + 1]
+
+
+def decode_scales(ref):
+    return jnp.exp2(ref[ref.shape[0] - 16 :, :].astype(jnp.int32).astype(F32) - BITS)
+
+
 def block_diagonal(x):
     low = iota((HALF, LANES), 1) < B
     swapped = pltpu.roll(x, B, 1)
@@ -243,11 +268,13 @@
         for k in range(4):
             inner_ref[s, :B, k * span : (k + 1) * span] = high[k * B : (k + 1) * B]
             inner_ref[s, B:, k * span : (k + 1) * span] = low[k * B : (k + 1) * B]
+    powers = []
     for s in range(count):
         right = jnp.concatenate([keep_right[s], got_right[s]], axis=1)
         both = lax.dot_general(inner_ref[s], right, (((1,), (1,)), ((), ())), preferred_element_type=F32)
         image = both[:B] + both[B:]
-        y_ref[s] = jnp.concatenate([image[:HALF], image[HALF:]], axis=1)
+        powers.append(encode(s, jnp.concatenate([image[:HALF], image[HALF:]], axis=1), y_ref))
+    encode_end(powers, y_ref)
 
 
 def start_kernel(count, nodes, ship_ref, sums_ref, more_ref, *refs):
@@ -272,8 +299,12 @@
 def orthogonal(ship_ref, own_ref, other_ref, basis, q_ref):
     n = note(ship_ref)
     cap = q_ref.shape[0]
+    ahead = lax.axis_index("op") < 2
+    own_scales, other_scales = decode_scales(own_ref), decode_scales(other_ref)
     for s in range(cap):
-        q_ref[s] = (own_ref[s] + other_ref[s]) * inside(n[s : s + 1], n[cap + s : cap + s + 1])
+        own, other = decode(own_ref, s, own_scales), decode(other_ref, s, other_scales)
+        image = jnp.where(ahead, own, other) + jnp.where(ahead, other, own)
+        q_ref[s] = image * inside(n[s : s + 1], n[cap + s : cap + s + 1])
     image = q_ref[...].reshape(cap * HALF, LANES)
     rows = []
     rest = image
@@ -450,6 +481,7 @@
     environment = shape((cap, B, WIDE), BF16)
     vector = shape((cap, HALF, LANES))
     tile = shape((8, LANES))
+    code = shape((cap * HALF + 16, LANES), jnp.int16)
     payload = shape((cap * HALF + 32, LANES), BF16)
     order, *ships, home = call(
         ship_kernel, "ship",
@@ -482,12 +514,12 @@
     early = []
     for t in range(2):
         q, y, scale = call(
-            start, "first", (vector, vector, tile), (ships[t], sums, more, *envs[t]), "v" * 7, inner)
+            start, "first", (vector, code, tile), (ships[t], sums, more, *envs[t]), "v" * 7, inner)
         basis[t].append(q)
         images[t] = (y, lax.ppermute(y, "op", swap_x))
     for k in range(1, ITERS):
         for t in range(2):
-            outs = [vector, vector, tile]
+            outs = [vector, code, tile]
             if k == ITERS - 1:
                 outs.append(shape((2 * cap * HALF, LANES), BF16))
             q, y, a, *parcel = call(

time: 59 us -> 57.8 us (0.980)
  waiting for transfers between devices: 11.6 us -> 10.3 us
  Pallas kernels: 18.1 us -> 19.3 us
  starting transfers between devices: 26.6 us -> 25.5 us
    ppermute x6, starting transfers between devices: 7.9 us -> 6.36 us  [paired(): images[t] = (y, lax.ppermute(y, 'op', swap_x))]
    ppermute x2, starting transfers between devices: 1.18 us -> 2.66 us  [paired(): lax.ppermute(x, ('sector', 'op'), route(t, True))]
    ppermute x6, waiting for transfers between devices: 7.07 us -> 5.78 us  [paired(): images[t] = (y, lax.ppermute(y, 'op', swap_x))]
    pallas_call x13, Pallas kernels: 18.1 us -> 19.3 us  [call(): pl.pallas_call(kernel, out_shape=out_shape, in_specs=[pl.BlockSpec(memory...]
    ppermute x10, starting transfers between devices: 12.7 us -> 11.6 us  [across(): return lax.ppermute(x, 'op', swap_core)]
  transfers between devices with their start and end apart: 22 -> 22, of which waited for: 7 -> 8; matrix products, arithmetic and copies ran while one was open for 0% -> 0% of each run, Pallas kernels for 23% -> 26%
where the time goes in v4:
time: 57.8 us; the launch traced here: 57.6 us
  starting transfers between devices  25.5 us (44%)
  Pallas kernels  19.3 us (33%)
  waiting for transfers between devices  10.3 us (18%)
  local copies, waits for them, and re-layouts  0.96 us (2%)
  between operations  0.78 us (1%)
  other arithmetic  0.71 us (1%)
    pallas_call x13, Pallas kernels, call(): pl.pallas_call(kernel, out_shape=out_shape, in_specs=[pl.BlockSpec(memory...  19.3 us
    ppermute x10, starting transfers between devices, across(): return lax.ppermute(x, 'op', swap_core)  11.6 us
    ppermute x6, starting transfers between devices, paired(): images[t] = (y, lax.ppermute(y, 'op', swap_x))  6.36 us
    ppermute x6, waiting for transfers between devices, paired(): images[t] = (y, lax.ppermute(y, 'op', swap_x))  5.78 us
    ppermute x10, waiting for transfers between devices, across(): return lax.ppermute(x, 'op', swap_core)  4.53 us
    ppermute x2, starting transfers between devices, paired(): lax.ppermute(x, ('sector', 'op'), route(t, False))  3.73 us
    ppermute x2, starting transfers between devices, paired(): lax.ppermute(x, ('sector', 'op'), route(t, True))  2.66 us
    ppermute x2, starting transfers between devices, paired(): early += [lax.ppermute(x, ('sector', 'op'), route(t, True)) for x in parcel]  1.18 us
  transfers between devices with their start and end apart: 22, of which 8 were waited for; matrix products, arithmetic and copies ran while one was open for 0% of the time, Pallas kernels for 26%

profile of v4, /device:TPU:0, one launch (start us, length us, event | category | flops | bytes accessed | tf_op | source)
XLA Modules:
  0.0 57.6 jit_solution(13129076923063280345)
XLA Ops:
  0.6 0.7 %pad_add_fusion.meta_ref.refs_1_ = s32[10,32]{1,0:T(8,128)S(1)} fusion(s32[7,32]{1,0:T(8,128)} %bitcast.7, s32[2,32]{1,0:T(2,128)} %bitcast.8, s32[1,32]{1,0:T(1,128)} %bitcast.9), kind=kLoop, calls=%fused_computation | loop fusion | flops 640 | bytes 2560 | tf_op jit(solution)/shard_map/concatenate | solution.py:464
  1.4 0.9 %copy-done.2 = bf16[32,4096]{1,0:T(8,128)(2,1)S(1)} copy-done((bf16[32,4096]{1,0:T(8,128)(2,1)S(1)}, bf16[32,4096]{1,0:T(8,128)(2,1)}, u32[]{:S(2)}) %copy-start.2) | copy-done | bytes 262168
  2.3 2.3 %ship.1 = (s32[32]{0:T(128)S(1)}, bf16[288,128]{1,0:T(8,128)(2,1)S(1)}, bf16[288,128]{1,0:T(8,128)(2,1)S(1)}, bf16[1024,128]{1,0:T(8,128)(2,1)S(1)}) custom-call(s32[10,32]{1,0:T(8,128)S(1)} %pad_add_fusion.meta_ref.refs_1_, bf16[32,4096]{1,0:T(8,128)(2,1)S(1)} %copy-done.2), custom_call_target="tpu_custom_call" | custom-call | flops 2000000000 | bytes 1024 | tf_op jit(solution)/shard_map/ship/pallas_call | solution.py:104
  4.6 3.1 %collective-permute-start = (bf16[288,128]{1,0:T(8,128)(2,1)S(1)}, bf16[288,128]{1,0:T(8,128)(2,1)S(1)}, u32[]{:S(2)}, u32[]{:S(2)}) collective-permute-start(bf16[288,128]{1,0:T(8,128)(2,1)S(1)} %get-tuple-element.39), channel_id=1, source_target_pairs={{0,4},{1,13},{2,6},{3,15},{4,8},{5,1},{6,10},{7,3},{8,12},{9,5},{1... | collective-permute-start | bytes 221192 | tf_op jit(solution)/shard_map/ppermute | solution.py:490
  7.7 0.7 %collective-permute-start.1 = (bf16[288,128]{1,0:T(8,128)(2,1)S(1)}, bf16[288,128]{1,0:T(8,128)(2,1)S(1)}, u32[]{:S(2)}, u32[]{:S(2)}) collective-permute-start(bf16[288,128]{1,0:T(8,128)(2,1)S(1)} %get-tuple-element.40), channel_id=1, source_target_pairs={{0,0},{1,9},{2,2},{3,11},{4,4},{5,13},{6,6},{7,15},{8,8},{9,1},{10... | collective-permute-start | bytes 221192 | tf_op jit(solution)/shard_map/ppermute | solution.py:490
  8.4 0.0 copy-start.1
  8.4 2.1 %arrange.2 = (bf16[8,64,512]{2,1,0:T(8,128)(2,1)S(1)}, bf16[8,64,512]{2,1,0:T(8,128)(2,1)S(1)}, bf16[8,64,512]{2,1,0:T(8,128)(2,1)S(1)}, bf16[8,64,512]{2,1,0:T(8,128)(2,1)S(1)}) custom-call(s32[32]{0:T(128)S(1)} %get-tuple-element.38.refs_0_.refs_3_, s32[10,32]{1,0:T(8,128)S(1)} %pad_add_fusion.meta_ref.refs_1_, bf16[7,32,4096]{2,1,0:T(8,128)(2,1)S(1)} %bitcast.5, ...), custom_call_target="tpu_custom_call" | custom-call | flops 3000000000 | bytes 1024 | tf_op jit(solution)/shard_map/arrange/pallas_call | solution.py:104
  10.5 2.9 %collective-permute-start.3 = (bf16[8,64,512]{2,1,0:T(8,128)(2,1)S(1)}, bf16[8,64,512]{2,1,0:T(8,128)(2,1)S(1)}, u32[]{:S(2)}, u32[]{:S(2)}) collective-permute-start(bf16[8,64,512]{2,1,0:T(8,128)(2,1)S(1)} %get-tuple-element.44), channel_id=1, source_target_pairs={{0,1},{1,0},{2,3},{3,2},{4,5},{5,4},{6,7},{7,6},{8,9},{9,8},{10,11... | collective-permute-start | bytes 1572872 | tf_op jit(solution)/shard_map/ppermute | solution.py:476
  13.4 0.0 collective-permute-done.far_ref.refs_0_.refs_8_
  13.4 0.0 collective-permute-done.1.near_ref.refs_0_
  13.4 2.0 %arrange.3 = (bf16[8,64,512]{2,1,0:T(8,128)(2,1)S(1)}, bf16[8,64,512]{2,1,0:T(8,128)(2,1)S(1)}, bf16[8,64,512]{2,1,0:T(8,128)(2,1)S(1)}, bf16[8,64,512]{2,1,0:T(8,128)(2,1)S(1)}) custom-call(s32[32]{0:T(128)S(1)} %get-tuple-element.38.refs_0_.refs_3_, s32[10,32]{1,0:T(8,128)S(1)} %pad_add_fusion.meta_ref.refs_1_, bf16[7,32,4096]{2,1,0:T(8,128)(2,1)S(1)} %bitcast.6, ...), custom_call_target="tpu_custom_call" | custom-call | flops 3000000000 | bytes 1024 | tf_op jit(solution)/shard_map/arrange/pallas_call | solution.py:104
  15.5 1.9 %collective-permute-start.4 = (bf16[8,64,512]{2,1,0:T(8,128)(2,1)S(1)}, bf16[8,64,512]{2,1,0:T(8,128)(2,1)S(1)}, u32[]{:S(2)}, u32[]{:S(2)}) collective-permute-start(bf16[8,64,512]{2,1,0:T(8,128)(2,1)S(1)} %get-tuple-element.45), channel_id=1, source_target_pairs={{0,1},{1,0},{2,3},{3,2},{4,5},{5,4},{6,7},{7,6},{8,9},{9,8},{10,11... | collective-permute-start | bytes 1572872 | tf_op jit(solution)/shard_map/ppermute | solution.py:476
  17.4 0.1 collective-permute-start.5
  17.5 0.4 collective-permute-start.6
  17.9 0.1 collective-permute-start.2
  18.0 2.5 %collective-permute-done.2.refs_2_ = f32[8,128]{1,0:T(8,128)S(1)} collective-permute-done((f32[8,128]{1,0:T(8,128)S(1)}, f32[8,128]{1,0:T(8,128)S(1)}, u32[]{:S(2)}, u32[]{:S(2)}) %collective-permute-start.2) | collective-permute-done | bytes 4128 | tf_op jit(solution)/shard_map/ppermute | solution.py:476
  20.4 0.0 collective-permute-done.3.refs_5_.refs_6_.refs_7_
  20.4 0.0 collective-permute-done.4.refs_6_.refs_7_.refs_8_
  20.4 1.3 %first.2 = (f32[8,32,128]{2,1,0:T(8,128)S(1)}, s16[272,128]{1,0:T(8,128)(2,1)S(1)}, f32[8,128]{1,0:T(8,128)S(1)}) custom-call(bf16[288,128]{1,0:T(8,128)(2,1)S(1)} %collective-permute-done.far_ref.refs_0_.refs_8_, f32[8,128]{1,0:T(8,128)S(1)} %sums.1.refs_3_.refs_1_, f32[8,128]{1,0:T(8,128)S(1)} %collective-permute-done.2.refs_2_, ...), custom_call_target="tpu_custom_call" | custom-call | bytes 6000000 | tf_op jit(solution)/shard_map/first/pallas_call | solution.py:104
  21.7 1.6 %collective-permute-start.10 = (s16[272,128]{1,0:T(8,128)(2,1)S(1)}, s16[272,128]{1,0:T(8,128)(2,1)S(1)}, u32[]{:S(2)}, u32[]{:S(2)}) collective-permute-start(s16[272,128]{1,0:T(8,128)(2,1)S(1)} %get-tuple-element.56.refs_1_), channel_id=1, source_target_pairs={{0,2},{1,3},{2,0},{3,1},{4,6},{5,7},{6,4},{7,5},{8,10},{9,11},{10,... | collective-permute-start | bytes 208904 | tf_op jit(solution)/shard_map/ppermute | solution.py:519
  23.3 1.7 %first.3 = (f32[8,32,128]{2,1,0:T(8,128)S(1)}, s16[272,128]{1,0:T(8,128)(2,1)S(1)}, f32[8,128]{1,0:T(8,128)}) custom-call(bf16[288,128]{1,0:T(8,128)(2,1)S(1)} %collective-permute-done.1.near_ref.refs_0_, f32[8,128]{1,0:T(8,128)S(1)} %sums.1.refs_3_.refs_1_, f32[8,128]{1,0:T(8,128)S(1)} %collective-permute-done.2.refs_2_, ...), custom_call_target="tpu_custom_call" | custom-call | bytes 6000000 | tf_op jit(solution)/shard_map/first/pallas_call | solution.py:104
  25.0 0.5 collective-permute-start.7
  25.5 0.7 %collective-permute-done.10.refs_2_ = s16[272,128]{1,0:T(8,128)(2,1)S(1)} collective-permute-done((s16[272,128]{1,0:T(8,128)(2,1)S(1)}, s16[272,128]{1,0:T(8,128)(2,1)S(1)}, u32[]{:S(2)}, u32[]{:S(2)}) %collective-permute-start.10) | collective-permute-done | bytes 69664 | tf_op jit(solution)/shard_map/ppermute | solution.py:519
  26.3 1.7 %second.3 = (f32[8,32,128]{2,1,0:T(8,128)S(1)}, s16[272,128]{1,0:T(8,128)(2,1)S(1)}, f32[8,128]{1,0:T(8,128)S(1)}) custom-call(bf16[288,128]{1,0:T(8,128)(2,1)S(1)} %collective-permute-done.far_ref.refs_0_.refs_8_, s16[272,128]{1,0:T(8,128)(2,1)S(1)} %get-tuple-element.56.refs_1_, s16[272,128]{1,0:T(8,128)(2,1)S(1)} %collective-permute-done.10.refs_2_, ...), custom_call_target="tpu_custom_call" | custom-call | bytes 6000000 | tf_op jit(solution)/shard_map/second/pallas_call | solution.py:104
  28.0 1.6 %collective-permute-start.11 = (s16[272,128]{1,0:T(8,128)(2,1)S(1)}, s16[272,128]{1,0:T(8,128)(2,1)S(1)}, u32[]{:S(2)}, u32[]{:S(2)}) collective-permute-start(s16[272,128]{1,0:T(8,128)(2,1)S(1)} %get-tuple-element.58.refs_1_), channel_id=1, source_target_pairs={{0,2},{1,3},{2,0},{3,1},{4,6},{5,7},{6,4},{7,5},{8,10},{9,11},{10,... | collective-permute-start | bytes 208904 | tf_op jit(solution)/shard_map/ppermute | solution.py:530
  29.5 1.7 %second.2 = (f32[8,32,128]{2,1,0:T(8,128)S(1)}, s16[272,128]{1,0:T(8,128)(2,1)S(1)}, f32[8,128]{1,0:T(8,128)S(1)}) custom-call(bf16[288,128]{1,0:T(8,128)(2,1)S(1)} %collective-permute-done.1.near_ref.refs_0_, s16[272,128]{1,0:T(8,128)(2,1)S(1)} %get-tuple-element.51.refs_1_, s16[272,128]{1,0:T(8,128)(2,1)S(1)} %collective-permute-done.7.refs_2_, ...), custom_call_target="tpu_custom_call" | custom-call | bytes 6000000 | tf_op jit(solution)/shard_map/second/pallas_call | solution.py:104
  31.2 0.6 %collective-permute-start.8 = (s16[272,128]{1,0:T(8,128)(2,1)S(1)}, s16[272,128]{1,0:T(8,128)(2,1)S(1)}, u32[]{:S(2)}, u32[]{:S(2)}) collective-permute-start(s16[272,128]{1,0:T(8,128)(2,1)S(1)} %get-tuple-element.53.refs_1_), channel_id=1, source_target_pairs={{0,2},{1,3},{2,0},{3,1},{4,6},{5,7},{6,4},{7,5},{8,10},{9,11},{10,... | collective-permute-start | bytes 208904 | tf_op jit(solution)/shard_map/ppermute | solution.py:530
  31.8 0.5 collective-permute-done.11.refs_2_
  32.3 1.7 %third.3 = (f32[8,32,128]{2,1,0:T(8,128)S(1)}, s16[272,128]{1,0:T(8,128)(2,1)S(1)}, f32[8,128]{1,0:T(8,128)S(1)}, bf16[512,128]{1,0:T(8,128)(2,1)S(1)}) custom-call(bf16[288,128]{1,0:T(8,128)(2,1)S(1)} %collective-permute-done.far_ref.refs_0_.refs_8_, s16[272,128]{1,0:T(8,128)(2,1)S(1)} %get-tuple-element.58.refs_1_, ...), custom_call_target="tpu_custom_call" | custom-call | bytes 6000000 | tf_op jit(solution)/shard_map/third/pallas_call | solution.py:104
  34.1 0.5 collective-permute-start.12
  34.6 1.0 %collective-permute-done.8.refs_2_ = s16[272,128]{1,0:T(8,128)(2,1)S(1)} collective-permute-done((s16[272,128]{1,0:T(8,128)(2,1)S(1)}, s16[272,128]{1,0:T(8,128)(2,1)S(1)}, u32[]{:S(2)}, u32[]{:S(2)}) %collective-permute-start.8) | collective-permute-done | bytes 69664 | tf_op jit(solution)/shard_map/ppermute | solution.py:530
  35.6 1.7 %third.2 = (f32[8,32,128]{2,1,0:T(8,128)S(1)}, s16[272,128]{1,0:T(8,128)(2,1)S(1)}, f32[8,128]{1,0:T(8,128)S(1)}, bf16[512,128]{1,0:T(8,128)(2,1)S(1)}) custom-call(bf16[288,128]{1,0:T(8,128)(2,1)S(1)} %collective-permute-done.1.near_ref.refs_0_, s16[272,128]{1,0:T(8,128)(2,1)S(1)} %get-tuple-element.53.refs_1_, ...), custom_call_target="tpu_custom_call" | custom-call | bytes 6000000 | tf_op jit(solution)/shard_map/third/pallas_call | solution.py:104
  37.3 0.7 %collective-permute-start.9 = (bf16[512,128]{1,0:T(8,128)(2,1)S(1)}, bf16[512,128]{1,0:T(8,128)(2,1)S(1)}, u32[]{:S(2)}, u32[]{:S(2)}) collective-permute-start(bf16[512,128]{1,0:T(8,128)(2,1)S(1)} %get-tuple-element.55), channel_id=1, source_target_pairs={{0,0},{9,1},{2,2},{11,3},{4,4},{13,5},{6,6},{15,7},{8,8},{1,9},{10... | collective-permute-start | bytes 393224 | tf_op jit(solution)/shard_map/ppermute | solution.py:531
  38.0 0.7 %collective-permute-start.16 = (s16[272,128]{1,0:T(8,128)(2,1)S(1)}, s16[272,128]{1,0:T(8,128)(2,1)S(1)}, u32[]{:S(2)}, u32[]{:S(2)}) collective-permute-start(s16[272,128]{1,0:T(8,128)(2,1)S(1)} %get-tuple-element.65.refs_9_), channel_id=1, source_target_pairs={{0,2},{1,3},{2,0},{3,1},{4,6},{5,7},{6,4},{7,5},{8,10},{9,11},{10,... | collective-permute-start | bytes 208904 | tf_op jit(solution)/shard_map/ppermute | solution.py:530
  38.7 1.4 %collective-permute-start.15 = (s16[272,128]{1,0:T(8,128)(2,1)S(1)}, s16[272,128]{1,0:T(8,128)(2,1)S(1)}, u32[]{:S(2)}, u32[]{:S(2)}) collective-permute-start(s16[272,128]{1,0:T(8,128)(2,1)S(1)} %get-tuple-element.61.refs_1_), channel_id=1, source_target_pairs={{0,2},{1,3},{2,0},{3,1},{4,6},{5,7},{6,4},{7,5},{8,10},{9,11},{10,... | collective-permute-start | bytes 208904 | tf_op jit(solution)/shard_map/ppermute | solution.py:530
  40.1 2.8 %collective-permute-done.16.refs_10_ = s16[272,128]{1,0:T(8,128)(2,1)S(1)} collective-permute-done((s16[272,128]{1,0:T(8,128)(2,1)S(1)}, s16[272,128]{1,0:T(8,128)(2,1)S(1)}, u32[]{:S(2)}, u32[]{:S(2)}) %collective-permute-start.16) | collective-permute-done | bytes 69664 | tf_op jit(solution)/shard_map/ppermute | solution.py:530
  42.9 0.7 %collective-permute-done.15.refs_2_ = s16[272,128]{1,0:T(8,128)(2,1)S(1)} collective-permute-done((s16[272,128]{1,0:T(8,128)(2,1)S(1)}, s16[272,128]{1,0:T(8,128)(2,1)S(1)}, u32[]{:S(2)}, u32[]{:S(2)}) %collective-permute-start.15) | collective-permute-done | bytes 69664 | tf_op jit(solution)/shard_map/ppermute | solution.py:530
  43.6 0.7 %table.1 = (f32[8,32,128]{2,1,0:T(8,128)S(1)}, f32[8,32,128]{2,1,0:T(8,128)S(1)}, f32[8,128]{1,0:T(8,128)S(1)}) custom-call(bf16[288,128]{1,0:T(8,128)(2,1)S(1)} %collective-permute-done.1.near_ref.refs_0_, s16[272,128]{1,0:T(8,128)(2,1)S(1)} %get-tuple-element.61.refs_1_, s16[272,128]{1,0:T(8,128)(2,1)S(1)} %collective-permute-done.15.refs_2_, ...), custom_call_target="tpu_custom_call" | custom-call | bytes 3000000 | tf_op jit(solution)/shard_map/table/pallas_call | solution.py:104
  44.3 0.1 collective-permute-start.17
  44.4 1.2 %collective-permute-done.17.other_ref = f32[8,128]{1,0:T(8,128)S(1)} collective-permute-done((f32[8,128]{1,0:T(8,128)S(1)}, f32[8,128]{1,0:T(8,128)S(1)}, u32[]{:S(2)}, u32[]{:S(2)}) %collective-permute-start.17) | collective-permute-done | bytes 4128 | tf_op jit(solution)/shard_map/ppermute | solution.py:476
  45.6 0.7 %collective-permute-start.18 = (bf16[272,128]{1,0:T(8,128)(2,1)S(1)}, bf16[272,128]{1,0:T(8,128)(2,1)S(1)}, u32[]{:S(2)}, u32[]{:S(2)}) collective-permute-start(bf16[272,128]{1,0:T(8,128)(2,1)S(1)} %get-tuple-element.72), channel_id=1, source_target_pairs={{0,0},{9,1},{2,2},{11,3},{4,4},{13,5},{6,6},{15,7},{8,8},{1,9},{10... | collective-permute-start | bytes 208904 | tf_op jit(solution)/shard_map/ppermute | solution.py:541
  46.3 2.0 %collective-permute-start.19 = (bf16[272,128]{1,0:T(8,128)(2,1)S(1)}, bf16[272,128]{1,0:T(8,128)(2,1)S(1)}, u32[]{:S(2)}, u32[]{:S(2)}) collective-permute-start(bf16[272,128]{1,0:T(8,128)(2,1)S(1)} %get-tuple-element.73), channel_id=1, source_target_pairs={{4,0},{13,1},{6,2},{15,3},{8,4},{1,5},{10,6},{3,7},{12,8},{5,9},{1... | collective-permute-start | bytes 208904 | tf_op jit(solution)/shard_map/ppermute | solution.py:541
  48.3 1.4 %collective-permute-start.14 = (bf16[512,128]{1,0:T(8,128)(2,1)S(1)}, bf16[512,128]{1,0:T(8,128)(2,1)S(1)}, u32[]{:S(2)}, u32[]{:S(2)}) collective-permute-start(bf16[512,128]{1,0:T(8,128)(2,1)S(1)} %collective-permute-done.12.refs_4_), channel_id=1, source_target_pairs={{0,1},{1,0},{2,3},{3,2},{4,5},{5,4},{6,7},{7,6},{8,9},{9,8},{10,11... | collective-permute-start | bytes 393224 | tf_op jit(solution)/shard_map/ppermute | solution.py:476
  49.7 0.1 collective-permute-start.13
  49.8 3.2 %collective-permute-start.20 = (bf16[272,128]{1,0:T(8,128)(2,1)S(1)}, bf16[272,128]{1,0:T(8,128)(2,1)S(1)}, u32[]{:S(2)}, u32[]{:S(2)}) collective-permute-start(bf16[272,128]{1,0:T(8,128)(2,1)S(1)} %collective-permute-done.18.refs_7_), channel_id=1, source_target_pairs={{0,1},{1,0},{2,3},{3,2},{4,5},{5,4},{6,7},{7,6},{8,9},{9,8},{10,11... | collective-permute-start | bytes 208904 | tf_op jit(solution)/shard_map/ppermute | solution.py:476
  53.0 1.4 %collective-permute-start.21 = (bf16[272,128]{1,0:T(8,128)(2,1)S(1)}, bf16[272,128]{1,0:T(8,128)(2,1)S(1)}, u32[]{:S(2)}, u32[]{:S(2)}) collective-permute-start(bf16[272,128]{1,0:T(8,128)(2,1)S(1)} %collective-permute-done.19.refs_8_), channel_id=1, source_target_pairs={{0,1},{1,0},{2,3},{3,2},{4,5},{5,4},{6,7},{7,6},{8,9},{9,8},{10,11... | collective-permute-start | bytes 208904 | tf_op jit(solution)/shard_map/ppermute | solution.py:476
  54.4 0.9 %collective-permute-done.21.refs_10_ = bf16[272,128]{1,0:T(8,128)(2,1)S(1)} collective-permute-done((bf16[272,128]{1,0:T(8,128)(2,1)S(1)}, bf16[272,128]{1,0:T(8,128)(2,1)S(1)}, u32[]{:S(2)}, u32[]{:S(2)}) %collective-permute-start.21) | collective-permute-done | bytes 69664 | tf_op jit(solution)/shard_map/ppermute | solution.py:476
  55.3 2.3 %finish.1 = (f32[32,4096]{1,0:T(8,128)}, f32[3,3]{1,0:T(4,128)}) custom-call(s32[32]{0:T(128)S(1)} %get-tuple-element.38.refs_0_.refs_3_, f32[8,128]{1,0:T(8,128)S(1)} %get-tuple-element.46.refs_1_, bf16[1024,128]{1,0:T(8,128)(2,1)S(1)} %get-tuple-element.47.refs_2_, bf16[512,128]{1,0:T(8,128)(2,1)S(1)} %collective-permute-done.9.refs_3_, ...), custom_call_target="tpu_custom_call" | custom-call | bytes 6000000 | tf_op jit(solution)/shard_map/finish/pallas_call | solution.py:104
  (16 shorter events, 0.1 us)
Async XLA Ops:
  1.3 1.0 %copy-start.2 = (bf16[32,4096]{1,0:T(8,128)(2,1)S(1)}, bf16[32,4096]{1,0:T(8,128)(2,1)}, u32[]{:S(2)}) copy-start(bf16[32,4096]{1,0:T(8,128)(2,1)} %start_ref.1) | copy-start | bytes 786436
  2.3 6.1 %copy-start = (bf16[32,7,4096]{2,0,1:T(8,128)(2,1)S(1)}, bf16[32,7,4096]{2,0,1:T(8,128)(2,1)}, u32[]{:S(2)}) copy-start(bf16[32,7,4096]{2,0,1:T(8,128)(2,1)} %param.9) | copy-start | bytes 5505028
  4.6 8.8 %collective-permute-start = (bf16[288,128]{1,0:T(8,128)(2,1)S(1)}, bf16[288,128]{1,0:T(8,128)(2,1)S(1)}, u32[]{:S(2)}, u32[]{:S(2)}) collective-permute-start(bf16[288,128]{1,0:T(8,128)(2,1)S(1)} %get-tuple-element.39), channel_id=1, source_target_pairs={{0,4},{1,13},{2,6},{3,15},{4,8},{5,1},{6,10},{7,3},{8,12},{9,5},{1... | collective-permute-start | bytes 221192 | tf_op jit(solution)/shard_map/ppermute | solution.py:490
  7.7 5.7 %collective-permute-start.1 = (bf16[288,128]{1,0:T(8,128)(2,1)S(1)}, bf16[288,128]{1,0:T(8,128)(2,1)S(1)}, u32[]{:S(2)}, u32[]{:S(2)}) collective-permute-start(bf16[288,128]{1,0:T(8,128)(2,1)S(1)} %get-tuple-element.40), channel_id=1, source_target_pairs={{0,0},{1,9},{2,2},{3,11},{4,4},{5,13},{6,6},{7,15},{8,8},{9,1},{10... | collective-permute-start | bytes 221192 | tf_op jit(solution)/shard_map/ppermute | solution.py:490
  8.4 5.1 %copy-start.1 = (bf16[32,7,4096]{2,0,1:T(8,128)(2,1)S(1)}, bf16[32,7,4096]{2,0,1:T(8,128)(2,1)}, u32[]{:S(2)}) copy-start(bf16[32,7,4096]{2,0,1:T(8,128)(2,1)} %param.10) | copy-start | bytes 5505028
  10.5 9.9 %collective-permute-start.3 = (bf16[8,64,512]{2,1,0:T(8,128)(2,1)S(1)}, bf16[8,64,512]{2,1,0:T(8,128)(2,1)S(1)}, u32[]{:S(2)}, u32[]{:S(2)}) collective-permute-start(bf16[8,64,512]{2,1,0:T(8,128)(2,1)S(1)} %get-tuple-element.44), channel_id=1, source_target_pairs={{0,1},{1,0},{2,3},{3,2},{4,5},{5,4},{6,7},{7,6},{8,9},{9,8},{10,11... | collective-permute-start | bytes 1572872 | tf_op jit(solution)/shard_map/ppermute | solution.py:476
  15.5 5.0 %collective-permute-start.4 = (bf16[8,64,512]{2,1,0:T(8,128)(2,1)S(1)}, bf16[8,64,512]{2,1,0:T(8,128)(2,1)S(1)}, u32[]{:S(2)}, u32[]{:S(2)}) collective-permute-start(bf16[8,64,512]{2,1,0:T(8,128)(2,1)S(1)} %get-tuple-element.45), channel_id=1, source_target_pairs={{0,1},{1,0},{2,3},{3,2},{4,5},{5,4},{6,7},{7,6},{8,9},{9,8},{10,11... | collective-permute-start | bytes 1572872 | tf_op jit(solution)/shard_map/ppermute | solution.py:476
  17.4 5.9 %collective-permute-start.5 = (bf16[8,64,512]{2,1,0:T(8,128)(2,1)S(1)}, bf16[8,64,512]{2,1,0:T(8,128)(2,1)S(1)}, u32[]{:S(2)}, u32[]{:S(2)}) collective-permute-start(bf16[8,64,512]{2,1,0:T(8,128)(2,1)S(1)} %get-tuple-element.49), channel_id=1, source_target_pairs={{0,1},{1,0},{2,3},{3,2},{4,5},{5,4},{6,7},{7,6},{8,9},{9,8},{10,11... | collective-permute-start | bytes 1572872 | tf_op jit(solution)/shard_map/ppermute | solution.py:476
  17.5 5.8 %collective-permute-start.6 = (bf16[8,64,512]{2,1,0:T(8,128)(2,1)S(1)}, bf16[8,64,512]{2,1,0:T(8,128)(2,1)S(1)}, u32[]{:S(2)}, u32[]{:S(2)}) collective-permute-start(bf16[8,64,512]{2,1,0:T(8,128)(2,1)S(1)} %get-tuple-element.50), channel_id=1, source_target_pairs={{0,1},{1,0},{2,3},{3,2},{4,5},{5,4},{6,7},{7,6},{8,9},{9,8},{10,11... | collective-permute-start | bytes 1572872 | tf_op jit(solution)/shard_map/ppermute | solution.py:476
  17.9 2.5 %collective-permute-start.2 = (f32[8,128]{1,0:T(8,128)S(1)}, f32[8,128]{1,0:T(8,128)S(1)}, u32[]{:S(2)}, u32[]{:S(2)}) collective-permute-start(f32[8,128]{1,0:T(8,128)S(1)} %sums.1.refs_3_.refs_1_), channel_id=1, source_target_pairs={{0,1},{1,0},{2,3},{3,2},{4,5},{5,4},{6,7},{7,6},{8,9},{9,8},{10,11... | collective-permute-start | bytes 12296 | tf_op jit(solution)/shard_map/ppermute | solution.py:476
  21.7 4.5 %collective-permute-start.10 = (s16[272,128]{1,0:T(8,128)(2,1)S(1)}, s16[272,128]{1,0:T(8,128)(2,1)S(1)}, u32[]{:S(2)}, u32[]{:S(2)}) collective-permute-start(s16[272,128]{1,0:T(8,128)(2,1)S(1)} %get-tuple-element.56.refs_1_), channel_id=1, source_target_pairs={{0,2},{1,3},{2,0},{3,1},{4,6},{5,7},{6,4},{7,5},{8,10},{9,11},{10,... | collective-permute-start | bytes 208904 | tf_op jit(solution)/shard_map/ppermute | solution.py:519
  25.0 4.5 %collective-permute-start.7 = (s16[272,128]{1,0:T(8,128)(2,1)S(1)}, s16[272,128]{1,0:T(8,128)(2,1)S(1)}, u32[]{:S(2)}, u32[]{:S(2)}) collective-permute-start(s16[272,128]{1,0:T(8,128)(2,1)S(1)} %get-tuple-element.51.refs_1_), channel_id=1, source_target_pairs={{0,2},{1,3},{2,0},{3,1},{4,6},{5,7},{6,4},{7,5},{8,10},{9,11},{10,... | collective-permute-start | bytes 208904 | tf_op jit(solution)/shard_map/ppermute | solution.py:519
  28.0 4.4 %collective-permute-start.11 = (s16[272,128]{1,0:T(8,128)(2,1)S(1)}, s16[272,128]{1,0:T(8,128)(2,1)S(1)}, u32[]{:S(2)}, u32[]{:S(2)}) collective-permute-start(s16[272,128]{1,0:T(8,128)(2,1)S(1)} %get-tuple-element.58.refs_1_), channel_id=1, source_target_pairs={{0,2},{1,3},{2,0},{3,1},{4,6},{5,7},{6,4},{7,5},{8,10},{9,11},{10,... | collective-permute-start | bytes 208904 | tf_op jit(solution)/shard_map/ppermute | solution.py:530
  31.2 4.4 %collective-permute-start.8 = (s16[272,128]{1,0:T(8,128)(2,1)S(1)}, s16[272,128]{1,0:T(8,128)(2,1)S(1)}, u32[]{:S(2)}, u32[]{:S(2)}) collective-permute-start(s16[272,128]{1,0:T(8,128)(2,1)S(1)} %get-tuple-element.53.refs_1_), channel_id=1, source_target_pairs={{0,2},{1,3},{2,0},{3,1},{4,6},{5,7},{6,4},{7,5},{8,10},{9,11},{10,... | collective-permute-start | bytes 208904 | tf_op jit(solution)/shard_map/ppermute | solution.py:530
  34.1 14.2 %collective-permute-start.12 = (bf16[512,128]{1,0:T(8,128)(2,1)S(1)}, bf16[512,128]{1,0:T(8,128)(2,1)S(1)}, u32[]{:S(2)}, u32[]{:S(2)}) collective-permute-start(bf16[512,128]{1,0:T(8,128)(2,1)S(1)} %get-tuple-element.60), channel_id=1, source_target_pairs={{4,0},{13,1},{6,2},{15,3},{8,4},{1,5},{10,6},{3,7},{12,8},{5,9},{1... | collective-permute-start | bytes 393224 | tf_op jit(solution)/shard_map/ppermute | solution.py:531
  37.3 12.4 %collective-permute-start.9 = (bf16[512,128]{1,0:T(8,128)(2,1)S(1)}, bf16[512,128]{1,0:T(8,128)(2,1)S(1)}, u32[]{:S(2)}, u32[]{:S(2)}) collective-permute-start(bf16[512,128]{1,0:T(8,128)(2,1)S(1)} %get-tuple-element.55), channel_id=1, source_target_pairs={{0,0},{9,1},{2,2},{11,3},{4,4},{13,5},{6,6},{15,7},{8,8},{1,9},{10... | collective-permute-start | bytes 393224 | tf_op jit(solution)/shard_map/ppermute | solution.py:531
  38.0 4.9 %collective-permute-start.16 = (s16[272,128]{1,0:T(8,128)(2,1)S(1)}, s16[272,128]{1,0:T(8,128)(2,1)S(1)}, u32[]{:S(2)}, u32[]{:S(2)}) collective-permute-start(s16[272,128]{1,0:T(8,128)(2,1)S(1)} %get-tuple-element.65.refs_9_), channel_id=1, source_target_pairs={{0,2},{1,3},{2,0},{3,1},{4,6},{5,7},{6,4},{7,5},{8,10},{9,11},{10,... | collective-permute-start | bytes 208904 | tf_op jit(solution)/shard_map/ppermute | solution.py:530
  38.7 4.9 %collective-permute-start.15 = (s16[272,128]{1,0:T(8,128)(2,1)S(1)}, s16[272,128]{1,0:T(8,128)(2,1)S(1)}, u32[]{:S(2)}, u32[]{:S(2)}) collective-permute-start(s16[272,128]{1,0:T(8,128)(2,1)S(1)} %get-tuple-element.61.refs_1_), channel_id=1, source_target_pairs={{0,2},{1,3},{2,0},{3,1},{4,6},{5,7},{6,4},{7,5},{8,10},{9,11},{10,... | collective-permute-start | bytes 208904 | tf_op jit(solution)/shard_map/ppermute | solution.py:530
  44.3 1.2 %collective-permute-start.17 = (f32[8,128]{1,0:T(8,128)S(1)}, f32[8,128]{1,0:T(8,128)S(1)}, u32[]{:S(2)}, u32[]{:S(2)}) collective-permute-start(f32[8,128]{1,0:T(8,128)S(1)} %get-tuple-element.69.table_ref), channel_id=1, source_target_pairs={{0,1},{1,0},{2,3},{3,2},{4,5},{5,4},{6,7},{7,6},{8,9},{9,8},{10,11... | collective-permute-start | bytes 12296 | tf_op jit(solution)/shard_map/ppermute | solution.py:476
  45.6 4.2 %collective-permute-start.18 = (bf16[272,128]{1,0:T(8,128)(2,1)S(1)}, bf16[272,128]{1,0:T(8,128)(2,1)S(1)}, u32[]{:S(2)}, u32[]{:S(2)}) collective-permute-start(bf16[272,128]{1,0:T(8,128)(2,1)S(1)} %get-tuple-element.72), channel_id=1, source_target_pairs={{0,0},{9,1},{2,2},{11,3},{4,4},{13,5},{6,6},{15,7},{8,8},{1,9},{10... | collective-permute-start | bytes 208904 | tf_op jit(solution)/shard_map/ppermute | solution.py:541
  46.3 6.7 %collective-permute-start.19 = (bf16[272,128]{1,0:T(8,128)(2,1)S(1)}, bf16[272,128]{1,0:T(8,128)(2,1)S(1)}, u32[]{:S(2)}, u32[]{:S(2)}) collective-permute-start(bf16[272,128]{1,0:T(8,128)(2,1)S(1)} %get-tuple-element.73), channel_id=1, source_target_pairs={{4,0},{13,1},{6,2},{15,3},{8,4},{1,5},{10,6},{3,7},{12,8},{5,9},{1... | collective-permute-start | bytes 208904 | tf_op jit(solution)/shard_map/ppermute | solution.py:541
  48.3 7.0 %collective-permute-start.14 = (bf16[512,128]{1,0:T(8,128)(2,1)S(1)}, bf16[512,128]{1,0:T(8,128)(2,1)S(1)}, u32[]{:S(2)}, u32[]{:S(2)}) collective-permute-start(bf16[512,128]{1,0:T(8,128)(2,1)S(1)} %collective-permute-done.12.refs_4_), channel_id=1, source_target_pairs={{0,1},{1,0},{2,3},{3,2},{4,5},{5,4},{6,7},{7,6},{8,9},{9,8},{10,11... | collective-permute-start | bytes 393224 | tf_op jit(solution)/shard_map/ppermute | solution.py:476
  49.7 5.6 %collective-permute-start.13 = (bf16[512,128]{1,0:T(8,128)(2,1)S(1)}, bf16[512,128]{1,0:T(8,128)(2,1)S(1)}, u32[]{:S(2)}, u32[]{:S(2)}) collective-permute-start(bf16[512,128]{1,0:T(8,128)(2,1)S(1)} %collective-permute-done.9.refs_3_), channel_id=1, source_target_pairs={{0,1},{1,0},{2,3},{3,2},{4,5},{5,4},{6,7},{7,6},{8,9},{9,8},{10,11... | collective-permute-start | bytes 393224 | tf_op jit(solution)/shard_map/ppermute | solution.py:476
  49.8 4.6 %collective-permute-start.20 = (bf16[272,128]{1,0:T(8,128)(2,1)S(1)}, bf16[272,128]{1,0:T(8,128)(2,1)S(1)}, u32[]{:S(2)}, u32[]{:S(2)}) collective-permute-start(bf16[272,128]{1,0:T(8,128)(2,1)S(1)} %collective-permute-done.18.refs_7_), channel_id=1, source_target_pairs={{0,1},{1,0},{2,3},{3,2},{4,5},{5,4},{6,7},{7,6},{8,9},{9,8},{10,11... | collective-permute-start | bytes 208904 | tf_op jit(solution)/shard_map/ppermute | solution.py:476
  53.0 2.3 %collective-permute-start.21 = (bf16[272,128]{1,0:T(8,128)(2,1)S(1)}, bf16[272,128]{1,0:T(8,128)(2,1)S(1)}, u32[]{:S(2)}, u32[]{:S(2)}) collective-permute-start(bf16[272,128]{1,0:T(8,128)(2,1)S(1)} %collective-permute-done.19.refs_8_), channel_id=1, source_target_pairs={{0,1},{1,0},{2,3},{3,2},{4,5},{5,4},{6,7},{7,6},{8,9},{9,8},{10,11... | collective-permute-start | bytes 208904 | tf_op jit(solution)/shard_map/ppermute | solution.py:476

commit v5 on v4

--- a/solution.py
+++ b/solution.py
@@ -131,7 +131,27 @@
         order_ref[jnp.where(place >= slots, place - slots, place)] = j
 
 
-def arrange_kernel(masked, order_ref, meta_ref, env_ref, _, *outs):
+def note(ref):
+    return ref[ref.shape[0] - 32 :, :].astype(F32)
+
+
+def arrived_kernel(near_in_ref, far_in_ref, _, near_ref, far_ref):
+    near_ref[...] = near_in_ref[...]
+    far_ref[...] = far_in_ref[...]
+
+
+def riding_sums(ships):
+    pieces = [note(ref)[16:19] for ref in ships]
+    tile = jnp.concatenate(pieces + [jnp.zeros((HALF - 6, LANES), F32)], axis=0)
+    tile = jnp.where(iota((HALF, LANES), 1) >= B, tile, 0.0)
+    return jnp.concatenate([tile, jnp.zeros_like(tile)], axis=1)
+
+
+def arrange_kernel(order_ref, meta_ref, env_ref, *refs):
+    ships, outs = refs[:-4], refs[-4:]
+    masked = not ships
+    if ships:
+        riding = riding_sums(ships)
     chans, slots = env_ref.shape[:2]
     cap = outs[0].shape[0]
     first = blocks_first(order_ref, 0, slots, slots)
@@ -155,6 +175,8 @@
                 slot = order_ref[k]
                 kept = [meta_ref[3 + w, slot].astype(F32) for w in used]
                 x = x * jnp.where(low, kept[0], kept[-1])
+            elif g == 3 and k in (2 * cap, 3 * cap):
+                x = x + riding
             x = x.astype(BF16)
             for p in range(2):
                 outs[k // cap][k % cap, p * HALF : (p + 1) * HALF, g * LANES : (g + 1) * LANES] = x[
@@ -196,18 +218,6 @@
         ref[HALF * cap :, :] = jnp.concatenate(lines + pieces + [blank], axis=0).astype(BF16)
 
 
-def note(ref):
-    return ref[ref.shape[0] - 32 :, :].astype(F32)
-
-
-def sums_kernel(near_ref, far_ref, _, out_ref):
-    lines = []
-    for ref in (near_ref, far_ref):
-        n = note(ref)
-        lines.append(n[16:17] + n[17:18] + n[18:19])
-    out_ref[...] = jnp.concatenate(lines + [jnp.zeros((6, LANES), F32)], axis=0)
-
-
 BITS = 14
 
 
@@ -277,16 +287,21 @@
     encode_end(powers, y_ref)
 
 
-def start_kernel(count, nodes, ship_ref, sums_ref, more_ref, *refs):
-    envs, (q_ref, y_ref, scale_ref, inner_ref) = refs[:4], refs[4:]
+def start_kernel(count, nodes, t, *refs):
+    ships, envs, (q_ref, y_ref, scale_ref, inner_ref) = refs[:2], refs[2:6], refs[6:]
     node, core = position()
+    ship_ref = ships[t]
+    mine = [note(ref)[16:19] for ref in ships]
+    tile = envs[3][0, :HALF, WIDE - LANES :].astype(F32)
+    tile = jnp.where(iota((HALF, LANES), 1) >= B, tile, pltpu.roll(tile, B, 1))
+    theirs = [tile[0:3], tile[3:6]]
     by_node = []
     for e in range(nodes):
         value = jnp.zeros((1, LANES), F32)
-        for ref, c in ((sums_ref, core), (more_ref, 1 - core)):
-            for t in range(2):
-                source = lax.rem(node + 2 * nodes - 2 * c - t, nodes)
-                value = value + jnp.where(source == e, ref[t : t + 1, :], 0.0)
+        for sums, c in ((mine, core), (theirs, 1 - core)):
+            for hop, p in enumerate(sums):
+                source = lax.rem(node + 2 * nodes - 2 * c - hop, nodes)
+                value = value + jnp.where(source == e, p[0:1] + p[1:2] + p[2:3], 0.0)
         by_node.append(value)
     squares = (by_node[0] + by_node[1]) + (by_node[2] + by_node[3])
     scale = 1.0 / jnp.sqrt(squares / count + 1e-06)
@@ -327,8 +342,10 @@
     rows = orthogonal(ship_ref, own_ref, other_ref, basis, q_ref)
     along_ref[...] = jnp.concatenate(rows + [jnp.zeros((8 - count, LANES), F32)], axis=0)
     for ref in parcel_ref:
-        vectors = [r[...].reshape(-1, LANES) for r in (*basis[1:], q_ref)]
-        ref[...] = jnp.concatenate(vectors, axis=0).astype(BF16)
+        mine = jnp.where(lax.axis_index("op") < 2, basis[1][...], q_ref[...])
+        mine = mine.reshape(-1, LANES).astype(BF16)
+        blank = jnp.zeros((ref.shape[0] - mine.shape[0], LANES), BF16)
+        ref[...] = jnp.concatenate([mine, blank], axis=0)
     product(q_ref, envs, y_ref, inner_ref, False)
 
 
@@ -409,7 +426,7 @@
 
 
 def finish_kernel(count, nodes, order_ref, scale_ref, home_ref, *refs):
-    early, late, (out_ref, proj_ref) = refs[:4], refs[4:8], refs[8:]
+    early, late, (out_ref, proj_ref) = refs[:8], refs[8:12], refs[12:]
     node, core = position()
     slots = out_ref.shape[0]
     rows = home_ref.shape[0] // 4
@@ -421,7 +438,7 @@
         tail = ref[rows:, :].astype(F32)
         four = tail[0:4] + tail[4:8] + tail[8:12]
         lines = [jnp.where(host == e, four, v) for e, v in enumerate(lines)]
-        sources.append((early[k], ref, host * 4 + hop))
+        sources.append((*early[2 * k : 2 * k + 2], ref, host * 4 + hop))
     table = jnp.concatenate(lines, axis=0)
     sets = 4 * nodes
     projections, rest = combine(
@@ -430,12 +447,14 @@
     proj_ref[...] = jnp.concatenate(lines, axis=0)[:, :ITERS]
     scale = scale_ref[0:1, :]
     blocks = []
-    for k, (two, one, index) in enumerate(sources):
+    ahead = lax.axis_index("op") < 2
+    for k, (mine_ref, more_ref, last_ref, index) in enumerate(sources):
         mine = iota((sets, LANES), 0) == index
         coeff = [jnp.sum(jnp.where(mine, v, 0.0), axis=0, keepdims=True) for v in rest]
         x = coeff[0] * (home_ref[rows * k : rows * (k + 1), :].astype(F32) * scale)
-        x = x + coeff[1] * two[:rows, :].astype(F32) + coeff[2] * two[rows:, :].astype(F32)
-        x = x + coeff[3] * one[:rows, :].astype(F32)
+        here, there = mine_ref[:rows, :].astype(F32), more_ref[:rows, :].astype(F32)
+        x = x + coeff[1] * jnp.where(ahead, here, there) + coeff[2] * jnp.where(ahead, there, here)
+        x = x + coeff[3] * last_ref[:rows, :].astype(F32)
         blocks.append(x)
     first = slots_last(order_ref, slots)
     second = from_kept_twice()
@@ -489,20 +508,16 @@
         (meta, start_vector), "sv", [pltpu.SMEM((nodes,), jnp.int32)], "svvv", 2.0, ROOMY, True)
     ships = [lax.ppermute(x, ("sector", "op"), route(t, False)) for t, x in enumerate(ships)]
 
-    def arrange(masked, env, after):
+    def arrange(env, *more):
         sets = call(
-            lambda *refs: arrange_kernel(masked, *refs), "arrange", (environment,) * 4, (order, meta, env, after),
-            "ssva", cost=3.0, limit=ARRANGE, compute=True)
+            arrange_kernel, "arrange", (environment,) * 4, (order, meta, env, *more), "ssv" + "v" * len(more),
+            cost=3.0, limit=ARRANGE, compute=True)
         return sets[:2], [across(x) for x in sets[2:]]
 
-    keep_left, got_left = arrange(True, left, order)
-    (sums,) = call(sums_kernel, "sums", (tile,), (*ships, keep_left[0]), "vva", cost=0.3)
-    keep_right, got_right = arrange(False, right, sums)
+    keep_left, got_left = arrange(left)
+    ships = call(arrived_kernel, "arrived", (payload, payload), (*ships, keep_left[0]), "vva", cost=0.3)
+    keep_right, got_right = arrange(right, *ships)
     envs = [(keep_left[t], keep_right[t], got_left[t], got_right[t]) for t in range(2)]
-    more = across(sums)
-
-    def start(*refs):
-        start_kernel(count, nodes, *refs)
 
     def step(k):
         return lambda *refs: step_kernel(k, *refs)
@@ -514,14 +529,15 @@
     early = []
     for t in range(2):
         q, y, scale = call(
-            start, "first", (vector, code, tile), (ships[t], sums, more, *envs[t]), "v" * 7, inner)
+            lambda *refs, t=t: start_kernel(count, nodes, t, *refs), "first", (vector, code, tile),
+            (*ships, *envs[t]), "v" * 6, inner)
         basis[t].append(q)
         images[t] = (y, lax.ppermute(y, "op", swap_x))
     for k in range(1, ITERS):
         for t in range(2):
             outs = [vector, code, tile]
             if k == ITERS - 1:
-                outs.append(shape((2 * cap * HALF, LANES), BF16))
+                outs.append(shape(code.shape, BF16))
             q, y, a, *parcel = call(
                 step(k), ("second", "third")[k - 1], tuple(outs),
                 (ships[t], *images[t], *basis[t], *envs[t]), "v" * (7 + k), inner)
@@ -529,7 +545,9 @@
             along[t].append(a)
             images[t] = (y, lax.ppermute(y, "op", swap_x))
             early += [lax.ppermute(x, ("sector", "op"), route(t, True)) for x in parcel]
-    early += [across(x) for x in early]
+    early = [(x, lax.ppermute(x, "op", swap_x)) for x in early]
+    early += [tuple(across(x) for x in pair) for pair in early]
+    early = [x for pair in early for x in pair]
 
     operands = []
     for t in range(2):
@@ -546,7 +564,7 @@
 
     return call(
         finish, "finish", (shape((slots, B * B)), shape((ITERS, ITERS))),
-        (order, scale, home, *early, *late), "s" + "v" * 10)
+        (order, scale, home, *early, *late), "s" + "v" * 14)
 
 
 def pack_rows(data, index, nodes, cap):
@@ -626,7 +644,7 @@
     def on_device(start_vector, extents, offsets, env_left, env_right, channel_mask):
         nodes, ops = mesh.shape["sector"], mesh.shape["op"]
         slots, chans = env_left.shape[:2]
-        fits = nodes == 4 and ops == 4 and slots == 8 * nodes and chans <= 8
+        fits = nodes == 4 and ops == 4 and slots == 8 * nodes and chans < 8
         body = paired if fits else general
         return body(start_vector, extents, offsets, env_left, env_right, channel_mask)
 

time: 57.8 us -> 54.2 us (0.938)
  waiting for transfers between devices: 10.3 us -> 4.04 us
  starting transfers between devices: 25.5 us -> 28.4 us
    ppermute x6, waiting for transfers between devices: 5.78 us -> 1.95 us  [paired(): images[t] = (y, lax.ppermute(y, 'op', swap_x))]
    ppermute x10 -> x11, starting transfers between devices: 11.6 us -> 7.89 us  [across(): return lax.ppermute(x, 'op', swap_core)]
    ppermute x2, starting transfers between devices: 1.18 us -> 3.87 us  [paired(): early += [lax.ppermute(x, ('sector', 'op'), route(t, True)) for x in parcel]]
    ppermute x10 -> x11, waiting for transfers between devices: 4.53 us -> 2.07 us  [across(): return lax.ppermute(x, 'op', swap_core)]
    ppermute x0 -> x2, starting transfers between devices: none -> 2.03 us  [paired(): early = [(x, lax.ppermute(x, 'op', swap_x)) for x in early]]
    ppermute x2, starting transfers between devices: 2.66 us -> 4.28 us  [paired(): lax.ppermute(x, ('sector', 'op'), route(t, True))]
  transfers between devices with their start and end apart: 22 -> 25, of which waited for: 8 -> 6; matrix products, arithmetic and copies ran while one was open for 0% -> 0% of each run, Pallas kernels for 26% -> 27%
where the time goes in v5:
time: 54.2 us; the launch traced here: 54 us
  starting transfers between devices  28.4 us (52%)
  Pallas kernels  19.1 us (35%)
  waiting for transfers between devices  4.04 us (7%)
  local copies, waits for them, and re-layouts  0.95 us (2%)
  between operations  0.81 us (1%)
  other arithmetic  0.71 us (1%)
    pallas_call x13, Pallas kernels, call(): pl.pallas_call(kernel, out_shape=out_shape, in_specs=[pl.BlockSpec(memory...  19.1 us
    ppermute x11, starting transfers between devices, across(): return lax.ppermute(x, 'op', swap_core)  7.89 us
    ppermute x6, starting transfers between devices, paired(): images[t] = (y, lax.ppermute(y, 'op', swap_x))  6.57 us
    ppermute x2, starting transfers between devices, paired(): lax.ppermute(x, ('sector', 'op'), route(t, True))  4.28 us
    ppermute x2, starting transfers between devices, paired(): early += [lax.ppermute(x, ('sector', 'op'), route(t, True)) for x in parcel]  3.87 us
    ppermute x2, starting transfers between devices, paired(): lax.ppermute(x, ('sector', 'op'), route(t, False))  3.74 us
    ppermute x11, waiting for transfers between devices, across(): return lax.ppermute(x, 'op', swap_core)  2.07 us
    ppermute x2, starting transfers between devices, paired(): early = [(x, lax.ppermute(x, 'op', swap_x)) for x in early]  2.03 us
  transfers between devices with their start and end apart: 25, of which 6 were waited for; matrix products, arithmetic and copies ran while one was open for 0% of the time, Pallas kernels for 27%

profile of v5, /device:TPU:0, one launch (start us, length us, event | category | flops | bytes accessed | tf_op | source)
XLA Modules:
  0.0 54.0 jit_solution(6705456775293615252)
XLA Ops:
  0.6 0.7 %pad_add_fusion.meta_ref = s32[10,32]{1,0:T(8,128)S(1)} fusion(s32[7,32]{1,0:T(8,128)} %bitcast.7, s32[2,32]{1,0:T(2,128)} %bitcast.8, s32[1,32]{1,0:T(1,128)} %bitcast.9), kind=kLoop, calls=%fused_computation | loop fusion | flops 640 | bytes 2560 | tf_op jit(solution)/shard_map/concatenate | solution.py:483
  1.4 0.9 %copy-done.2 = bf16[32,4096]{1,0:T(8,128)(2,1)S(1)} copy-done((bf16[32,4096]{1,0:T(8,128)(2,1)S(1)}, bf16[32,4096]{1,0:T(8,128)(2,1)}, u32[]{:S(2)}) %copy-start.2) | copy-done | bytes 262168
  2.3 2.3 %ship.1 = (s32[32]{0:T(128)S(1)}, bf16[288,128]{1,0:T(8,128)(2,1)S(1)}, bf16[288,128]{1,0:T(8,128)(2,1)S(1)}, bf16[1024,128]{1,0:T(8,128)(2,1)S(1)}) custom-call(s32[10,32]{1,0:T(8,128)S(1)} %pad_add_fusion.meta_ref, bf16[32,4096]{1,0:T(8,128)(2,1)S(1)} %copy-done.2), custom_call_target="tpu_custom_call" | custom-call | flops 2000000000 | bytes 1024 | tf_op jit(solution)/shard_map/ship/pallas_call | solution.py:104
  4.6 0.7 %collective-permute-start = (bf16[288,128]{1,0:T(8,128)(2,1)S(1)}, bf16[288,128]{1,0:T(8,128)(2,1)S(1)}, u32[]{:S(2)}, u32[]{:S(2)}) collective-permute-start(bf16[288,128]{1,0:T(8,128)(2,1)S(1)} %get-tuple-element.41), channel_id=1, source_target_pairs={{0,0},{1,9},{2,2},{3,11},{4,4},{5,13},{6,6},{7,15},{8,8},{9,1},{10... | collective-permute-start | bytes 221192 | tf_op jit(solution)/shard_map/ppermute | solution.py:509
  5.3 3.1 %collective-permute-start.1 = (bf16[288,128]{1,0:T(8,128)(2,1)S(1)}, bf16[288,128]{1,0:T(8,128)(2,1)S(1)}, u32[]{:S(2)}, u32[]{:S(2)}) collective-permute-start(bf16[288,128]{1,0:T(8,128)(2,1)S(1)} %get-tuple-element.42), channel_id=1, source_target_pairs={{0,4},{1,13},{2,6},{3,15},{4,8},{5,1},{6,10},{7,3},{8,12},{9,5},{1... | collective-permute-start | bytes 221192 | tf_op jit(solution)/shard_map/ppermute | solution.py:509
  8.4 2.1 %arrange.2 = (bf16[8,64,512]{2,1,0:T(8,128)(2,1)S(1)}, bf16[8,64,512]{2,1,0:T(8,128)(2,1)S(1)}, bf16[8,64,512]{2,1,0:T(8,128)(2,1)S(1)}, bf16[8,64,512]{2,1,0:T(8,128)(2,1)S(1)}) custom-call(s32[32]{0:T(128)S(1)} %get-tuple-element.40.order_ref.refs_0_, s32[10,32]{1,0:T(8,128)S(1)} %pad_add_fusion.meta_ref, bf16[7,32,4096]{2,1,0:T(8,128)(2,1)S(1)} %bitcast.5), custom_call_target="tpu_custom_call" | custom-call | flops 3000000000 | bytes 1024 | tf_op jit(solution)/shard_map/arrange/pallas_call | solution.py:104
  10.5 2.9 %collective-permute-start.2 = (bf16[8,64,512]{2,1,0:T(8,128)(2,1)S(1)}, bf16[8,64,512]{2,1,0:T(8,128)(2,1)S(1)}, u32[]{:S(2)}, u32[]{:S(2)}) collective-permute-start(bf16[8,64,512]{2,1,0:T(8,128)(2,1)S(1)} %get-tuple-element.48), channel_id=1, source_target_pairs={{0,1},{1,0},{2,3},{3,2},{4,5},{5,4},{6,7},{7,6},{8,9},{9,8},{10,11... | collective-permute-start | bytes 1572872 | tf_op jit(solution)/shard_map/ppermute | solution.py:495
  13.4 0.0 collective-permute-done.1.far_in_ref
  13.5 2.1 %arrange.3 = (bf16[8,64,512]{2,1,0:T(8,128)(2,1)S(1)}, bf16[8,64,512]{2,1,0:T(8,128)(2,1)S(1)}, bf16[8,64,512]{2,1,0:T(8,128)(2,1)S(1)}, bf16[8,64,512]{2,1,0:T(8,128)(2,1)S(1)}) custom-call(s32[32]{0:T(128)S(1)} %get-tuple-element.40.order_ref.refs_0_, s32[10,32]{1,0:T(8,128)S(1)} %pad_add_fusion.meta_ref, bf16[7,32,4096]{2,1,0:T(8,128)(2,1)S(1)} %bitcast.6, ...), custom_call_target="tpu_custom_call" | custom-call | flops 3000000000 | bytes 1024 | tf_op jit(solution)/shard_map/arrange/pallas_call | solution.py:104
  15.5 0.3 collective-permute-start.3
  15.8 0.3 collective-permute-start.4
  16.1 0.2 collective-permute-start.5
  16.3 1.2 %collective-permute-done.3.refs_5_.refs_7_.refs_8_ = bf16[8,64,512]{2,1,0:T(8,128)(2,1)S(1)} collective-permute-done((bf16[8,64,512]{2,1,0:T(8,128)(2,1)S(1)}, bf16[8,64,512]{2,1,0:T(8,128)(2,1)S(1)}, u32[]{:S(2)}, u32[]{:S(2)}) %collective-permute-start.3) | collective-permute-done | bytes 524320 | tf_op jit(solution)/shard_map/ppermute | solution.py:495
  17.5 1.3 %first.2 = (f32[8,32,128]{2,1,0:T(8,128)S(1)}, s16[272,128]{1,0:T(8,128)(2,1)S(1)}, f32[8,128]{1,0:T(8,128)S(1)}) custom-call(bf16[288,128]{1,0:T(8,128)(2,1)S(1)} %get-tuple-element.44.refs_0_, bf16[288,128]{1,0:T(8,128)(2,1)S(1)} %get-tuple-element.45.refs_1_.refs_0_.refs_8_, bf16[8,64,512]{2,1,0:T(8,128)(2,1)S(1)} %get-tuple-element.46.refs_2_.refs_4_.refs_5_, ...), custom_call_target="tpu_custom_call" | custom-call | bytes 6000000 | tf_op jit(solution)/shard_map/first/pallas_call | solution.py:104
  18.8 1.7 %collective-permute-start.10 = (s16[272,128]{1,0:T(8,128)(2,1)S(1)}, s16[272,128]{1,0:T(8,128)(2,1)S(1)}, u32[]{:S(2)}, u32[]{:S(2)}) collective-permute-start(s16[272,128]{1,0:T(8,128)(2,1)S(1)} %get-tuple-element.60.refs_1_), channel_id=1, source_target_pairs={{0,2},{1,3},{2,0},{3,1},{4,6},{5,7},{6,4},{7,5},{8,10},{9,11},{10,... | collective-permute-start | bytes 208904 | tf_op jit(solution)/shard_map/ppermute | solution.py:535
  20.5 1.3 %first.3 = (f32[8,32,128]{2,1,0:T(8,128)S(1)}, s16[272,128]{1,0:T(8,128)(2,1)S(1)}, f32[8,128]{1,0:T(8,128)}) custom-call(bf16[288,128]{1,0:T(8,128)(2,1)S(1)} %get-tuple-element.44.refs_0_, bf16[288,128]{1,0:T(8,128)(2,1)S(1)} %get-tuple-element.45.refs_1_.refs_0_.refs_8_, bf16[8,64,512]{2,1,0:T(8,128)(2,1)S(1)} %get-tuple-element.43._.refs_2_.refs_4_.refs_5_, ...), custom_call_target="tpu_custom_call" | custom-call | bytes 6000000 | tf_op jit(solution)/shard_map/first/pallas_call | solution.py:104
  21.9 0.4 collective-permute-start.6
  22.3 0.9 %collective-permute-done.10.refs_2_ = s16[272,128]{1,0:T(8,128)(2,1)S(1)} collective-permute-done((s16[272,128]{1,0:T(8,128)(2,1)S(1)}, s16[272,128]{1,0:T(8,128)(2,1)S(1)}, u32[]{:S(2)}, u32[]{:S(2)}) %collective-permute-start.10) | collective-permute-done | bytes 69664 | tf_op jit(solution)/shard_map/ppermute | solution.py:535
  23.2 1.7 %second.3 = (f32[8,32,128]{2,1,0:T(8,128)S(1)}, s16[272,128]{1,0:T(8,128)(2,1)S(1)}, f32[8,128]{1,0:T(8,128)S(1)}) custom-call(bf16[288,128]{1,0:T(8,128)(2,1)S(1)} %get-tuple-element.45.refs_1_.refs_0_.refs_8_, s16[272,128]{1,0:T(8,128)(2,1)S(1)} %get-tuple-element.60.refs_1_, s16[272,128]{1,0:T(8,128)(2,1)S(1)} %collective-permute-done.10.refs_2_, ...), custom_call_target="tpu_custom_call" | custom-call | bytes 6000000 | tf_op jit(solution)/shard_map/second/pallas_call | solution.py:104
  24.9 1.7 %collective-permute-start.11 = (s16[272,128]{1,0:T(8,128)(2,1)S(1)}, s16[272,128]{1,0:T(8,128)(2,1)S(1)}, u32[]{:S(2)}, u32[]{:S(2)}) collective-permute-start(s16[272,128]{1,0:T(8,128)(2,1)S(1)} %get-tuple-element.62.refs_1_), channel_id=1, source_target_pairs={{0,2},{1,3},{2,0},{3,1},{4,6},{5,7},{6,4},{7,5},{8,10},{9,11},{10,... | collective-permute-start | bytes 208904 | tf_op jit(solution)/shard_map/ppermute | solution.py:546
  26.6 0.0 collective-permute-done.6.refs_2_
  26.6 1.7 %second.2 = (f32[8,32,128]{2,1,0:T(8,128)S(1)}, s16[272,128]{1,0:T(8,128)(2,1)S(1)}, f32[8,128]{1,0:T(8,128)S(1)}) custom-call(bf16[288,128]{1,0:T(8,128)(2,1)S(1)} %get-tuple-element.44.refs_0_, s16[272,128]{1,0:T(8,128)(2,1)S(1)} %get-tuple-element.55.refs_1_, s16[272,128]{1,0:T(8,128)(2,1)S(1)} %collective-permute-done.6.refs_2_, ...), custom_call_target="tpu_custom_call" | custom-call | bytes 6000000 | tf_op jit(solution)/shard_map/second/pallas_call | solution.py:104
  28.4 0.5 collective-permute-start.7
  28.8 0.5 collective-permute-done.11.refs_2_
  29.3 1.7 %third.3 = (f32[8,32,128]{2,1,0:T(8,128)S(1)}, s16[272,128]{1,0:T(8,128)(2,1)S(1)}, f32[8,128]{1,0:T(8,128)S(1)}, bf16[272,128]{1,0:T(8,128)(2,1)S(1)}) custom-call(bf16[288,128]{1,0:T(8,128)(2,1)S(1)} %get-tuple-element.45.refs_1_.refs_0_.refs_8_, s16[272,128]{1,0:T(8,128)(2,1)S(1)} %get-tuple-element.62.refs_1_, ...), custom_call_target="tpu_custom_call" | custom-call | bytes 6000000 | tf_op jit(solution)/shard_map/third/pallas_call | solution.py:104
  31.0 2.2 %collective-permute-start.19 = (s16[272,128]{1,0:T(8,128)(2,1)S(1)}, s16[272,128]{1,0:T(8,128)(2,1)S(1)}, u32[]{:S(2)}, u32[]{:S(2)}) collective-permute-start(s16[272,128]{1,0:T(8,128)(2,1)S(1)} %get-tuple-element.69.refs_9_), channel_id=1, source_target_pairs={{0,2},{1,3},{2,0},{3,1},{4,6},{5,7},{6,4},{7,5},{8,10},{9,11},{10,... | collective-permute-start | bytes 208904 | tf_op jit(solution)/shard_map/ppermute | solution.py:546
  33.2 0.2 collective-permute-done.7.refs_2_
  33.4 1.7 %third.2 = (f32[8,32,128]{2,1,0:T(8,128)S(1)}, s16[272,128]{1,0:T(8,128)(2,1)S(1)}, f32[8,128]{1,0:T(8,128)S(1)}, bf16[272,128]{1,0:T(8,128)(2,1)S(1)}) custom-call(bf16[288,128]{1,0:T(8,128)(2,1)S(1)} %get-tuple-element.44.refs_0_, s16[272,128]{1,0:T(8,128)(2,1)S(1)} %get-tuple-element.57.refs_1_, s16[272,128]{1,0:T(8,128)(2,1)S(1)} %collective-permute-done.7.refs_2_, ...), custom_call_target="tpu_custom_call" | custom-call | bytes 6000000 | tf_op jit(solution)/shard_map/third/pallas_call | solution.py:104
  35.1 0.1 collective-permute-start.18
  35.2 3.0 %collective-permute-start.12 = (bf16[272,128]{1,0:T(8,128)(2,1)S(1)}, bf16[272,128]{1,0:T(8,128)(2,1)S(1)}, u32[]{:S(2)}, u32[]{:S(2)}) collective-permute-start(bf16[272,128]{1,0:T(8,128)(2,1)S(1)} %get-tuple-element.64), channel_id=1, source_target_pairs={{4,0},{13,1},{6,2},{15,3},{8,4},{1,5},{10,6},{3,7},{12,8},{5,9},{1... | collective-permute-start | bytes 208904 | tf_op jit(solution)/shard_map/ppermute | solution.py:547
  38.2 0.8 %collective-permute-start.8 = (bf16[272,128]{1,0:T(8,128)(2,1)S(1)}, bf16[272,128]{1,0:T(8,128)(2,1)S(1)}, u32[]{:S(2)}, u32[]{:S(2)}) collective-permute-start(bf16[272,128]{1,0:T(8,128)(2,1)S(1)} %get-tuple-element.59), channel_id=1, source_target_pairs={{0,0},{9,1},{2,2},{11,3},{4,4},{13,5},{6,6},{15,7},{8,8},{1,9},{10... | collective-permute-start | bytes 208904 | tf_op jit(solution)/shard_map/ppermute | solution.py:547
  39.1 0.4 collective-permute-done.18.refs_2_
  39.5 0.7 %table.1 = (f32[8,32,128]{2,1,0:T(8,128)S(1)}, f32[8,32,128]{2,1,0:T(8,128)S(1)}, f32[8,128]{1,0:T(8,128)S(1)}) custom-call(bf16[288,128]{1,0:T(8,128)(2,1)S(1)} %get-tuple-element.44.refs_0_, s16[272,128]{1,0:T(8,128)(2,1)S(1)} %get-tuple-element.65.refs_1_, s16[272,128]{1,0:T(8,128)(2,1)S(1)} %collective-permute-done.18.refs_2_, ...), custom_call_target="tpu_custom_call" | custom-call | bytes 3000000 | tf_op jit(solution)/shard_map/table/pallas_call | solution.py:104
  40.2 0.1 collective-permute-start.20
  40.3 0.0 collective-permute-done.12.refs_5_
  40.3 0.5 collective-permute-start.16
  40.8 1.6 %collective-permute-start.13 = (bf16[272,128]{1,0:T(8,128)(2,1)S(1)}, bf16[272,128]{1,0:T(8,128)(2,1)S(1)}, u32[]{:S(2)}, u32[]{:S(2)}) collective-permute-start(bf16[272,128]{1,0:T(8,128)(2,1)S(1)} %collective-permute-done.12.refs_5_), channel_id=1, source_target_pairs={{0,2},{1,3},{2,0},{3,1},{4,6},{5,7},{6,4},{7,5},{8,10},{9,11},{10,... | collective-permute-start | bytes 208904 | tf_op jit(solution)/shard_map/ppermute | solution.py:548
  42.4 0.0 collective-permute-done.8.refs_3_
  42.4 0.5 collective-permute-start.9
  42.9 0.7 %collective-permute-start.21 = (bf16[272,128]{1,0:T(8,128)(2,1)S(1)}, bf16[272,128]{1,0:T(8,128)(2,1)S(1)}, u32[]{:S(2)}, u32[]{:S(2)}) collective-permute-start(bf16[272,128]{1,0:T(8,128)(2,1)S(1)} %get-tuple-element.76), channel_id=1, source_target_pairs={{0,0},{9,1},{2,2},{11,3},{4,4},{13,5},{6,6},{15,7},{8,8},{1,9},{10... | collective-permute-start | bytes 208904 | tf_op jit(solution)/shard_map/ppermute | solution.py:559
  43.5 3.6 %collective-permute-start.22 = (bf16[272,128]{1,0:T(8,128)(2,1)S(1)}, bf16[272,128]{1,0:T(8,128)(2,1)S(1)}, u32[]{:S(2)}, u32[]{:S(2)}) collective-permute-start(bf16[272,128]{1,0:T(8,128)(2,1)S(1)} %get-tuple-element.77), channel_id=1, source_target_pairs={{4,0},{13,1},{6,2},{15,3},{8,4},{1,5},{10,6},{3,7},{12,8},{5,9},{1... | collective-permute-start | bytes 208904 | tf_op jit(solution)/shard_map/ppermute | solution.py:559
  47.1 1.4 %collective-permute-start.14 = (bf16[272,128]{1,0:T(8,128)(2,1)S(1)}, bf16[272,128]{1,0:T(8,128)(2,1)S(1)}, u32[]{:S(2)}, u32[]{:S(2)}) collective-permute-start(bf16[272,128]{1,0:T(8,128)(2,1)S(1)} %collective-permute-done.8.refs_3_), channel_id=1, source_target_pairs={{0,1},{1,0},{2,3},{3,2},{4,5},{5,4},{6,7},{7,6},{8,9},{9,8},{10,11... | collective-permute-start | bytes 208904 | tf_op jit(solution)/shard_map/ppermute | solution.py:495
  48.6 0.1 collective-permute-start.17
  48.7 0.4 collective-permute-start.15
  49.1 0.1 collective-permute-start.23
  49.2 1.6 %collective-permute-start.24 = (bf16[272,128]{1,0:T(8,128)(2,1)S(1)}, bf16[272,128]{1,0:T(8,128)(2,1)S(1)}, u32[]{:S(2)}, u32[]{:S(2)}) collective-permute-start(bf16[272,128]{1,0:T(8,128)(2,1)S(1)} %collective-permute-done.22.refs_12_), channel_id=1, source_target_pairs={{0,1},{1,0},{2,3},{3,2},{4,5},{5,4},{6,7},{7,6},{8,9},{9,8},{10,11... | collective-permute-start | bytes 208904 | tf_op jit(solution)/shard_map/ppermute | solution.py:495
  50.8 0.9 %collective-permute-done.24.refs_14_ = bf16[272,128]{1,0:T(8,128)(2,1)S(1)} collective-permute-done((bf16[272,128]{1,0:T(8,128)(2,1)S(1)}, bf16[272,128]{1,0:T(8,128)(2,1)S(1)}, u32[]{:S(2)}, u32[]{:S(2)}) %collective-permute-start.24) | collective-permute-done | bytes 69664 | tf_op jit(solution)/shard_map/ppermute | solution.py:495
  51.7 2.3 %finish.1 = (f32[32,4096]{1,0:T(8,128)}, f32[3,3]{1,0:T(4,128)}) custom-call(s32[32]{0:T(128)S(1)} %get-tuple-element.40.order_ref.refs_0_, f32[8,128]{1,0:T(8,128)S(1)} %get-tuple-element.50.refs_1_, bf16[1024,128]{1,0:T(8,128)(2,1)S(1)} %get-tuple-element.51.refs_2_, bf16[272,128]{1,0:T(8,128)(2,1)S(1)} %collective-permute-done.8.refs_3_, ...), custom_call_target="tpu_custom_call" | custom-call | bytes 6000000 | tf_op jit(solution)/shard_map/finish/pallas_call | solution.py:104
  (22 shorter events, 0.1 us)
Async XLA Ops:
  1.3 1.0 %copy-start.2 = (bf16[32,4096]{1,0:T(8,128)(2,1)S(1)}, bf16[32,4096]{1,0:T(8,128)(2,1)}, u32[]{:S(2)}) copy-start(bf16[32,4096]{1,0:T(8,128)(2,1)} %start_ref.1) | copy-start | bytes 786436
  2.3 6.1 %copy-start = (bf16[32,7,4096]{2,0,1:T(8,128)(2,1)S(1)}, bf16[32,7,4096]{2,0,1:T(8,128)(2,1)}, u32[]{:S(2)}) copy-start(bf16[32,7,4096]{2,0,1:T(8,128)(2,1)} %param.9) | copy-start | bytes 5505028
  4.6 8.8 %collective-permute-start = (bf16[288,128]{1,0:T(8,128)(2,1)S(1)}, bf16[288,128]{1,0:T(8,128)(2,1)S(1)}, u32[]{:S(2)}, u32[]{:S(2)}) collective-permute-start(bf16[288,128]{1,0:T(8,128)(2,1)S(1)} %get-tuple-element.41), channel_id=1, source_target_pairs={{0,0},{1,9},{2,2},{3,11},{4,4},{5,13},{6,6},{7,15},{8,8},{9,1},{10... | collective-permute-start | bytes 221192 | tf_op jit(solution)/shard_map/ppermute | solution.py:509
  5.3 8.1 %collective-permute-start.1 = (bf16[288,128]{1,0:T(8,128)(2,1)S(1)}, bf16[288,128]{1,0:T(8,128)(2,1)S(1)}, u32[]{:S(2)}, u32[]{:S(2)}) collective-permute-start(bf16[288,128]{1,0:T(8,128)(2,1)S(1)} %get-tuple-element.42), channel_id=1, source_target_pairs={{0,4},{1,13},{2,6},{3,15},{4,8},{5,1},{6,10},{7,3},{8,12},{9,5},{1... | collective-permute-start | bytes 221192 | tf_op jit(solution)/shard_map/ppermute | solution.py:509
  8.4 5.1 %copy-start.1 = (bf16[32,7,4096]{2,0,1:T(8,128)(2,1)S(1)}, bf16[32,7,4096]{2,0,1:T(8,128)(2,1)}, u32[]{:S(2)}) copy-start(bf16[32,7,4096]{2,0,1:T(8,128)(2,1)} %param.10) | copy-start | bytes 5505028
  10.5 5.8 %collective-permute-start.2 = (bf16[8,64,512]{2,1,0:T(8,128)(2,1)S(1)}, bf16[8,64,512]{2,1,0:T(8,128)(2,1)S(1)}, u32[]{:S(2)}, u32[]{:S(2)}) collective-permute-start(bf16[8,64,512]{2,1,0:T(8,128)(2,1)S(1)} %get-tuple-element.48), channel_id=1, source_target_pairs={{0,1},{1,0},{2,3},{3,2},{4,5},{5,4},{6,7},{7,6},{8,9},{9,8},{10,11... | collective-permute-start | bytes 1572872 | tf_op jit(solution)/shard_map/ppermute | solution.py:495
  15.5 2.0 %collective-permute-start.3 = (bf16[8,64,512]{2,1,0:T(8,128)(2,1)S(1)}, bf16[8,64,512]{2,1,0:T(8,128)(2,1)S(1)}, u32[]{:S(2)}, u32[]{:S(2)}) collective-permute-start(bf16[8,64,512]{2,1,0:T(8,128)(2,1)S(1)} %get-tuple-element.49), channel_id=1, source_target_pairs={{0,1},{1,0},{2,3},{3,2},{4,5},{5,4},{6,7},{7,6},{8,9},{9,8},{10,11... | collective-permute-start | bytes 1572872 | tf_op jit(solution)/shard_map/ppermute | solution.py:495
  15.8 4.7 %collective-permute-start.4 = (bf16[8,64,512]{2,1,0:T(8,128)(2,1)S(1)}, bf16[8,64,512]{2,1,0:T(8,128)(2,1)S(1)}, u32[]{:S(2)}, u32[]{:S(2)}) collective-permute-start(bf16[8,64,512]{2,1,0:T(8,128)(2,1)S(1)} %get-tuple-element.53), channel_id=1, source_target_pairs={{0,1},{1,0},{2,3},{3,2},{4,5},{5,4},{6,7},{7,6},{8,9},{9,8},{10,11... | collective-permute-start | bytes 1572872 | tf_op jit(solution)/shard_map/ppermute | solution.py:495
  16.1 4.4 %collective-permute-start.5 = (bf16[8,64,512]{2,1,0:T(8,128)(2,1)S(1)}, bf16[8,64,512]{2,1,0:T(8,128)(2,1)S(1)}, u32[]{:S(2)}, u32[]{:S(2)}) collective-permute-start(bf16[8,64,512]{2,1,0:T(8,128)(2,1)S(1)} %get-tuple-element.54), channel_id=1, source_target_pairs={{0,1},{1,0},{2,3},{3,2},{4,5},{5,4},{6,7},{7,6},{8,9},{9,8},{10,11... | collective-permute-start | bytes 1572872 | tf_op jit(solution)/shard_map/ppermute | solution.py:495
  18.8 4.4 %collective-permute-start.10 = (s16[272,128]{1,0:T(8,128)(2,1)S(1)}, s16[272,128]{1,0:T(8,128)(2,1)S(1)}, u32[]{:S(2)}, u32[]{:S(2)}) collective-permute-start(s16[272,128]{1,0:T(8,128)(2,1)S(1)} %get-tuple-element.60.refs_1_), channel_id=1, source_target_pairs={{0,2},{1,3},{2,0},{3,1},{4,6},{5,7},{6,4},{7,5},{8,10},{9,11},{10,... | collective-permute-start | bytes 208904 | tf_op jit(solution)/shard_map/ppermute | solution.py:535
  21.9 4.7 %collective-permute-start.6 = (s16[272,128]{1,0:T(8,128)(2,1)S(1)}, s16[272,128]{1,0:T(8,128)(2,1)S(1)}, u32[]{:S(2)}, u32[]{:S(2)}) collective-permute-start(s16[272,128]{1,0:T(8,128)(2,1)S(1)} %get-tuple-element.55.refs_1_), channel_id=1, source_target_pairs={{0,2},{1,3},{2,0},{3,1},{4,6},{5,7},{6,4},{7,5},{8,10},{9,11},{10,... | collective-permute-start | bytes 208904 | tf_op jit(solution)/shard_map/ppermute | solution.py:535
  24.9 4.4 %collective-permute-start.11 = (s16[272,128]{1,0:T(8,128)(2,1)S(1)}, s16[272,128]{1,0:T(8,128)(2,1)S(1)}, u32[]{:S(2)}, u32[]{:S(2)}) collective-permute-start(s16[272,128]{1,0:T(8,128)(2,1)S(1)} %get-tuple-element.62.refs_1_), channel_id=1, source_target_pairs={{0,2},{1,3},{2,0},{3,1},{4,6},{5,7},{6,4},{7,5},{8,10},{9,11},{10,... | collective-permute-start | bytes 208904 | tf_op jit(solution)/shard_map/ppermute | solution.py:546
  28.4 5.0 %collective-permute-start.7 = (s16[272,128]{1,0:T(8,128)(2,1)S(1)}, s16[272,128]{1,0:T(8,128)(2,1)S(1)}, u32[]{:S(2)}, u32[]{:S(2)}) collective-permute-start(s16[272,128]{1,0:T(8,128)(2,1)S(1)} %get-tuple-element.57.refs_1_), channel_id=1, source_target_pairs={{0,2},{1,3},{2,0},{3,1},{4,6},{5,7},{6,4},{7,5},{8,10},{9,11},{10,... | collective-permute-start | bytes 208904 | tf_op jit(solution)/shard_map/ppermute | solution.py:546
  31.0 8.1 %collective-permute-start.19 = (s16[272,128]{1,0:T(8,128)(2,1)S(1)}, s16[272,128]{1,0:T(8,128)(2,1)S(1)}, u32[]{:S(2)}, u32[]{:S(2)}) collective-permute-start(s16[272,128]{1,0:T(8,128)(2,1)S(1)} %get-tuple-element.69.refs_9_), channel_id=1, source_target_pairs={{0,2},{1,3},{2,0},{3,1},{4,6},{5,7},{6,4},{7,5},{8,10},{9,11},{10,... | collective-permute-start | bytes 208904 | tf_op jit(solution)/shard_map/ppermute | solution.py:546
  35.1 4.4 %collective-permute-start.18 = (s16[272,128]{1,0:T(8,128)(2,1)S(1)}, s16[272,128]{1,0:T(8,128)(2,1)S(1)}, u32[]{:S(2)}, u32[]{:S(2)}) collective-permute-start(s16[272,128]{1,0:T(8,128)(2,1)S(1)} %get-tuple-element.65.refs_1_), channel_id=1, source_target_pairs={{0,2},{1,3},{2,0},{3,1},{4,6},{5,7},{6,4},{7,5},{8,10},{9,11},{10,... | collective-permute-start | bytes 208904 | tf_op jit(solution)/shard_map/ppermute | solution.py:546
  35.2 5.1 %collective-permute-start.12 = (bf16[272,128]{1,0:T(8,128)(2,1)S(1)}, bf16[272,128]{1,0:T(8,128)(2,1)S(1)}, u32[]{:S(2)}, u32[]{:S(2)}) collective-permute-start(bf16[272,128]{1,0:T(8,128)(2,1)S(1)} %get-tuple-element.64), channel_id=1, source_target_pairs={{4,0},{13,1},{6,2},{15,3},{8,4},{1,5},{10,6},{3,7},{12,8},{5,9},{1... | collective-permute-start | bytes 208904 | tf_op jit(solution)/shard_map/ppermute | solution.py:547
  38.2 4.1 %collective-permute-start.8 = (bf16[272,128]{1,0:T(8,128)(2,1)S(1)}, bf16[272,128]{1,0:T(8,128)(2,1)S(1)}, u32[]{:S(2)}, u32[]{:S(2)}) collective-permute-start(bf16[272,128]{1,0:T(8,128)(2,1)S(1)} %get-tuple-element.59), channel_id=1, source_target_pairs={{0,0},{9,1},{2,2},{11,3},{4,4},{13,5},{6,6},{15,7},{8,8},{1,9},{10... | collective-permute-start | bytes 208904 | tf_op jit(solution)/shard_map/ppermute | solution.py:547
  40.2 2.6 %collective-permute-start.20 = (f32[8,128]{1,0:T(8,128)S(1)}, f32[8,128]{1,0:T(8,128)S(1)}, u32[]{:S(2)}, u32[]{:S(2)}) collective-permute-start(f32[8,128]{1,0:T(8,128)S(1)} %get-tuple-element.73.table_ref), channel_id=1, source_target_pairs={{0,1},{1,0},{2,3},{3,2},{4,5},{5,4},{6,7},{7,6},{8,9},{9,8},{10,11... | collective-permute-start | bytes 12296 | tf_op jit(solution)/shard_map/ppermute | solution.py:495
  40.3 6.8 %collective-permute-start.16 = (bf16[272,128]{1,0:T(8,128)(2,1)S(1)}, bf16[272,128]{1,0:T(8,128)(2,1)S(1)}, u32[]{:S(2)}, u32[]{:S(2)}) collective-permute-start(bf16[272,128]{1,0:T(8,128)(2,1)S(1)} %collective-permute-done.12.refs_5_), channel_id=1, source_target_pairs={{0,1},{1,0},{2,3},{3,2},{4,5},{5,4},{6,7},{7,6},{8,9},{9,8},{10,11... | collective-permute-start | bytes 208904 | tf_op jit(solution)/shard_map/ppermute | solution.py:495
  40.8 7.8 %collective-permute-start.13 = (bf16[272,128]{1,0:T(8,128)(2,1)S(1)}, bf16[272,128]{1,0:T(8,128)(2,1)S(1)}, u32[]{:S(2)}, u32[]{:S(2)}) collective-permute-start(bf16[272,128]{1,0:T(8,128)(2,1)S(1)} %collective-permute-done.12.refs_5_), channel_id=1, source_target_pairs={{0,2},{1,3},{2,0},{3,1},{4,6},{5,7},{6,4},{7,5},{8,10},{9,11},{10,... | collective-permute-start | bytes 208904 | tf_op jit(solution)/shard_map/ppermute | solution.py:548
  42.4 6.3 %collective-permute-start.9 = (bf16[272,128]{1,0:T(8,128)(2,1)S(1)}, bf16[272,128]{1,0:T(8,128)(2,1)S(1)}, u32[]{:S(2)}, u32[]{:S(2)}) collective-permute-start(bf16[272,128]{1,0:T(8,128)(2,1)S(1)} %collective-permute-done.8.refs_3_), channel_id=1, source_target_pairs={{0,2},{1,3},{2,0},{3,1},{4,6},{5,7},{6,4},{7,5},{8,10},{9,11},{10,... | collective-permute-start | bytes 208904 | tf_op jit(solution)/shard_map/ppermute | solution.py:548
  42.9 6.2 %collective-permute-start.21 = (bf16[272,128]{1,0:T(8,128)(2,1)S(1)}, bf16[272,128]{1,0:T(8,128)(2,1)S(1)}, u32[]{:S(2)}, u32[]{:S(2)}) collective-permute-start(bf16[272,128]{1,0:T(8,128)(2,1)S(1)} %get-tuple-element.76), channel_id=1, source_target_pairs={{0,0},{9,1},{2,2},{11,3},{4,4},{13,5},{6,6},{15,7},{8,8},{1,9},{10... | collective-permute-start | bytes 208904 | tf_op jit(solution)/shard_map/ppermute | solution.py:559
  43.5 5.6 %collective-permute-start.22 = (bf16[272,128]{1,0:T(8,128)(2,1)S(1)}, bf16[272,128]{1,0:T(8,128)(2,1)S(1)}, u32[]{:S(2)}, u32[]{:S(2)}) collective-permute-start(bf16[272,128]{1,0:T(8,128)(2,1)S(1)} %get-tuple-element.77), channel_id=1, source_target_pairs={{4,0},{13,1},{6,2},{15,3},{8,4},{1,5},{10,6},{3,7},{12,8},{5,9},{1... | collective-permute-start | bytes 208904 | tf_op jit(solution)/shard_map/ppermute | solution.py:559
  47.1 3.6 %collective-permute-start.14 = (bf16[272,128]{1,0:T(8,128)(2,1)S(1)}, bf16[272,128]{1,0:T(8,128)(2,1)S(1)}, u32[]{:S(2)}, u32[]{:S(2)}) collective-permute-start(bf16[272,128]{1,0:T(8,128)(2,1)S(1)} %collective-permute-done.8.refs_3_), channel_id=1, source_target_pairs={{0,1},{1,0},{2,3},{3,2},{4,5},{5,4},{6,7},{7,6},{8,9},{9,8},{10,11... | collective-permute-start | bytes 208904 | tf_op jit(solution)/shard_map/ppermute | solution.py:495
  48.6 2.2 %collective-permute-start.17 = (bf16[272,128]{1,0:T(8,128)(2,1)S(1)}, bf16[272,128]{1,0:T(8,128)(2,1)S(1)}, u32[]{:S(2)}, u32[]{:S(2)}) collective-permute-start(bf16[272,128]{1,0:T(8,128)(2,1)S(1)} %collective-permute-done.13.refs_6_), channel_id=1, source_target_pairs={{0,1},{1,0},{2,3},{3,2},{4,5},{5,4},{6,7},{7,6},{8,9},{9,8},{10,11... | collective-permute-start | bytes 208904 | tf_op jit(solution)/shard_map/ppermute | solution.py:495
  48.7 2.1 %collective-permute-start.15 = (bf16[272,128]{1,0:T(8,128)(2,1)S(1)}, bf16[272,128]{1,0:T(8,128)(2,1)S(1)}, u32[]{:S(2)}, u32[]{:S(2)}) collective-permute-start(bf16[272,128]{1,0:T(8,128)(2,1)S(1)} %collective-permute-done.9.refs_4_), channel_id=1, source_target_pairs={{0,1},{1,0},{2,3},{3,2},{4,5},{5,4},{6,7},{7,6},{8,9},{9,8},{10,11... | collective-permute-start | bytes 208904 | tf_op jit(solution)/shard_map/ppermute | solution.py:495
  49.1 1.7 %collective-permute-start.23 = (bf16[272,128]{1,0:T(8,128)(2,1)S(1)}, bf16[272,128]{1,0:T(8,128)(2,1)S(1)}, u32[]{:S(2)}, u32[]{:S(2)}) collective-permute-start(bf16[272,128]{1,0:T(8,128)(2,1)S(1)} %collective-permute-done.21.refs_11_), channel_id=1, source_target_pairs={{0,1},{1,0},{2,3},{3,2},{4,5},{5,4},{6,7},{7,6},{8,9},{9,8},{10,11... | collective-permute-start | bytes 208904 | tf_op jit(solution)/shard_map/ppermute | solution.py:495
  49.2 2.5 %collective-permute-start.24 = (bf16[272,128]{1,0:T(8,128)(2,1)S(1)}, bf16[272,128]{1,0:T(8,128)(2,1)S(1)}, u32[]{:S(2)}, u32[]{:S(2)}) collective-permute-start(bf16[272,128]{1,0:T(8,128)(2,1)S(1)} %collective-permute-done.22.refs_12_), channel_id=1, source_target_pairs={{0,1},{1,0},{2,3},{3,2},{4,5},{5,4},{6,7},{7,6},{8,9},{9,8},{10,11... | collective-permute-start | bytes 208904 | tf_op jit(solution)/shard_map/ppermute | solution.py:495

commit v6 on v5

--- a/solution.py
+++ b/solution.py
@@ -147,16 +147,25 @@
     return jnp.concatenate([tile, jnp.zeros_like(tile)], axis=1)
 
 
-def arrange_kernel(order_ref, meta_ref, env_ref, *refs):
-    ships, outs = refs[:-4], refs[-4:]
-    masked = not ships
-    if ships:
+def arrange_kernel(masked, *refs):
+    ins, outs = refs[:-4], refs[-4:]
+    if masked:
+        first_ref, env_ref, meta_ref = ins
+    else:
+        first_ref, env_ref, *ships = ins
         riding = riding_sums(ships)
     chans, slots = env_ref.shape[:2]
     cap = outs[0].shape[0]
-    first = blocks_first(order_ref, 0, slots, slots)
+    first = first_ref[...]
     second = pair_to_kept()
-    low = iota((1, 2 * LANES), 1) % LANES < B
+    if masked:
+        rows = []
+        for w in range(8):
+            row = meta_ref[3 + w : 4 + w, :].astype(F32) if w < chans else jnp.zeros((1, slots), F32)
+            rows.append(jnp.broadcast_to(jnp.concatenate([row] * 8, axis=1), (LANES, 8 * slots)))
+        mask = lax.dot_general(
+            first, jnp.concatenate(rows, axis=0).astype(BF16), (((1,), (1,)), ((), ())),
+            preferred_element_type=F32)
     blank = jnp.zeros((slots, LANES), BF16)
     for g in range(4):
         used = [w for w in (2 * g, 2 * g + 1) if w < chans]
@@ -167,15 +176,13 @@
                 parts = [env_ref[w, :, i * LANES : (i + 1) * LANES] for w in used]
                 rows.append(jnp.concatenate(parts + [blank] * (2 - len(used)), axis=1))
             x = jnp.concatenate(rows, axis=0)
-            x = jnp.dot(first, x, preferred_element_type=F32).astype(BF16)
-            chunks.append(jnp.dot(x, second, preferred_element_type=F32))
+            x = jnp.dot(first, x, preferred_element_type=F32)
+            if masked:
+                x = x * mask[:, 2 * g * LANES : 2 * (g + 1) * LANES]
+            chunks.append(jnp.dot(x.astype(BF16), second, preferred_element_type=F32))
         for k in range(slots):
             x = jnp.concatenate([chunk[8 * k : 8 * k + 8] for chunk in chunks], axis=0)
-            if masked:
-                slot = order_ref[k]
-                kept = [meta_ref[3 + w, slot].astype(F32) for w in used]
-                x = x * jnp.where(low, kept[0], kept[-1])
-            elif g == 3 and k in (2 * cap, 3 * cap):
+            if not masked and g == 3 and k in (2 * cap, 3 * cap):
                 x = x + riding
             x = x.astype(BF16)
             for p in range(2):
@@ -184,11 +191,13 @@
                 ]
 
 
-def ship_kernel(meta_ref, start_ref, order_ref, near_ref, far_ref, home_ref, seen):
+def ship_kernel(meta_ref, start_ref, first_ref, last_ref, near_ref, far_ref, home_ref, order_ref, seen):
     sort_slots(position()[1], meta_ref, order_ref, seen)
     slots = start_ref.shape[0]
     cap = slots // 4
     first = blocks_first(order_ref, 0, slots, slots)
+    first_ref[...] = first
+    last_ref[...] = slots_last(order_ref, slots)
     second = to_kept()
     chunks = []
     for c in range(4):
@@ -425,7 +434,7 @@
     return projections, rest
 
 
-def finish_kernel(count, nodes, order_ref, scale_ref, home_ref, *refs):
+def finish_kernel(count, nodes, back_ref, scale_ref, home_ref, *refs):
     early, late, (out_ref, proj_ref) = refs[:8], refs[8:12], refs[12:]
     node, core = position()
     slots = out_ref.shape[0]
@@ -456,7 +465,7 @@
         x = x + coeff[1] * jnp.where(ahead, here, there) + coeff[2] * jnp.where(ahead, there, here)
         x = x + coeff[3] * last_ref[:rows, :].astype(F32)
         blocks.append(x)
-    first = slots_last(order_ref, slots)
+    first = back_ref[...]
     second = from_kept_twice()
     per = rows // HALF
     for c in range(4):
@@ -502,21 +511,23 @@
     tile = shape((8, LANES))
     code = shape((cap * HALF + 16, LANES), jnp.int16)
     payload = shape((cap * HALF + 32, LANES), BF16)
-    order, *ships, home = call(
+    one_hots = shape((8 * slots, 8 * slots), BF16)
+    first, back, *ships, home = call(
         ship_kernel, "ship",
-        (shape((slots,), jnp.int32), payload, payload, shape((slots * HALF, LANES), BF16)),
-        (meta, start_vector), "sv", [pltpu.SMEM((nodes,), jnp.int32)], "svvv", 2.0, ROOMY, True)
+        (one_hots, one_hots, payload, payload, shape((slots * HALF, LANES), BF16)),
+        (meta, start_vector), "sv",
+        [pltpu.SMEM((slots,), jnp.int32), pltpu.SMEM((nodes,), jnp.int32)], "vvvvv", 2.0, ROOMY, True)
     ships = [lax.ppermute(x, ("sector", "op"), route(t, False)) for t, x in enumerate(ships)]
 
-    def arrange(env, *more):
+    def arrange(masked, operands, kinds):
         sets = call(
-            arrange_kernel, "arrange", (environment,) * 4, (order, meta, env, *more), "ssv" + "v" * len(more),
+            lambda *refs: arrange_kernel(masked, *refs), "arrange", (environment,) * 4, operands, kinds,
             cost=3.0, limit=ARRANGE, compute=True)
         return sets[:2], [across(x) for x in sets[2:]]
 
-    keep_left, got_left = arrange(left)
+    keep_left, got_left = arrange(True, (first, left, meta), "vvv")
     ships = call(arrived_kernel, "arrived", (payload, payload), (*ships, keep_left[0]), "vva", cost=0.3)
-    keep_right, got_right = arrange(right, *ships)
+    keep_right, got_right = arrange(False, (first, right, *ships), "vvvv")
     envs = [(keep_left[t], keep_right[t], got_left[t], got_right[t]) for t in range(2)]
 
     def step(k):
@@ -564,7 +575,7 @@
 
     return call(
         finish, "finish", (shape((slots, B * B)), shape((ITERS, ITERS))),
-        (order, scale, home, *early, *late), "s" + "v" * 14)
+        (back, scale, home, *early, *late), "v" * 15)
 
 
 def pack_rows(data, index, nodes, cap):

time: 54.2 us -> 52.3 us (0.965)
  Pallas kernels: 19.1 us -> 16.8 us
    pallas_call x13, Pallas kernels: 19.1 us -> 16.8 us  [call(): pl.pallas_call(kernel, out_shape=out_shape, in_specs=[pl.BlockSpec(memory...]
  transfers between devices with their start and end apart: 25 -> 25, of which waited for: 6 -> 7; matrix products, arithmetic and copies ran while one was open for 0% -> 0% of each run, Pallas kernels for 27% -> 25%
where the time goes in v6:
time: 52.3 us; the launch traced here: 52.1 us
  starting transfers between devices  28.5 us (54%)
  Pallas kernels  16.8 us (32%)
  waiting for transfers between devices  4.34 us (8%)
  local copies, waits for them, and re-layouts  0.95 us (2%)
  between operations  0.8 us (2%)
  other arithmetic  0.71 us (1%)
    pallas_call x13, Pallas kernels, call(): pl.pallas_call(kernel, out_shape=out_shape, in_specs=[pl.BlockSpec(memory...  16.8 us
    ppermute x11, starting transfers between devices, across(): return lax.ppermute(x, 'op', swap_core)  7.98 us
    ppermute x6, starting transfers between devices, paired(): images[t] = (y, lax.ppermute(y, 'op', swap_x))  6.47 us
    ppermute x2, starting transfers between devices, paired(): lax.ppermute(x, ('sector', 'op'), route(t, True))  4.37 us
    ppermute x2, starting transfers between devices, paired(): early += [lax.ppermute(x, ('sector', 'op'), route(t, True)) for x in parcel]  3.95 us
    ppermute x2, starting transfers between devices, paired(): lax.ppermute(x, ('sector', 'op'), route(t, False))  3.75 us
    ppermute x2, starting transfers between devices, paired(): early = [(x, lax.ppermute(x, 'op', swap_x)) for x in early]  2.03 us
    ppermute x6, waiting for transfers between devices, paired(): images[t] = (y, lax.ppermute(y, 'op', swap_x))  2 us
  transfers between devices with their start and end apart: 25, of which 7 were waited for; matrix products, arithmetic and copies ran while one was open for 0% of the time, Pallas kernels for 25%

profile of v6, /device:TPU:0, one launch (start us, length us, event | category | flops | bytes accessed | tf_op | source)
XLA Modules:
  0.0 52.1 jit_solution(9302838306561381305)
XLA Ops:
  0.6 0.7 %pad_add_fusion.meta_ref.refs_2_ = s32[10,32]{1,0:T(8,128)S(1)} fusion(s32[7,32]{1,0:T(8,128)} %bitcast.7, s32[2,32]{1,0:T(2,128)} %bitcast.8, s32[1,32]{1,0:T(1,128)} %bitcast.9), kind=kLoop, calls=%fused_computation | loop fusion | flops 640 | bytes 2560 | tf_op jit(solution)/shard_map/concatenate | solution.py:492
  1.4 0.9 %copy-done.2 = bf16[32,4096]{1,0:T(8,128)(2,1)S(1)} copy-done((bf16[32,4096]{1,0:T(8,128)(2,1)S(1)}, bf16[32,4096]{1,0:T(8,128)(2,1)}, u32[]{:S(2)}) %copy-start.2) | copy-done | bytes 262168
  2.3 1.8 %ship.1 = (bf16[256,256]{1,0:T(8,128)(2,1)S(1)}, bf16[256,256]{1,0:T(8,128)(2,1)S(1)}, bf16[288,128]{1,0:T(8,128)(2,1)S(1)}, bf16[288,128]{1,0:T(8,128)(2,1)S(1)}, bf16[1024,128]{1,0:T(8,128)(2,1)S(1)}) custom-call(s32[10,32]{1,0:T(8,128)S(1)} %pad_add_fusion.meta_ref.refs_2_, bf16[32,4096]{1,0:T(8,128)(2,1)S(1)} %copy-done.2), custom_call_target="tpu_custom_call" | custom-call | flops 2000000000 | bytes 1024 | tf_op jit(solution)/shard_map/ship/pallas_call | solution.py:104
  4.1 0.7 %collective-permute-start = (bf16[288,128]{1,0:T(8,128)(2,1)S(1)}, bf16[288,128]{1,0:T(8,128)(2,1)S(1)}, u32[]{:S(2)}, u32[]{:S(2)}) collective-permute-start(bf16[288,128]{1,0:T(8,128)(2,1)S(1)} %get-tuple-element.42), channel_id=1, source_target_pairs={{0,0},{1,9},{2,2},{3,11},{4,4},{5,13},{6,6},{7,15},{8,8},{9,1},{10... | collective-permute-start | bytes 221192 | tf_op jit(solution)/shard_map/ppermute | solution.py:520
  4.7 3.1 %collective-permute-start.1 = (bf16[288,128]{1,0:T(8,128)(2,1)S(1)}, bf16[288,128]{1,0:T(8,128)(2,1)S(1)}, u32[]{:S(2)}, u32[]{:S(2)}) collective-permute-start(bf16[288,128]{1,0:T(8,128)(2,1)S(1)} %get-tuple-element.43), channel_id=1, source_target_pairs={{0,4},{1,13},{2,6},{3,15},{4,8},{5,1},{6,10},{7,3},{8,12},{9,5},{1... | collective-permute-start | bytes 221192 | tf_op jit(solution)/shard_map/ppermute | solution.py:520
  7.8 1.7 %arrange.2 = (bf16[8,64,512]{2,1,0:T(8,128)(2,1)S(1)}, bf16[8,64,512]{2,1,0:T(8,128)(2,1)S(1)}, bf16[8,64,512]{2,1,0:T(8,128)(2,1)S(1)}, bf16[8,64,512]{2,1,0:T(8,128)(2,1)S(1)}) custom-call(bf16[256,256]{1,0:T(8,128)(2,1)S(1)} %get-tuple-element.44.refs_0_, bf16[7,32,4096]{2,1,0:T(8,128)(2,1)S(1)} %bitcast.5, s32[10,32]{1,0:T(8,128)S(1)} %pad_add_fusion.meta_ref.refs_2_), custom_call_target="tpu_custom_call" | custom-call | flops 3000000000 | bytes 1024 | tf_op jit(solution)/shard_map/arrange/pallas_call | solution.py:104
  9.5 2.9 %collective-permute-start.2 = (bf16[8,64,512]{2,1,0:T(8,128)(2,1)S(1)}, bf16[8,64,512]{2,1,0:T(8,128)(2,1)S(1)}, u32[]{:S(2)}, u32[]{:S(2)}) collective-permute-start(bf16[8,64,512]{2,1,0:T(8,128)(2,1)S(1)} %get-tuple-element.50), channel_id=1, source_target_pairs={{0,1},{1,0},{2,3},{3,2},{4,5},{5,4},{6,7},{7,6},{8,9},{9,8},{10,11... | collective-permute-start | bytes 1572872 | tf_op jit(solution)/shard_map/ppermute | solution.py:504
  12.4 0.0 collective-permute-done.near_in_ref
  12.5 0.3 collective-permute-done.1.far_in_ref
  12.8 1.4 %arrange.3 = (bf16[8,64,512]{2,1,0:T(8,128)(2,1)S(1)}, bf16[8,64,512]{2,1,0:T(8,128)(2,1)S(1)}, bf16[8,64,512]{2,1,0:T(8,128)(2,1)S(1)}, bf16[8,64,512]{2,1,0:T(8,128)(2,1)S(1)}) custom-call(bf16[256,256]{1,0:T(8,128)(2,1)S(1)} %get-tuple-element.44.refs_0_, bf16[7,32,4096]{2,1,0:T(8,128)(2,1)S(1)} %bitcast.6, ...), custom_call_target="tpu_custom_call" | custom-call | flops 3000000000 | bytes 1024 | tf_op jit(solution)/shard_map/arrange/pallas_call | solution.py:104
  14.2 0.4 collective-permute-start.3
  14.6 0.2 collective-permute-start.4
  14.8 0.3 collective-permute-start.5
  15.1 1.1 %collective-permute-done.3.refs_5_.refs_7_.refs_8_ = bf16[8,64,512]{2,1,0:T(8,128)(2,1)S(1)} collective-permute-done((bf16[8,64,512]{2,1,0:T(8,128)(2,1)S(1)}, bf16[8,64,512]{2,1,0:T(8,128)(2,1)S(1)}, u32[]{:S(2)}, u32[]{:S(2)}) %collective-permute-start.3) | collective-permute-done | bytes 524320 | tf_op jit(solution)/shard_map/ppermute | solution.py:504
  16.2 1.3 %first.2 = (f32[8,32,128]{2,1,0:T(8,128)S(1)}, s16[272,128]{1,0:T(8,128)(2,1)S(1)}, f32[8,128]{1,0:T(8,128)S(1)}) custom-call(bf16[288,128]{1,0:T(8,128)(2,1)S(1)} %get-tuple-element.46.refs_2_.refs_0_, bf16[288,128]{1,0:T(8,128)(2,1)S(1)} %get-tuple-element.47.refs_3_.refs_1_.refs_0_.refs_8_, ...), custom_call_target="tpu_custom_call" | custom-call | bytes 6000000 | tf_op jit(solution)/shard_map/first/pallas_call | solution.py:104
  17.5 1.8 %collective-permute-start.10 = (s16[272,128]{1,0:T(8,128)(2,1)S(1)}, s16[272,128]{1,0:T(8,128)(2,1)S(1)}, u32[]{:S(2)}, u32[]{:S(2)}) collective-permute-start(s16[272,128]{1,0:T(8,128)(2,1)S(1)} %get-tuple-element.62.refs_1_), channel_id=1, source_target_pairs={{0,2},{1,3},{2,0},{3,1},{4,6},{5,7},{6,4},{7,5},{8,10},{9,11},{10,... | collective-permute-start | bytes 208904 | tf_op jit(solution)/shard_map/ppermute | solution.py:546
  19.3 0.0 collective-permute-done.4.refs_4_.refs_6_.refs_7_
  19.3 1.3 %first.3 = (f32[8,32,128]{2,1,0:T(8,128)S(1)}, s16[272,128]{1,0:T(8,128)(2,1)S(1)}, f32[8,128]{1,0:T(8,128)}) custom-call(bf16[288,128]{1,0:T(8,128)(2,1)S(1)} %get-tuple-element.46.refs_2_.refs_0_, bf16[288,128]{1,0:T(8,128)(2,1)S(1)} %get-tuple-element.47.refs_3_.refs_1_.refs_0_.refs_8_, ...), custom_call_target="tpu_custom_call" | custom-call | bytes 6000000 | tf_op jit(solution)/shard_map/first/pallas_call | solution.py:104
  20.6 0.4 collective-permute-start.6
  21.0 1.0 %collective-permute-done.10.refs_2_ = s16[272,128]{1,0:T(8,128)(2,1)S(1)} collective-permute-done((s16[272,128]{1,0:T(8,128)(2,1)S(1)}, s16[272,128]{1,0:T(8,128)(2,1)S(1)}, u32[]{:S(2)}, u32[]{:S(2)}) %collective-permute-start.10) | collective-permute-done | bytes 69664 | tf_op jit(solution)/shard_map/ppermute | solution.py:546
  22.0 1.7 %second.3 = (f32[8,32,128]{2,1,0:T(8,128)S(1)}, s16[272,128]{1,0:T(8,128)(2,1)S(1)}, f32[8,128]{1,0:T(8,128)S(1)}) custom-call(bf16[288,128]{1,0:T(8,128)(2,1)S(1)} %get-tuple-element.47.refs_3_.refs_1_.refs_0_.refs_8_, s16[272,128]{1,0:T(8,128)(2,1)S(1)} %get-tuple-element.62.refs_1_, s16[272,128]{1,0:T(8,128)(2,1)S(1)} %collective-permute-done.10.refs_2_, ...), custom_call_target="tpu_custom_call" | custom-call | bytes 6000000 | tf_op jit(solution)/shard_map/second/pallas_call | solution.py:104
  23.7 1.7 %collective-permute-start.11 = (s16[272,128]{1,0:T(8,128)(2,1)S(1)}, s16[272,128]{1,0:T(8,128)(2,1)S(1)}, u32[]{:S(2)}, u32[]{:S(2)}) collective-permute-start(s16[272,128]{1,0:T(8,128)(2,1)S(1)} %get-tuple-element.64.refs_1_), channel_id=1, source_target_pairs={{0,2},{1,3},{2,0},{3,1},{4,6},{5,7},{6,4},{7,5},{8,10},{9,11},{10,... | collective-permute-start | bytes 208904 | tf_op jit(solution)/shard_map/ppermute | solution.py:557
  25.4 1.7 %second.2 = (f32[8,32,128]{2,1,0:T(8,128)S(1)}, s16[272,128]{1,0:T(8,128)(2,1)S(1)}, f32[8,128]{1,0:T(8,128)S(1)}) custom-call(bf16[288,128]{1,0:T(8,128)(2,1)S(1)} %get-tuple-element.46.refs_2_.refs_0_, s16[272,128]{1,0:T(8,128)(2,1)S(1)} %get-tuple-element.57.refs_1_, s16[272,128]{1,0:T(8,128)(2,1)S(1)} %collective-permute-done.6.refs_2_, ...), custom_call_target="tpu_custom_call" | custom-call | bytes 6000000 | tf_op jit(solution)/shard_map/second/pallas_call | solution.py:104
  27.1 0.5 collective-permute-start.7
  27.5 0.5 collective-permute-done.11.refs_2_
  28.1 1.7 %third.3 = (f32[8,32,128]{2,1,0:T(8,128)S(1)}, s16[272,128]{1,0:T(8,128)(2,1)S(1)}, f32[8,128]{1,0:T(8,128)S(1)}, bf16[272,128]{1,0:T(8,128)(2,1)S(1)}) custom-call(bf16[288,128]{1,0:T(8,128)(2,1)S(1)} %get-tuple-element.47.refs_3_.refs_1_.refs_0_.refs_8_, s16[272,128]{1,0:T(8,128)(2,1)S(1)} %get-tuple-element.64.refs_1_, ...), custom_call_target="tpu_custom_call" | custom-call | bytes 6000000 | tf_op jit(solution)/shard_map/third/pallas_call | solution.py:104
  29.8 2.1 %collective-permute-start.19 = (s16[272,128]{1,0:T(8,128)(2,1)S(1)}, s16[272,128]{1,0:T(8,128)(2,1)S(1)}, u32[]{:S(2)}, u32[]{:S(2)}) collective-permute-start(s16[272,128]{1,0:T(8,128)(2,1)S(1)} %get-tuple-element.71.refs_9_), channel_id=1, source_target_pairs={{0,2},{1,3},{2,0},{3,1},{4,6},{5,7},{6,4},{7,5},{8,10},{9,11},{10,... | collective-permute-start | bytes 208904 | tf_op jit(solution)/shard_map/ppermute | solution.py:557
  31.9 0.2 collective-permute-done.7.refs_2_
  32.0 1.7 %third.2 = (f32[8,32,128]{2,1,0:T(8,128)S(1)}, s16[272,128]{1,0:T(8,128)(2,1)S(1)}, f32[8,128]{1,0:T(8,128)S(1)}, bf16[272,128]{1,0:T(8,128)(2,1)S(1)}) custom-call(bf16[288,128]{1,0:T(8,128)(2,1)S(1)} %get-tuple-element.46.refs_2_.refs_0_, s16[272,128]{1,0:T(8,128)(2,1)S(1)} %get-tuple-element.59.refs_1_, ...), custom_call_target="tpu_custom_call" | custom-call | bytes 6000000 | tf_op jit(solution)/shard_map/third/pallas_call | solution.py:104
  33.8 0.1 collective-permute-start.18
  33.8 3.1 %collective-permute-start.12 = (bf16[272,128]{1,0:T(8,128)(2,1)S(1)}, bf16[272,128]{1,0:T(8,128)(2,1)S(1)}, u32[]{:S(2)}, u32[]{:S(2)}) collective-permute-start(bf16[272,128]{1,0:T(8,128)(2,1)S(1)} %get-tuple-element.66), channel_id=1, source_target_pairs={{4,0},{13,1},{6,2},{15,3},{8,4},{1,5},{10,6},{3,7},{12,8},{5,9},{1... | collective-permute-start | bytes 208904 | tf_op jit(solution)/shard_map/ppermute | solution.py:558
  37.0 0.8 %collective-permute-start.8 = (bf16[272,128]{1,0:T(8,128)(2,1)S(1)}, bf16[272,128]{1,0:T(8,128)(2,1)S(1)}, u32[]{:S(2)}, u32[]{:S(2)}) collective-permute-start(bf16[272,128]{1,0:T(8,128)(2,1)S(1)} %get-tuple-element.61), channel_id=1, source_target_pairs={{0,0},{9,1},{2,2},{11,3},{4,4},{13,5},{6,6},{15,7},{8,8},{1,9},{10... | collective-permute-start | bytes 208904 | tf_op jit(solution)/shard_map/ppermute | solution.py:558
  37.8 0.0 collective-permute-done.19.refs_10_
  37.8 0.3 collective-permute-done.18.refs_2_
  38.1 0.7 %table.1 = (f32[8,32,128]{2,1,0:T(8,128)S(1)}, f32[8,32,128]{2,1,0:T(8,128)S(1)}, f32[8,128]{1,0:T(8,128)S(1)}) custom-call(bf16[288,128]{1,0:T(8,128)(2,1)S(1)} %get-tuple-element.46.refs_2_.refs_0_, s16[272,128]{1,0:T(8,128)(2,1)S(1)} %get-tuple-element.67.refs_1_, s16[272,128]{1,0:T(8,128)(2,1)S(1)} %collective-permute-done.18.refs_2_, ...), custom_call_target="tpu_custom_call" | custom-call | bytes 3000000 | tf_op jit(solution)/shard_map/table/pallas_call | solution.py:104
  38.8 0.1 collective-permute-start.20
  38.9 0.5 collective-permute-start.16
  39.4 1.7 %collective-permute-start.13 = (bf16[272,128]{1,0:T(8,128)(2,1)S(1)}, bf16[272,128]{1,0:T(8,128)(2,1)S(1)}, u32[]{:S(2)}, u32[]{:S(2)}) collective-permute-start(bf16[272,128]{1,0:T(8,128)(2,1)S(1)} %collective-permute-done.12.refs_5_), channel_id=1, source_target_pairs={{0,2},{1,3},{2,0},{3,1},{4,6},{5,7},{6,4},{7,5},{8,10},{9,11},{10,... | collective-permute-start | bytes 208904 | tf_op jit(solution)/shard_map/ppermute | solution.py:559
  41.1 0.4 collective-permute-start.9
  41.5 0.7 %collective-permute-start.21 = (bf16[272,128]{1,0:T(8,128)(2,1)S(1)}, bf16[272,128]{1,0:T(8,128)(2,1)S(1)}, u32[]{:S(2)}, u32[]{:S(2)}) collective-permute-start(bf16[272,128]{1,0:T(8,128)(2,1)S(1)} %get-tuple-element.78), channel_id=1, source_target_pairs={{0,0},{9,1},{2,2},{11,3},{4,4},{13,5},{6,6},{15,7},{8,8},{1,9},{10... | collective-permute-start | bytes 208904 | tf_op jit(solution)/shard_map/ppermute | solution.py:570
  42.1 3.7 %collective-permute-start.22 = (bf16[272,128]{1,0:T(8,128)(2,1)S(1)}, bf16[272,128]{1,0:T(8,128)(2,1)S(1)}, u32[]{:S(2)}, u32[]{:S(2)}) collective-permute-start(bf16[272,128]{1,0:T(8,128)(2,1)S(1)} %get-tuple-element.79), channel_id=1, source_target_pairs={{4,0},{13,1},{6,2},{15,3},{8,4},{1,5},{10,6},{3,7},{12,8},{5,9},{1... | collective-permute-start | bytes 208904 | tf_op jit(solution)/shard_map/ppermute | solution.py:570
  45.9 1.4 %collective-permute-start.14 = (bf16[272,128]{1,0:T(8,128)(2,1)S(1)}, bf16[272,128]{1,0:T(8,128)(2,1)S(1)}, u32[]{:S(2)}, u32[]{:S(2)}) collective-permute-start(bf16[272,128]{1,0:T(8,128)(2,1)S(1)} %collective-permute-done.8.refs_3_), channel_id=1, source_target_pairs={{0,1},{1,0},{2,3},{3,2},{4,5},{5,4},{6,7},{7,6},{8,9},{9,8},{10,11... | collective-permute-start | bytes 208904 | tf_op jit(solution)/shard_map/ppermute | solution.py:504
  47.3 0.1 collective-permute-start.17
  47.4 0.4 collective-permute-start.15
  47.8 0.1 collective-permute-start.23
  47.9 1.6 %collective-permute-start.24 = (bf16[272,128]{1,0:T(8,128)(2,1)S(1)}, bf16[272,128]{1,0:T(8,128)(2,1)S(1)}, u32[]{:S(2)}, u32[]{:S(2)}) collective-permute-start(bf16[272,128]{1,0:T(8,128)(2,1)S(1)} %collective-permute-done.22.refs_12_), channel_id=1, source_target_pairs={{0,1},{1,0},{2,3},{3,2},{4,5},{5,4},{6,7},{7,6},{8,9},{9,8},{10,11... | collective-permute-start | bytes 208904 | tf_op jit(solution)/shard_map/ppermute | solution.py:504
  49.5 0.9 %collective-permute-done.24.refs_14_ = bf16[272,128]{1,0:T(8,128)(2,1)S(1)} collective-permute-done((bf16[272,128]{1,0:T(8,128)(2,1)S(1)}, bf16[272,128]{1,0:T(8,128)(2,1)S(1)}, u32[]{:S(2)}, u32[]{:S(2)}) %collective-permute-start.24) | collective-permute-done | bytes 69664 | tf_op jit(solution)/shard_map/ppermute | solution.py:504
  50.4 1.8 %finish.1 = (f32[32,4096]{1,0:T(8,128)}, f32[3,3]{1,0:T(4,128)}) custom-call(bf16[256,256]{1,0:T(8,128)(2,1)S(1)} %get-tuple-element.41.refs_0_, f32[8,128]{1,0:T(8,128)S(1)} %get-tuple-element.52.refs_1_, bf16[1024,128]{1,0:T(8,128)(2,1)S(1)} %get-tuple-element.53.refs_2_, bf16[272,128]{1,0:T(8,128)(2,1)S(1)} %collective-permute-done.8.refs_3_, ...), custom_call_target="tpu_custom_call" | custom-call | bytes 6000000 | tf_op jit(solution)/shard_map/finish/pallas_call | solution.py:104
  (22 shorter events, 0.1 us)
Async XLA Ops:
  1.3 1.0 %copy-start.2 = (bf16[32,4096]{1,0:T(8,128)(2,1)S(1)}, bf16[32,4096]{1,0:T(8,128)(2,1)}, u32[]{:S(2)}) copy-start(bf16[32,4096]{1,0:T(8,128)(2,1)} %start_ref.1) | copy-start | bytes 786436
  2.3 5.5 %copy-start = (bf16[32,7,4096]{2,0,1:T(8,128)(2,1)S(1)}, bf16[32,7,4096]{2,0,1:T(8,128)(2,1)}, u32[]{:S(2)}) copy-start(bf16[32,7,4096]{2,0,1:T(8,128)(2,1)} %param.9) | copy-start | bytes 5505028
  4.1 8.4 %collective-permute-start = (bf16[288,128]{1,0:T(8,128)(2,1)S(1)}, bf16[288,128]{1,0:T(8,128)(2,1)S(1)}, u32[]{:S(2)}, u32[]{:S(2)}) collective-permute-start(bf16[288,128]{1,0:T(8,128)(2,1)S(1)} %get-tuple-element.42), channel_id=1, source_target_pairs={{0,0},{1,9},{2,2},{3,11},{4,4},{5,13},{6,6},{7,15},{8,8},{9,1},{10... | collective-permute-start | bytes 221192 | tf_op jit(solution)/shard_map/ppermute | solution.py:520
  4.7 8.1 %collective-permute-start.1 = (bf16[288,128]{1,0:T(8,128)(2,1)S(1)}, bf16[288,128]{1,0:T(8,128)(2,1)S(1)}, u32[]{:S(2)}, u32[]{:S(2)}) collective-permute-start(bf16[288,128]{1,0:T(8,128)(2,1)S(1)} %get-tuple-element.43), channel_id=1, source_target_pairs={{0,4},{1,13},{2,6},{3,15},{4,8},{5,1},{6,10},{7,3},{8,12},{9,5},{1... | collective-permute-start | bytes 221192 | tf_op jit(solution)/shard_map/ppermute | solution.py:520
  7.8 5.0 %copy-start.1 = (bf16[32,7,4096]{2,0,1:T(8,128)(2,1)S(1)}, bf16[32,7,4096]{2,0,1:T(8,128)(2,1)}, u32[]{:S(2)}) copy-start(bf16[32,7,4096]{2,0,1:T(8,128)(2,1)} %param.10) | copy-start | bytes 5505028
  9.5 5.6 %collective-permute-start.2 = (bf16[8,64,512]{2,1,0:T(8,128)(2,1)S(1)}, bf16[8,64,512]{2,1,0:T(8,128)(2,1)S(1)}, u32[]{:S(2)}, u32[]{:S(2)}) collective-permute-start(bf16[8,64,512]{2,1,0:T(8,128)(2,1)S(1)} %get-tuple-element.50), channel_id=1, source_target_pairs={{0,1},{1,0},{2,3},{3,2},{4,5},{5,4},{6,7},{7,6},{8,9},{9,8},{10,11... | collective-permute-start | bytes 1572872 | tf_op jit(solution)/shard_map/ppermute | solution.py:504
  14.2 2.0 %collective-permute-start.3 = (bf16[8,64,512]{2,1,0:T(8,128)(2,1)S(1)}, bf16[8,64,512]{2,1,0:T(8,128)(2,1)S(1)}, u32[]{:S(2)}, u32[]{:S(2)}) collective-permute-start(bf16[8,64,512]{2,1,0:T(8,128)(2,1)S(1)} %get-tuple-element.51), channel_id=1, source_target_pairs={{0,1},{1,0},{2,3},{3,2},{4,5},{5,4},{6,7},{7,6},{8,9},{9,8},{10,11... | collective-permute-start | bytes 1572872 | tf_op jit(solution)/shard_map/ppermute | solution.py:504
  14.6 4.7 %collective-permute-start.4 = (bf16[8,64,512]{2,1,0:T(8,128)(2,1)S(1)}, bf16[8,64,512]{2,1,0:T(8,128)(2,1)S(1)}, u32[]{:S(2)}, u32[]{:S(2)}) collective-permute-start(bf16[8,64,512]{2,1,0:T(8,128)(2,1)S(1)} %get-tuple-element.55), channel_id=1, source_target_pairs={{0,1},{1,0},{2,3},{3,2},{4,5},{5,4},{6,7},{7,6},{8,9},{9,8},{10,11... | collective-permute-start | bytes 1572872 | tf_op jit(solution)/shard_map/ppermute | solution.py:504
  14.8 4.5 %collective-permute-start.5 = (bf16[8,64,512]{2,1,0:T(8,128)(2,1)S(1)}, bf16[8,64,512]{2,1,0:T(8,128)(2,1)S(1)}, u32[]{:S(2)}, u32[]{:S(2)}) collective-permute-start(bf16[8,64,512]{2,1,0:T(8,128)(2,1)S(1)} %get-tuple-element.56), channel_id=1, source_target_pairs={{0,1},{1,0},{2,3},{3,2},{4,5},{5,4},{6,7},{7,6},{8,9},{9,8},{10,11... | collective-permute-start | bytes 1572872 | tf_op jit(solution)/shard_map/ppermute | solution.py:504
  17.5 4.5 %collective-permute-start.10 = (s16[272,128]{1,0:T(8,128)(2,1)S(1)}, s16[272,128]{1,0:T(8,128)(2,1)S(1)}, u32[]{:S(2)}, u32[]{:S(2)}) collective-permute-start(s16[272,128]{1,0:T(8,128)(2,1)S(1)} %get-tuple-element.62.refs_1_), channel_id=1, source_target_pairs={{0,2},{1,3},{2,0},{3,1},{4,6},{5,7},{6,4},{7,5},{8,10},{9,11},{10,... | collective-permute-start | bytes 208904 | tf_op jit(solution)/shard_map/ppermute | solution.py:546
  20.6 4.7 %collective-permute-start.6 = (s16[272,128]{1,0:T(8,128)(2,1)S(1)}, s16[272,128]{1,0:T(8,128)(2,1)S(1)}, u32[]{:S(2)}, u32[]{:S(2)}) collective-permute-start(s16[272,128]{1,0:T(8,128)(2,1)S(1)} %get-tuple-element.57.refs_1_), channel_id=1, source_target_pairs={{0,2},{1,3},{2,0},{3,1},{4,6},{5,7},{6,4},{7,5},{8,10},{9,11},{10,... | collective-permute-start | bytes 208904 | tf_op jit(solution)/shard_map/ppermute | solution.py:546
  23.7 4.4 %collective-permute-start.11 = (s16[272,128]{1,0:T(8,128)(2,1)S(1)}, s16[272,128]{1,0:T(8,128)(2,1)S(1)}, u32[]{:S(2)}, u32[]{:S(2)}) collective-permute-start(s16[272,128]{1,0:T(8,128)(2,1)S(1)} %get-tuple-element.64.refs_1_), channel_id=1, source_target_pairs={{0,2},{1,3},{2,0},{3,1},{4,6},{5,7},{6,4},{7,5},{8,10},{9,11},{10,... | collective-permute-start | bytes 208904 | tf_op jit(solution)/shard_map/ppermute | solution.py:557
  27.1 5.0 %collective-permute-start.7 = (s16[272,128]{1,0:T(8,128)(2,1)S(1)}, s16[272,128]{1,0:T(8,128)(2,1)S(1)}, u32[]{:S(2)}, u32[]{:S(2)}) collective-permute-start(s16[272,128]{1,0:T(8,128)(2,1)S(1)} %get-tuple-element.59.refs_1_), channel_id=1, source_target_pairs={{0,2},{1,3},{2,0},{3,1},{4,6},{5,7},{6,4},{7,5},{8,10},{9,11},{10,... | collective-permute-start | bytes 208904 | tf_op jit(solution)/shard_map/ppermute | solution.py:557
  29.8 8.0 %collective-permute-start.19 = (s16[272,128]{1,0:T(8,128)(2,1)S(1)}, s16[272,128]{1,0:T(8,128)(2,1)S(1)}, u32[]{:S(2)}, u32[]{:S(2)}) collective-permute-start(s16[272,128]{1,0:T(8,128)(2,1)S(1)} %get-tuple-element.71.refs_9_), channel_id=1, source_target_pairs={{0,2},{1,3},{2,0},{3,1},{4,6},{5,7},{6,4},{7,5},{8,10},{9,11},{10,... | collective-permute-start | bytes 208904 | tf_op jit(solution)/shard_map/ppermute | solution.py:557
  33.8 4.4 %collective-permute-start.18 = (s16[272,128]{1,0:T(8,128)(2,1)S(1)}, s16[272,128]{1,0:T(8,128)(2,1)S(1)}, u32[]{:S(2)}, u32[]{:S(2)}) collective-permute-start(s16[272,128]{1,0:T(8,128)(2,1)S(1)} %get-tuple-element.67.refs_1_), channel_id=1, source_target_pairs={{0,2},{1,3},{2,0},{3,1},{4,6},{5,7},{6,4},{7,5},{8,10},{9,11},{10,... | collective-permute-start | bytes 208904 | tf_op jit(solution)/shard_map/ppermute | solution.py:557
  33.8 5.1 %collective-permute-start.12 = (bf16[272,128]{1,0:T(8,128)(2,1)S(1)}, bf16[272,128]{1,0:T(8,128)(2,1)S(1)}, u32[]{:S(2)}, u32[]{:S(2)}) collective-permute-start(bf16[272,128]{1,0:T(8,128)(2,1)S(1)} %get-tuple-element.66), channel_id=1, source_target_pairs={{4,0},{13,1},{6,2},{15,3},{8,4},{1,5},{10,6},{3,7},{12,8},{5,9},{1... | collective-permute-start | bytes 208904 | tf_op jit(solution)/shard_map/ppermute | solution.py:558
  37.0 4.1 %collective-permute-start.8 = (bf16[272,128]{1,0:T(8,128)(2,1)S(1)}, bf16[272,128]{1,0:T(8,128)(2,1)S(1)}, u32[]{:S(2)}, u32[]{:S(2)}) collective-permute-start(bf16[272,128]{1,0:T(8,128)(2,1)S(1)} %get-tuple-element.61), channel_id=1, source_target_pairs={{0,0},{9,1},{2,2},{11,3},{4,4},{13,5},{6,6},{15,7},{8,8},{1,9},{10... | collective-permute-start | bytes 208904 | tf_op jit(solution)/shard_map/ppermute | solution.py:558
  38.8 2.6 %collective-permute-start.20 = (f32[8,128]{1,0:T(8,128)S(1)}, f32[8,128]{1,0:T(8,128)S(1)}, u32[]{:S(2)}, u32[]{:S(2)}) collective-permute-start(f32[8,128]{1,0:T(8,128)S(1)} %get-tuple-element.75.table_ref), channel_id=1, source_target_pairs={{0,1},{1,0},{2,3},{3,2},{4,5},{5,4},{6,7},{7,6},{8,9},{9,8},{10,11... | collective-permute-start | bytes 12296 | tf_op jit(solution)/shard_map/ppermute | solution.py:504
  38.9 6.9 %collective-permute-start.16 = (bf16[272,128]{1,0:T(8,128)(2,1)S(1)}, bf16[272,128]{1,0:T(8,128)(2,1)S(1)}, u32[]{:S(2)}, u32[]{:S(2)}) collective-permute-start(bf16[272,128]{1,0:T(8,128)(2,1)S(1)} %collective-permute-done.12.refs_5_), channel_id=1, source_target_pairs={{0,1},{1,0},{2,3},{3,2},{4,5},{5,4},{6,7},{7,6},{8,9},{9,8},{10,11... | collective-permute-start | bytes 208904 | tf_op jit(solution)/shard_map/ppermute | solution.py:504
  39.4 7.9 %collective-permute-start.13 = (bf16[272,128]{1,0:T(8,128)(2,1)S(1)}, bf16[272,128]{1,0:T(8,128)(2,1)S(1)}, u32[]{:S(2)}, u32[]{:S(2)}) collective-permute-start(bf16[272,128]{1,0:T(8,128)(2,1)S(1)} %collective-permute-done.12.refs_5_), channel_id=1, source_target_pairs={{0,2},{1,3},{2,0},{3,1},{4,6},{5,7},{6,4},{7,5},{8,10},{9,11},{10,... | collective-permute-start | bytes 208904 | tf_op jit(solution)/shard_map/ppermute | solution.py:559
  41.1 6.3 %collective-permute-start.9 = (bf16[272,128]{1,0:T(8,128)(2,1)S(1)}, bf16[272,128]{1,0:T(8,128)(2,1)S(1)}, u32[]{:S(2)}, u32[]{:S(2)}) collective-permute-start(bf16[272,128]{1,0:T(8,128)(2,1)S(1)} %collective-permute-done.8.refs_3_), channel_id=1, source_target_pairs={{0,2},{1,3},{2,0},{3,1},{4,6},{5,7},{6,4},{7,5},{8,10},{9,11},{10,... | collective-permute-start | bytes 208904 | tf_op jit(solution)/shard_map/ppermute | solution.py:559
  41.5 6.3 %collective-permute-start.21 = (bf16[272,128]{1,0:T(8,128)(2,1)S(1)}, bf16[272,128]{1,0:T(8,128)(2,1)S(1)}, u32[]{:S(2)}, u32[]{:S(2)}) collective-permute-start(bf16[272,128]{1,0:T(8,128)(2,1)S(1)} %get-tuple-element.78), channel_id=1, source_target_pairs={{0,0},{9,1},{2,2},{11,3},{4,4},{13,5},{6,6},{15,7},{8,8},{1,9},{10... | collective-permute-start | bytes 208904 | tf_op jit(solution)/shard_map/ppermute | solution.py:570
  42.1 5.7 %collective-permute-start.22 = (bf16[272,128]{1,0:T(8,128)(2,1)S(1)}, bf16[272,128]{1,0:T(8,128)(2,1)S(1)}, u32[]{:S(2)}, u32[]{:S(2)}) collective-permute-start(bf16[272,128]{1,0:T(8,128)(2,1)S(1)} %get-tuple-element.79), channel_id=1, source_target_pairs={{4,0},{13,1},{6,2},{15,3},{8,4},{1,5},{10,6},{3,7},{12,8},{5,9},{1... | collective-permute-start | bytes 208904 | tf_op jit(solution)/shard_map/ppermute | solution.py:570
  45.9 3.6 %collective-permute-start.14 = (bf16[272,128]{1,0:T(8,128)(2,1)S(1)}, bf16[272,128]{1,0:T(8,128)(2,1)S(1)}, u32[]{:S(2)}, u32[]{:S(2)}) collective-permute-start(bf16[272,128]{1,0:T(8,128)(2,1)S(1)} %collective-permute-done.8.refs_3_), channel_id=1, source_target_pairs={{0,1},{1,0},{2,3},{3,2},{4,5},{5,4},{6,7},{7,6},{8,9},{9,8},{10,11... | collective-permute-start | bytes 208904 | tf_op jit(solution)/shard_map/ppermute | solution.py:504
  47.3 2.2 %collective-permute-start.17 = (bf16[272,128]{1,0:T(8,128)(2,1)S(1)}, bf16[272,128]{1,0:T(8,128)(2,1)S(1)}, u32[]{:S(2)}, u32[]{:S(2)}) collective-permute-start(bf16[272,128]{1,0:T(8,128)(2,1)S(1)} %collective-permute-done.13.refs_6_), channel_id=1, source_target_pairs={{0,1},{1,0},{2,3},{3,2},{4,5},{5,4},{6,7},{7,6},{8,9},{9,8},{10,11... | collective-permute-start | bytes 208904 | tf_op jit(solution)/shard_map/ppermute | solution.py:504
  47.4 2.1 %collective-permute-start.15 = (bf16[272,128]{1,0:T(8,128)(2,1)S(1)}, bf16[272,128]{1,0:T(8,128)(2,1)S(1)}, u32[]{:S(2)}, u32[]{:S(2)}) collective-permute-start(bf16[272,128]{1,0:T(8,128)(2,1)S(1)} %collective-permute-done.9.refs_4_), channel_id=1, source_target_pairs={{0,1},{1,0},{2,3},{3,2},{4,5},{5,4},{6,7},{7,6},{8,9},{9,8},{10,11... | collective-permute-start | bytes 208904 | tf_op jit(solution)/shard_map/ppermute | solution.py:504
  47.8 1.7 %collective-permute-start.23 = (bf16[272,128]{1,0:T(8,128)(2,1)S(1)}, bf16[272,128]{1,0:T(8,128)(2,1)S(1)}, u32[]{:S(2)}, u32[]{:S(2)}) collective-permute-start(bf16[272,128]{1,0:T(8,128)(2,1)S(1)} %collective-permute-done.21.refs_11_), channel_id=1, source_target_pairs={{0,1},{1,0},{2,3},{3,2},{4,5},{5,4},{6,7},{7,6},{8,9},{9,8},{10,11... | collective-permute-start | bytes 208904 | tf_op jit(solution)/shard_map/ppermute | solution.py:504
  47.9 2.5 %collective-permute-start.24 = (bf16[272,128]{1,0:T(8,128)(2,1)S(1)}, bf16[272,128]{1,0:T(8,128)(2,1)S(1)}, u32[]{:S(2)}, u32[]{:S(2)}) collective-permute-start(bf16[272,128]{1,0:T(8,128)(2,1)S(1)} %collective-permute-done.22.refs_12_), channel_id=1, source_target_pairs={{0,1},{1,0},{2,3},{3,2},{4,5},{5,4},{6,7},{7,6},{8,9},{9,8},{10,11... | collective-permute-start | bytes 208904 | tf_op jit(solution)/shard_map/ppermute | solution.py:504

commit v7 on v6

--- a/solution.py
+++ b/solution.py
@@ -57,6 +57,16 @@
         jnp.where(same & (slot == order_ref[base + k]), 1.0, 0.0) for k in range(count)
     ]
     return jnp.concatenate(parts, axis=0).astype(BF16)
+
+
+def spread(first, lines):
+    rows = []
+    for line in lines:
+        row = jnp.concatenate([line.astype(F32)] * 8, axis=1)
+        rows.append(jnp.broadcast_to(row, (LANES, row.shape[1])))
+    return lax.dot_general(
+        first, jnp.concatenate(rows, axis=0).astype(BF16), (((1,), (1,)), ((), ())),
+        preferred_element_type=F32)
 
 
 def slots_last(order_ref, slots):
@@ -159,13 +169,8 @@
     first = first_ref[...]
     second = pair_to_kept()
     if masked:
-        rows = []
-        for w in range(8):
-            row = meta_ref[3 + w : 4 + w, :].astype(F32) if w < chans else jnp.zeros((1, slots), F32)
-            rows.append(jnp.broadcast_to(jnp.concatenate([row] * 8, axis=1), (LANES, 8 * slots)))
-        mask = lax.dot_general(
-            first, jnp.concatenate(rows, axis=0).astype(BF16), (((1,), (1,)), ((), ())),
-            preferred_element_type=F32)
+        lines = [meta_ref[3 + w : 4 + w, :] for w in range(chans)]
+        mask = spread(first, lines + [jnp.zeros_like(lines[0])] * (8 - chans))
     blank = jnp.zeros((slots, LANES), BF16)
     for g in range(4):
         used = [w for w in (2 * g, 2 * g + 1) if w < chans]
@@ -191,7 +196,7 @@
                 ]
 
 
-def ship_kernel(meta_ref, start_ref, first_ref, last_ref, near_ref, far_ref, home_ref, order_ref, seen):
+def ship_kernel(meta_ref, table_ref, start_ref, first_ref, last_ref, near_ref, far_ref, home_ref, order_ref, seen):
     sort_slots(position()[1], meta_ref, order_ref, seen)
     slots = start_ref.shape[0]
     cap = slots // 4
@@ -199,23 +204,27 @@
     first_ref[...] = first
     last_ref[...] = slots_last(order_ref, slots)
     second = to_kept()
+    bounds = spread(first, [table_ref[1 + d : 2 + d, :] for d in range(2)])
+    tall, broad = bounds[:, :LANES], bounds[:, LANES:]
+    lane, step = iota(tall.shape, 1), iota(tall.shape, 0) % 8
+    kept = lane % B
+    a = (2 * step + lane // B).astype(F32)
+    columns = jnp.where((2 * (kept % HALF) + kept // HALF).astype(F32) < broad, 1.0, 0.0)
     chunks = []
+    squares = None
     for c in range(4):
         rows = [start_ref[:, i * LANES : (i + 1) * LANES] for i in range(8 * c, 8 * c + 8)]
         x = jnp.dot(first, jnp.concatenate(rows, axis=0), preferred_element_type=F32).astype(BF16)
-        chunks.append(jnp.dot(x, second, preferred_element_type=F32))
-    halves = []
+        x = jnp.dot(x, second, preferred_element_type=F32) * jnp.where(a + 16 * c < tall, columns, 0.0)
+        chunks.append(x)
+        squares = x * x if squares is None else squares + x * x
     for k in range(slots):
-        slot = order_ref[k]
-        x = jnp.concatenate([chunk[8 * k : 8 * k + 8] for chunk in chunks], axis=0)
-        x = x * inside(meta_ref[1, slot].astype(F32), meta_ref[2, slot].astype(F32))
-        home_ref[HALF * k : HALF * (k + 1), :] = x.astype(BF16)
+        x = jnp.concatenate([chunk[8 * k : 8 * k + 8] for chunk in chunks], axis=0).astype(BF16)
+        home_ref[HALF * k : HALF * (k + 1), :] = x
         if k < 2 * cap:
-            (near_ref, far_ref)[k // cap][HALF * (k % cap) : HALF * (k % cap + 1), :] = x.astype(BF16)
-        if k % (2 * cap) == 0:
-            halves.append(x * x)
-        else:
-            halves[-1] = halves[-1] + x * x
+            (near_ref, far_ref)[k // cap][HALF * (k % cap) : HALF * (k % cap + 1), :] = x
+    half = squares.shape[0] // 2
+    halves = [squares[:half], squares[half:]]
     squares = wide(total_of(halves[0]) + total_of(halves[1]))
     pieces = [v.astype(F32) for v in split_three(squares)]
     blank = jnp.zeros((2 * 16 - 2 * cap - 3, LANES), F32)
@@ -223,7 +232,8 @@
         lines = []
         for d in range(2):
             for k in range(cap):
-                lines.append(jnp.full((1, LANES), meta_ref[1 + d, order_ref[t * cap + k]].astype(F32)))
+                at = 8 * (t * cap + k)
+                lines.append((tall, broad)[d][at : at + 1])
         ref[HALF * cap :, :] = jnp.concatenate(lines + pieces + [blank], axis=0).astype(BF16)
 
 
@@ -515,7 +525,7 @@
     first, back, *ships, home = call(
         ship_kernel, "ship",
         (one_hots, one_hots, payload, payload, shape((slots * HALF, LANES), BF16)),
-        (meta, start_vector), "sv",
+        (meta, meta, start_vector), "svv",
         [pltpu.SMEM((slots,), jnp.int32), pltpu.SMEM((nodes,), jnp.int32)], "vvvvv", 2.0, ROOMY, True)
     ships = [lax.ppermute(x, ("sector", "op"), route(t, False)) for t, x in enumerate(ships)]
 

time: 52.3 us -> 52.3 us (level)
  no operation moved by 1% of the time
where the time goes in v7:
time: 52.3 us; the launch traced here: 52.1 us
  starting transfers between devices  28.6 us (55%)
  Pallas kernels  16.7 us (32%)
  waiting for transfers between devices  4.34 us (8%)
  local copies, waits for them, and re-layouts  0.95 us (2%)
  between operations  0.8 us (2%)
  other arithmetic  0.71 us (1%)
    pallas_call x13, Pallas kernels, call(): pl.pallas_call(kernel, out_shape=out_shape, in_specs=[pl.BlockSpec(memory...  16.7 us
    ppermute x11, starting transfers between devices, across(): return lax.ppermute(x, 'op', swap_core)  7.98 us
    ppermute x6, starting transfers between devices, paired(): images[t] = (y, lax.ppermute(y, 'op', swap_x))  6.48 us
    ppermute x2, starting transfers between devices, paired(): lax.ppermute(x, ('sector', 'op'), route(t, True))  4.37 us
    ppermute x2, starting transfers between devices, paired(): early += [lax.ppermute(x, ('sector', 'op'), route(t, True)) for x in parcel]  3.96 us
    ppermute x2, starting transfers between devices, paired(): lax.ppermute(x, ('sector', 'op'), route(t, False))  3.77 us
    ppermute x2, starting transfers between devices, paired(): early = [(x, lax.ppermute(x, 'op', swap_x)) for x in early]  2.03 us
    ppermute x6, waiting for transfers between devices, paired(): images[t] = (y, lax.ppermute(y, 'op', swap_x))  1.99 us
  transfers between devices with their start and end apart: 25, of which 7 were waited for; matrix products, arithmetic and copies ran while one was open for 0% of the time, Pallas kernels for 25%

profile of v7, /device:TPU:0, one launch (start us, length us, event | category | flops | bytes accessed | tf_op | source)
XLA Modules:
  0.0 52.1 jit_solution(15881109799793241062)
XLA Ops:
  0.6 0.7 %pad_add_fusion.meta_ref.table_ref.refs_2_ = s32[10,32]{1,0:T(8,128)S(1)} fusion(s32[7,32]{1,0:T(8,128)} %bitcast.7, s32[2,32]{1,0:T(2,128)} %bitcast.8, s32[1,32]{1,0:T(1,128)} %bitcast.9), kind=kLoop, calls=%fused_computation | loop fusion | flops 640 | bytes 2560 | tf_op jit(solution)/shard_map/concatenate | solution.py:502
  1.4 0.9 %copy-done.2 = bf16[32,4096]{1,0:T(8,128)(2,1)S(1)} copy-done((bf16[32,4096]{1,0:T(8,128)(2,1)S(1)}, bf16[32,4096]{1,0:T(8,128)(2,1)}, u32[]{:S(2)}) %copy-start.2) | copy-done | bytes 262168
  2.3 1.7 %ship.1 = (bf16[256,256]{1,0:T(8,128)(2,1)S(1)}, bf16[256,256]{1,0:T(8,128)(2,1)S(1)}, bf16[288,128]{1,0:T(8,128)(2,1)S(1)}, bf16[288,128]{1,0:T(8,128)(2,1)S(1)}, bf16[1024,128]{1,0:T(8,128)(2,1)S(1)}) custom-call(s32[10,32]{1,0:T(8,128)S(1)} %pad_add_fusion.meta_ref.table_ref.refs_2_, s32[10,32]{1,0:T(8,128)S(1)} %pad_add_fusion.meta_ref.table_ref.refs_2_, ...), custom_call_target="tpu_custom_call" | custom-call | flops 2000000000 | bytes 1024 | tf_op jit(solution)/shard_map/ship/pallas_call | solution.py:114
  4.0 0.7 %collective-permute-start = (bf16[288,128]{1,0:T(8,128)(2,1)S(1)}, bf16[288,128]{1,0:T(8,128)(2,1)S(1)}, u32[]{:S(2)}, u32[]{:S(2)}) collective-permute-start(bf16[288,128]{1,0:T(8,128)(2,1)S(1)} %get-tuple-element.42), channel_id=1, source_target_pairs={{0,0},{1,9},{2,2},{3,11},{4,4},{5,13},{6,6},{7,15},{8,8},{9,1},{10... | collective-permute-start | bytes 221192 | tf_op jit(solution)/shard_map/ppermute | solution.py:530
  4.7 3.1 %collective-permute-start.1 = (bf16[288,128]{1,0:T(8,128)(2,1)S(1)}, bf16[288,128]{1,0:T(8,128)(2,1)S(1)}, u32[]{:S(2)}, u32[]{:S(2)}) collective-permute-start(bf16[288,128]{1,0:T(8,128)(2,1)S(1)} %get-tuple-element.43), channel_id=1, source_target_pairs={{0,4},{1,13},{2,6},{3,15},{4,8},{5,1},{6,10},{7,3},{8,12},{9,5},{1... | collective-permute-start | bytes 221192 | tf_op jit(solution)/shard_map/ppermute | solution.py:530
  7.8 1.7 %arrange.2 = (bf16[8,64,512]{2,1,0:T(8,128)(2,1)S(1)}, bf16[8,64,512]{2,1,0:T(8,128)(2,1)S(1)}, bf16[8,64,512]{2,1,0:T(8,128)(2,1)S(1)}, bf16[8,64,512]{2,1,0:T(8,128)(2,1)S(1)}) custom-call(bf16[256,256]{1,0:T(8,128)(2,1)S(1)} %get-tuple-element.44.refs_0_, bf16[7,32,4096]{2,1,0:T(8,128)(2,1)S(1)} %bitcast.5, ...), custom_call_target="tpu_custom_call" | custom-call | flops 3000000000 | bytes 1024 | tf_op jit(solution)/shard_map/arrange/pallas_call | solution.py:114
  9.5 2.9 %collective-permute-start.2 = (bf16[8,64,512]{2,1,0:T(8,128)(2,1)S(1)}, bf16[8,64,512]{2,1,0:T(8,128)(2,1)S(1)}, u32[]{:S(2)}, u32[]{:S(2)}) collective-permute-start(bf16[8,64,512]{2,1,0:T(8,128)(2,1)S(1)} %get-tuple-element.50), channel_id=1, source_target_pairs={{0,1},{1,0},{2,3},{3,2},{4,5},{5,4},{6,7},{7,6},{8,9},{9,8},{10,11... | collective-permute-start | bytes 1572872 | tf_op jit(solution)/shard_map/ppermute | solution.py:514
  12.4 0.0 collective-permute-done.near_in_ref
  12.5 0.3 collective-permute-done.1.far_in_ref
  12.8 1.4 %arrange.3 = (bf16[8,64,512]{2,1,0:T(8,128)(2,1)S(1)}, bf16[8,64,512]{2,1,0:T(8,128)(2,1)S(1)}, bf16[8,64,512]{2,1,0:T(8,128)(2,1)S(1)}, bf16[8,64,512]{2,1,0:T(8,128)(2,1)S(1)}) custom-call(bf16[256,256]{1,0:T(8,128)(2,1)S(1)} %get-tuple-element.44.refs_0_, bf16[7,32,4096]{2,1,0:T(8,128)(2,1)S(1)} %bitcast.6, ...), custom_call_target="tpu_custom_call" | custom-call | flops 3000000000 | bytes 1024 | tf_op jit(solution)/shard_map/arrange/pallas_call | solution.py:114
  14.2 0.4 collective-permute-start.3
  14.6 0.2 collective-permute-start.4
  14.8 0.3 collective-permute-start.5
  15.1 0.0 collective-permute-done.2.refs_4_.refs_6_.refs_7_
  15.1 1.1 %collective-permute-done.3.refs_5_.refs_7_.refs_8_ = bf16[8,64,512]{2,1,0:T(8,128)(2,1)S(1)} collective-permute-done((bf16[8,64,512]{2,1,0:T(8,128)(2,1)S(1)}, bf16[8,64,512]{2,1,0:T(8,128)(2,1)S(1)}, u32[]{:S(2)}, u32[]{:S(2)}) %collective-permute-start.3) | collective-permute-done | bytes 524320 | tf_op jit(solution)/shard_map/ppermute | solution.py:514
  16.2 1.3 %first.2 = (f32[8,32,128]{2,1,0:T(8,128)S(1)}, s16[272,128]{1,0:T(8,128)(2,1)S(1)}, f32[8,128]{1,0:T(8,128)S(1)}) custom-call(bf16[288,128]{1,0:T(8,128)(2,1)S(1)} %get-tuple-element.46.refs_2_.refs_0_, bf16[288,128]{1,0:T(8,128)(2,1)S(1)} %get-tuple-element.47.refs_3_.refs_1_.refs_0_.refs_8_, ...), custom_call_target="tpu_custom_call" | custom-call | bytes 6000000 | tf_op jit(solution)/shard_map/first/pallas_call | solution.py:114
  17.5 1.8 %collective-permute-start.10 = (s16[272,128]{1,0:T(8,128)(2,1)S(1)}, s16[272,128]{1,0:T(8,128)(2,1)S(1)}, u32[]{:S(2)}, u32[]{:S(2)}) collective-permute-start(s16[272,128]{1,0:T(8,128)(2,1)S(1)} %get-tuple-element.62.refs_1_), channel_id=1, source_target_pairs={{0,2},{1,3},{2,0},{3,1},{4,6},{5,7},{6,4},{7,5},{8,10},{9,11},{10,... | collective-permute-start | bytes 208904 | tf_op jit(solution)/shard_map/ppermute | solution.py:556
  19.3 1.3 %first.3 = (f32[8,32,128]{2,1,0:T(8,128)S(1)}, s16[272,128]{1,0:T(8,128)(2,1)S(1)}, f32[8,128]{1,0:T(8,128)}) custom-call(bf16[288,128]{1,0:T(8,128)(2,1)S(1)} %get-tuple-element.46.refs_2_.refs_0_, bf16[288,128]{1,0:T(8,128)(2,1)S(1)} %get-tuple-element.47.refs_3_.refs_1_.refs_0_.refs_8_, ...), custom_call_target="tpu_custom_call" | custom-call | bytes 6000000 | tf_op jit(solution)/shard_map/first/pallas_call | solution.py:114
  20.6 0.4 collective-permute-start.6
  21.0 1.0 %collective-permute-done.10.refs_2_ = s16[272,128]{1,0:T(8,128)(2,1)S(1)} collective-permute-done((s16[272,128]{1,0:T(8,128)(2,1)S(1)}, s16[272,128]{1,0:T(8,128)(2,1)S(1)}, u32[]{:S(2)}, u32[]{:S(2)}) %collective-permute-start.10) | collective-permute-done | bytes 69664 | tf_op jit(solution)/shard_map/ppermute | solution.py:556
  22.0 1.7 %second.3 = (f32[8,32,128]{2,1,0:T(8,128)S(1)}, s16[272,128]{1,0:T(8,128)(2,1)S(1)}, f32[8,128]{1,0:T(8,128)S(1)}) custom-call(bf16[288,128]{1,0:T(8,128)(2,1)S(1)} %get-tuple-element.47.refs_3_.refs_1_.refs_0_.refs_8_, s16[272,128]{1,0:T(8,128)(2,1)S(1)} %get-tuple-element.62.refs_1_, s16[272,128]{1,0:T(8,128)(2,1)S(1)} %collective-permute-done.10.refs_2_, ...), custom_call_target="tpu_custom_call" | custom-call | bytes 6000000 | tf_op jit(solution)/shard_map/second/pallas_call | solution.py:114
  23.7 1.7 %collective-permute-start.11 = (s16[272,128]{1,0:T(8,128)(2,1)S(1)}, s16[272,128]{1,0:T(8,128)(2,1)S(1)}, u32[]{:S(2)}, u32[]{:S(2)}) collective-permute-start(s16[272,128]{1,0:T(8,128)(2,1)S(1)} %get-tuple-element.64.refs_1_), channel_id=1, source_target_pairs={{0,2},{1,3},{2,0},{3,1},{4,6},{5,7},{6,4},{7,5},{8,10},{9,11},{10,... | collective-permute-start | bytes 208904 | tf_op jit(solution)/shard_map/ppermute | solution.py:567
  25.4 0.0 collective-permute-done.6.refs_2_
  25.4 1.7 %second.2 = (f32[8,32,128]{2,1,0:T(8,128)S(1)}, s16[272,128]{1,0:T(8,128)(2,1)S(1)}, f32[8,128]{1,0:T(8,128)S(1)}) custom-call(bf16[288,128]{1,0:T(8,128)(2,1)S(1)} %get-tuple-element.46.refs_2_.refs_0_, s16[272,128]{1,0:T(8,128)(2,1)S(1)} %get-tuple-element.57.refs_1_, s16[272,128]{1,0:T(8,128)(2,1)S(1)} %collective-permute-done.6.refs_2_, ...), custom_call_target="tpu_custom_call" | custom-call | bytes 6000000 | tf_op jit(solution)/shard_map/second/pallas_call | solution.py:114
  27.1 0.5 collective-permute-start.7
  27.5 0.5 collective-permute-done.11.refs_2_
  28.1 1.7 %third.3 = (f32[8,32,128]{2,1,0:T(8,128)S(1)}, s16[272,128]{1,0:T(8,128)(2,1)S(1)}, f32[8,128]{1,0:T(8,128)S(1)}, bf16[272,128]{1,0:T(8,128)(2,1)S(1)}) custom-call(bf16[288,128]{1,0:T(8,128)(2,1)S(1)} %get-tuple-element.47.refs_3_.refs_1_.refs_0_.refs_8_, s16[272,128]{1,0:T(8,128)(2,1)S(1)} %get-tuple-element.64.refs_1_, ...), custom_call_target="tpu_custom_call" | custom-call | bytes 6000000 | tf_op jit(solution)/shard_map/third/pallas_call | solution.py:114
  29.8 2.1 %collective-permute-start.19 = (s16[272,128]{1,0:T(8,128)(2,1)S(1)}, s16[272,128]{1,0:T(8,128)(2,1)S(1)}, u32[]{:S(2)}, u32[]{:S(2)}) collective-permute-start(s16[272,128]{1,0:T(8,128)(2,1)S(1)} %get-tuple-element.71.refs_9_), channel_id=1, source_target_pairs={{0,2},{1,3},{2,0},{3,1},{4,6},{5,7},{6,4},{7,5},{8,10},{9,11},{10,... | collective-permute-start | bytes 208904 | tf_op jit(solution)/shard_map/ppermute | solution.py:567
  31.9 0.2 collective-permute-done.7.refs_2_
  32.0 1.7 %third.2 = (f32[8,32,128]{2,1,0:T(8,128)S(1)}, s16[272,128]{1,0:T(8,128)(2,1)S(1)}, f32[8,128]{1,0:T(8,128)S(1)}, bf16[272,128]{1,0:T(8,128)(2,1)S(1)}) custom-call(bf16[288,128]{1,0:T(8,128)(2,1)S(1)} %get-tuple-element.46.refs_2_.refs_0_, s16[272,128]{1,0:T(8,128)(2,1)S(1)} %get-tuple-element.59.refs_1_, ...), custom_call_target="tpu_custom_call" | custom-call | bytes 6000000 | tf_op jit(solution)/shard_map/third/pallas_call | solution.py:114
  33.8 0.1 collective-permute-start.18
  33.8 3.1 %collective-permute-start.12 = (bf16[272,128]{1,0:T(8,128)(2,1)S(1)}, bf16[272,128]{1,0:T(8,128)(2,1)S(1)}, u32[]{:S(2)}, u32[]{:S(2)}) collective-permute-start(bf16[272,128]{1,0:T(8,128)(2,1)S(1)} %get-tuple-element.66), channel_id=1, source_target_pairs={{4,0},{13,1},{6,2},{15,3},{8,4},{1,5},{10,6},{3,7},{12,8},{5,9},{1... | collective-permute-start | bytes 208904 | tf_op jit(solution)/shard_map/ppermute | solution.py:568
  37.0 0.8 %collective-permute-start.8 = (bf16[272,128]{1,0:T(8,128)(2,1)S(1)}, bf16[272,128]{1,0:T(8,128)(2,1)S(1)}, u32[]{:S(2)}, u32[]{:S(2)}) collective-permute-start(bf16[272,128]{1,0:T(8,128)(2,1)S(1)} %get-tuple-element.61), channel_id=1, source_target_pairs={{0,0},{9,1},{2,2},{11,3},{4,4},{13,5},{6,6},{15,7},{8,8},{1,9},{10... | collective-permute-start | bytes 208904 | tf_op jit(solution)/shard_map/ppermute | solution.py:568
  37.8 0.3 collective-permute-done.18.refs_2_
  38.1 0.7 %table.1 = (f32[8,32,128]{2,1,0:T(8,128)S(1)}, f32[8,32,128]{2,1,0:T(8,128)S(1)}, f32[8,128]{1,0:T(8,128)S(1)}) custom-call(bf16[288,128]{1,0:T(8,128)(2,1)S(1)} %get-tuple-element.46.refs_2_.refs_0_, s16[272,128]{1,0:T(8,128)(2,1)S(1)} %get-tuple-element.67.refs_1_, s16[272,128]{1,0:T(8,128)(2,1)S(1)} %collective-permute-done.18.refs_2_, ...), custom_call_target="tpu_custom_call" | custom-call | bytes 3000000 | tf_op jit(solution)/shard_map/table/pallas_call | solution.py:114
  38.8 0.1 collective-permute-start.20
  38.9 0.5 collective-permute-start.16
  39.4 1.7 %collective-permute-start.13 = (bf16[272,128]{1,0:T(8,128)(2,1)S(1)}, bf16[272,128]{1,0:T(8,128)(2,1)S(1)}, u32[]{:S(2)}, u32[]{:S(2)}) collective-permute-start(bf16[272,128]{1,0:T(8,128)(2,1)S(1)} %collective-permute-done.12.refs_5_), channel_id=1, source_target_pairs={{0,2},{1,3},{2,0},{3,1},{4,6},{5,7},{6,4},{7,5},{8,10},{9,11},{10,... | collective-permute-start | bytes 208904 | tf_op jit(solution)/shard_map/ppermute | solution.py:569
  41.1 0.4 collective-permute-start.9
  41.5 0.7 %collective-permute-start.21 = (bf16[272,128]{1,0:T(8,128)(2,1)S(1)}, bf16[272,128]{1,0:T(8,128)(2,1)S(1)}, u32[]{:S(2)}, u32[]{:S(2)}) collective-permute-start(bf16[272,128]{1,0:T(8,128)(2,1)S(1)} %get-tuple-element.78), channel_id=1, source_target_pairs={{0,0},{9,1},{2,2},{11,3},{4,4},{13,5},{6,6},{15,7},{8,8},{1,9},{10... | collective-permute-start | bytes 208904 | tf_op jit(solution)/shard_map/ppermute | solution.py:580
  42.1 3.7 %collective-permute-start.22 = (bf16[272,128]{1,0:T(8,128)(2,1)S(1)}, bf16[272,128]{1,0:T(8,128)(2,1)S(1)}, u32[]{:S(2)}, u32[]{:S(2)}) collective-permute-start(bf16[272,128]{1,0:T(8,128)(2,1)S(1)} %get-tuple-element.79), channel_id=1, source_target_pairs={{4,0},{13,1},{6,2},{15,3},{8,4},{1,5},{10,6},{3,7},{12,8},{5,9},{1... | collective-permute-start | bytes 208904 | tf_op jit(solution)/shard_map/ppermute | solution.py:580
  45.9 1.4 %collective-permute-start.14 = (bf16[272,128]{1,0:T(8,128)(2,1)S(1)}, bf16[272,128]{1,0:T(8,128)(2,1)S(1)}, u32[]{:S(2)}, u32[]{:S(2)}) collective-permute-start(bf16[272,128]{1,0:T(8,128)(2,1)S(1)} %collective-permute-done.8.refs_3_), channel_id=1, source_target_pairs={{0,1},{1,0},{2,3},{3,2},{4,5},{5,4},{6,7},{7,6},{8,9},{9,8},{10,11... | collective-permute-start | bytes 208904 | tf_op jit(solution)/shard_map/ppermute | solution.py:514
  47.3 0.1 collective-permute-start.17
  47.4 0.4 collective-permute-start.15
  47.8 0.1 collective-permute-start.23
  47.9 1.6 %collective-permute-start.24 = (bf16[272,128]{1,0:T(8,128)(2,1)S(1)}, bf16[272,128]{1,0:T(8,128)(2,1)S(1)}, u32[]{:S(2)}, u32[]{:S(2)}) collective-permute-start(bf16[272,128]{1,0:T(8,128)(2,1)S(1)} %collective-permute-done.22.refs_12_), channel_id=1, source_target_pairs={{0,1},{1,0},{2,3},{3,2},{4,5},{5,4},{6,7},{7,6},{8,9},{9,8},{10,11... | collective-permute-start | bytes 208904 | tf_op jit(solution)/shard_map/ppermute | solution.py:514
  49.5 0.9 %collective-permute-done.24.refs_14_ = bf16[272,128]{1,0:T(8,128)(2,1)S(1)} collective-permute-done((bf16[272,128]{1,0:T(8,128)(2,1)S(1)}, bf16[272,128]{1,0:T(8,128)(2,1)S(1)}, u32[]{:S(2)}, u32[]{:S(2)}) %collective-permute-start.24) | collective-permute-done | bytes 69664 | tf_op jit(solution)/shard_map/ppermute | solution.py:514
  50.4 1.8 %finish.1 = (f32[32,4096]{1,0:T(8,128)}, f32[3,3]{1,0:T(4,128)}) custom-call(bf16[256,256]{1,0:T(8,128)(2,1)S(1)} %get-tuple-element.41.refs_0_, f32[8,128]{1,0:T(8,128)S(1)} %get-tuple-element.52.refs_1_, bf16[1024,128]{1,0:T(8,128)(2,1)S(1)} %get-tuple-element.53.refs_2_, bf16[272,128]{1,0:T(8,128)(2,1)S(1)} %collective-permute-done.8.refs_3_, ...), custom_call_target="tpu_custom_call" | custom-call | bytes 6000000 | tf_op jit(solution)/shard_map/finish/pallas_call | solution.py:114
  (22 shorter events, 0.1 us)
Async XLA Ops:
  1.3 1.0 %copy-start.2 = (bf16[32,4096]{1,0:T(8,128)(2,1)S(1)}, bf16[32,4096]{1,0:T(8,128)(2,1)}, u32[]{:S(2)}) copy-start(bf16[32,4096]{1,0:T(8,128)(2,1)} %start_ref.1) | copy-start | bytes 786436
  2.3 5.5 %copy-start = (bf16[32,7,4096]{2,0,1:T(8,128)(2,1)S(1)}, bf16[32,7,4096]{2,0,1:T(8,128)(2,1)}, u32[]{:S(2)}) copy-start(bf16[32,7,4096]{2,0,1:T(8,128)(2,1)} %param.9) | copy-start | bytes 5505028
  4.0 8.4 %collective-permute-start = (bf16[288,128]{1,0:T(8,128)(2,1)S(1)}, bf16[288,128]{1,0:T(8,128)(2,1)S(1)}, u32[]{:S(2)}, u32[]{:S(2)}) collective-permute-start(bf16[288,128]{1,0:T(8,128)(2,1)S(1)} %get-tuple-element.42), channel_id=1, source_target_pairs={{0,0},{1,9},{2,2},{3,11},{4,4},{5,13},{6,6},{7,15},{8,8},{9,1},{10... | collective-permute-start | bytes 221192 | tf_op jit(solution)/shard_map/ppermute | solution.py:530
  4.7 8.1 %collective-permute-start.1 = (bf16[288,128]{1,0:T(8,128)(2,1)S(1)}, bf16[288,128]{1,0:T(8,128)(2,1)S(1)}, u32[]{:S(2)}, u32[]{:S(2)}) collective-permute-start(bf16[288,128]{1,0:T(8,128)(2,1)S(1)} %get-tuple-element.43), channel_id=1, source_target_pairs={{0,4},{1,13},{2,6},{3,15},{4,8},{5,1},{6,10},{7,3},{8,12},{9,5},{1... | collective-permute-start | bytes 221192 | tf_op jit(solution)/shard_map/ppermute | solution.py:530
  7.8 5.0 %copy-start.1 = (bf16[32,7,4096]{2,0,1:T(8,128)(2,1)S(1)}, bf16[32,7,4096]{2,0,1:T(8,128)(2,1)}, u32[]{:S(2)}) copy-start(bf16[32,7,4096]{2,0,1:T(8,128)(2,1)} %param.10) | copy-start | bytes 5505028
  9.5 5.6 %collective-permute-start.2 = (bf16[8,64,512]{2,1,0:T(8,128)(2,1)S(1)}, bf16[8,64,512]{2,1,0:T(8,128)(2,1)S(1)}, u32[]{:S(2)}, u32[]{:S(2)}) collective-permute-start(bf16[8,64,512]{2,1,0:T(8,128)(2,1)S(1)} %get-tuple-element.50), channel_id=1, source_target_pairs={{0,1},{1,0},{2,3},{3,2},{4,5},{5,4},{6,7},{7,6},{8,9},{9,8},{10,11... | collective-permute-start | bytes 1572872 | tf_op jit(solution)/shard_map/ppermute | solution.py:514
  14.2 2.0 %collective-permute-start.3 = (bf16[8,64,512]{2,1,0:T(8,128)(2,1)S(1)}, bf16[8,64,512]{2,1,0:T(8,128)(2,1)S(1)}, u32[]{:S(2)}, u32[]{:S(2)}) collective-permute-start(bf16[8,64,512]{2,1,0:T(8,128)(2,1)S(1)} %get-tuple-element.51), channel_id=1, source_target_pairs={{0,1},{1,0},{2,3},{3,2},{4,5},{5,4},{6,7},{7,6},{8,9},{9,8},{10,11... | collective-permute-start | bytes 1572872 | tf_op jit(solution)/shard_map/ppermute | solution.py:514
  14.6 4.7 %collective-permute-start.4 = (bf16[8,64,512]{2,1,0:T(8,128)(2,1)S(1)}, bf16[8,64,512]{2,1,0:T(8,128)(2,1)S(1)}, u32[]{:S(2)}, u32[]{:S(2)}) collective-permute-start(bf16[8,64,512]{2,1,0:T(8,128)(2,1)S(1)} %get-tuple-element.55), channel_id=1, source_target_pairs={{0,1},{1,0},{2,3},{3,2},{4,5},{5,4},{6,7},{7,6},{8,9},{9,8},{10,11... | collective-permute-start | bytes 1572872 | tf_op jit(solution)/shard_map/ppermute | solution.py:514
  14.8 4.5 %collective-permute-start.5 = (bf16[8,64,512]{2,1,0:T(8,128)(2,1)S(1)}, bf16[8,64,512]{2,1,0:T(8,128)(2,1)S(1)}, u32[]{:S(2)}, u32[]{:S(2)}) collective-permute-start(bf16[8,64,512]{2,1,0:T(8,128)(2,1)S(1)} %get-tuple-element.56), channel_id=1, source_target_pairs={{0,1},{1,0},{2,3},{3,2},{4,5},{5,4},{6,7},{7,6},{8,9},{9,8},{10,11... | collective-permute-start | bytes 1572872 | tf_op jit(solution)/shard_map/ppermute | solution.py:514
  17.5 4.5 %collective-permute-start.10 = (s16[272,128]{1,0:T(8,128)(2,1)S(1)}, s16[272,128]{1,0:T(8,128)(2,1)S(1)}, u32[]{:S(2)}, u32[]{:S(2)}) collective-permute-start(s16[272,128]{1,0:T(8,128)(2,1)S(1)} %get-tuple-element.62.refs_1_), channel_id=1, source_target_pairs={{0,2},{1,3},{2,0},{3,1},{4,6},{5,7},{6,4},{7,5},{8,10},{9,11},{10,... | collective-permute-start | bytes 208904 | tf_op jit(solution)/shard_map/ppermute | solution.py:556
  20.6 4.7 %collective-permute-start.6 = (s16[272,128]{1,0:T(8,128)(2,1)S(1)}, s16[272,128]{1,0:T(8,128)(2,1)S(1)}, u32[]{:S(2)}, u32[]{:S(2)}) collective-permute-start(s16[272,128]{1,0:T(8,128)(2,1)S(1)} %get-tuple-element.57.refs_1_), channel_id=1, source_target_pairs={{0,2},{1,3},{2,0},{3,1},{4,6},{5,7},{6,4},{7,5},{8,10},{9,11},{10,... | collective-permute-start | bytes 208904 | tf_op jit(solution)/shard_map/ppermute | solution.py:556
  23.7 4.4 %collective-permute-start.11 = (s16[272,128]{1,0:T(8,128)(2,1)S(1)}, s16[272,128]{1,0:T(8,128)(2,1)S(1)}, u32[]{:S(2)}, u32[]{:S(2)}) collective-permute-start(s16[272,128]{1,0:T(8,128)(2,1)S(1)} %get-tuple-element.64.refs_1_), channel_id=1, source_target_pairs={{0,2},{1,3},{2,0},{3,1},{4,6},{5,7},{6,4},{7,5},{8,10},{9,11},{10,... | collective-permute-start | bytes 208904 | tf_op jit(solution)/shard_map/ppermute | solution.py:567
  27.1 5.0 %collective-permute-start.7 = (s16[272,128]{1,0:T(8,128)(2,1)S(1)}, s16[272,128]{1,0:T(8,128)(2,1)S(1)}, u32[]{:S(2)}, u32[]{:S(2)}) collective-permute-start(s16[272,128]{1,0:T(8,128)(2,1)S(1)} %get-tuple-element.59.refs_1_), channel_id=1, source_target_pairs={{0,2},{1,3},{2,0},{3,1},{4,6},{5,7},{6,4},{7,5},{8,10},{9,11},{10,... | collective-permute-start | bytes 208904 | tf_op jit(solution)/shard_map/ppermute | solution.py:567
  29.8 8.0 %collective-permute-start.19 = (s16[272,128]{1,0:T(8,128)(2,1)S(1)}, s16[272,128]{1,0:T(8,128)(2,1)S(1)}, u32[]{:S(2)}, u32[]{:S(2)}) collective-permute-start(s16[272,128]{1,0:T(8,128)(2,1)S(1)} %get-tuple-element.71.refs_9_), channel_id=1, source_target_pairs={{0,2},{1,3},{2,0},{3,1},{4,6},{5,7},{6,4},{7,5},{8,10},{9,11},{10,... | collective-permute-start | bytes 208904 | tf_op jit(solution)/shard_map/ppermute | solution.py:567
  33.8 4.4 %collective-permute-start.18 = (s16[272,128]{1,0:T(8,128)(2,1)S(1)}, s16[272,128]{1,0:T(8,128)(2,1)S(1)}, u32[]{:S(2)}, u32[]{:S(2)}) collective-permute-start(s16[272,128]{1,0:T(8,128)(2,1)S(1)} %get-tuple-element.67.refs_1_), channel_id=1, source_target_pairs={{0,2},{1,3},{2,0},{3,1},{4,6},{5,7},{6,4},{7,5},{8,10},{9,11},{10,... | collective-permute-start | bytes 208904 | tf_op jit(solution)/shard_map/ppermute | solution.py:567
  33.8 5.1 %collective-permute-start.12 = (bf16[272,128]{1,0:T(8,128)(2,1)S(1)}, bf16[272,128]{1,0:T(8,128)(2,1)S(1)}, u32[]{:S(2)}, u32[]{:S(2)}) collective-permute-start(bf16[272,128]{1,0:T(8,128)(2,1)S(1)} %get-tuple-element.66), channel_id=1, source_target_pairs={{4,0},{13,1},{6,2},{15,3},{8,4},{1,5},{10,6},{3,7},{12,8},{5,9},{1... | collective-permute-start | bytes 208904 | tf_op jit(solution)/shard_map/ppermute | solution.py:568
  37.0 4.1 %collective-permute-start.8 = (bf16[272,128]{1,0:T(8,128)(2,1)S(1)}, bf16[272,128]{1,0:T(8,128)(2,1)S(1)}, u32[]{:S(2)}, u32[]{:S(2)}) collective-permute-start(bf16[272,128]{1,0:T(8,128)(2,1)S(1)} %get-tuple-element.61), channel_id=1, source_target_pairs={{0,0},{9,1},{2,2},{11,3},{4,4},{13,5},{6,6},{15,7},{8,8},{1,9},{10... | collective-permute-start | bytes 208904 | tf_op jit(solution)/shard_map/ppermute | solution.py:568
  38.8 2.6 %collective-permute-start.20 = (f32[8,128]{1,0:T(8,128)S(1)}, f32[8,128]{1,0:T(8,128)S(1)}, u32[]{:S(2)}, u32[]{:S(2)}) collective-permute-start(f32[8,128]{1,0:T(8,128)S(1)} %get-tuple-element.75.table_ref), channel_id=1, source_target_pairs={{0,1},{1,0},{2,3},{3,2},{4,5},{5,4},{6,7},{7,6},{8,9},{9,8},{10,11... | collective-permute-start | bytes 12296 | tf_op jit(solution)/shard_map/ppermute | solution.py:514
  38.9 6.9 %collective-permute-start.16 = (bf16[272,128]{1,0:T(8,128)(2,1)S(1)}, bf16[272,128]{1,0:T(8,128)(2,1)S(1)}, u32[]{:S(2)}, u32[]{:S(2)}) collective-permute-start(bf16[272,128]{1,0:T(8,128)(2,1)S(1)} %collective-permute-done.12.refs_5_), channel_id=1, source_target_pairs={{0,1},{1,0},{2,3},{3,2},{4,5},{5,4},{6,7},{7,6},{8,9},{9,8},{10,11... | collective-permute-start | bytes 208904 | tf_op jit(solution)/shard_map/ppermute | solution.py:514
  39.4 7.9 %collective-permute-start.13 = (bf16[272,128]{1,0:T(8,128)(2,1)S(1)}, bf16[272,128]{1,0:T(8,128)(2,1)S(1)}, u32[]{:S(2)}, u32[]{:S(2)}) collective-permute-start(bf16[272,128]{1,0:T(8,128)(2,1)S(1)} %collective-permute-done.12.refs_5_), channel_id=1, source_target_pairs={{0,2},{1,3},{2,0},{3,1},{4,6},{5,7},{6,4},{7,5},{8,10},{9,11},{10,... | collective-permute-start | bytes 208904 | tf_op jit(solution)/shard_map/ppermute | solution.py:569
  41.1 6.3 %collective-permute-start.9 = (bf16[272,128]{1,0:T(8,128)(2,1)S(1)}, bf16[272,128]{1,0:T(8,128)(2,1)S(1)}, u32[]{:S(2)}, u32[]{:S(2)}) collective-permute-start(bf16[272,128]{1,0:T(8,128)(2,1)S(1)} %collective-permute-done.8.refs_3_), channel_id=1, source_target_pairs={{0,2},{1,3},{2,0},{3,1},{4,6},{5,7},{6,4},{7,5},{8,10},{9,11},{10,... | collective-permute-start | bytes 208904 | tf_op jit(solution)/shard_map/ppermute | solution.py:569
  41.5 6.3 %collective-permute-start.21 = (bf16[272,128]{1,0:T(8,128)(2,1)S(1)}, bf16[272,128]{1,0:T(8,128)(2,1)S(1)}, u32[]{:S(2)}, u32[]{:S(2)}) collective-permute-start(bf16[272,128]{1,0:T(8,128)(2,1)S(1)} %get-tuple-element.78), channel_id=1, source_target_pairs={{0,0},{9,1},{2,2},{11,3},{4,4},{13,5},{6,6},{15,7},{8,8},{1,9},{10... | collective-permute-start | bytes 208904 | tf_op jit(solution)/shard_map/ppermute | solution.py:580
  42.1 5.7 %collective-permute-start.22 = (bf16[272,128]{1,0:T(8,128)(2,1)S(1)}, bf16[272,128]{1,0:T(8,128)(2,1)S(1)}, u32[]{:S(2)}, u32[]{:S(2)}) collective-permute-start(bf16[272,128]{1,0:T(8,128)(2,1)S(1)} %get-tuple-element.79), channel_id=1, source_target_pairs={{4,0},{13,1},{6,2},{15,3},{8,4},{1,5},{10,6},{3,7},{12,8},{5,9},{1... | collective-permute-start | bytes 208904 | tf_op jit(solution)/shard_map/ppermute | solution.py:580
  45.9 3.6 %collective-permute-start.14 = (bf16[272,128]{1,0:T(8,128)(2,1)S(1)}, bf16[272,128]{1,0:T(8,128)(2,1)S(1)}, u32[]{:S(2)}, u32[]{:S(2)}) collective-permute-start(bf16[272,128]{1,0:T(8,128)(2,1)S(1)} %collective-permute-done.8.refs_3_), channel_id=1, source_target_pairs={{0,1},{1,0},{2,3},{3,2},{4,5},{5,4},{6,7},{7,6},{8,9},{9,8},{10,11... | collective-permute-start | bytes 208904 | tf_op jit(solution)/shard_map/ppermute | solution.py:514
  47.3 2.2 %collective-permute-start.17 = (bf16[272,128]{1,0:T(8,128)(2,1)S(1)}, bf16[272,128]{1,0:T(8,128)(2,1)S(1)}, u32[]{:S(2)}, u32[]{:S(2)}) collective-permute-start(bf16[272,128]{1,0:T(8,128)(2,1)S(1)} %collective-permute-done.13.refs_6_), channel_id=1, source_target_pairs={{0,1},{1,0},{2,3},{3,2},{4,5},{5,4},{6,7},{7,6},{8,9},{9,8},{10,11... | collective-permute-start | bytes 208904 | tf_op jit(solution)/shard_map/ppermute | solution.py:514
  47.4 2.1 %collective-permute-start.15 = (bf16[272,128]{1,0:T(8,128)(2,1)S(1)}, bf16[272,128]{1,0:T(8,128)(2,1)S(1)}, u32[]{:S(2)}, u32[]{:S(2)}) collective-permute-start(bf16[272,128]{1,0:T(8,128)(2,1)S(1)} %collective-permute-done.9.refs_4_), channel_id=1, source_target_pairs={{0,1},{1,0},{2,3},{3,2},{4,5},{5,4},{6,7},{7,6},{8,9},{9,8},{10,11... | collective-permute-start | bytes 208904 | tf_op jit(solution)/shard_map/ppermute | solution.py:514
  47.8 1.7 %collective-permute-start.23 = (bf16[272,128]{1,0:T(8,128)(2,1)S(1)}, bf16[272,128]{1,0:T(8,128)(2,1)S(1)}, u32[]{:S(2)}, u32[]{:S(2)}) collective-permute-start(bf16[272,128]{1,0:T(8,128)(2,1)S(1)} %collective-permute-done.21.refs_11_), channel_id=1, source_target_pairs={{0,1},{1,0},{2,3},{3,2},{4,5},{5,4},{6,7},{7,6},{8,9},{9,8},{10,11... | collective-permute-start | bytes 208904 | tf_op jit(solution)/shard_map/ppermute | solution.py:514
  47.9 2.5 %collective-permute-start.24 = (bf16[272,128]{1,0:T(8,128)(2,1)S(1)}, bf16[272,128]{1,0:T(8,128)(2,1)S(1)}, u32[]{:S(2)}, u32[]{:S(2)}) collective-permute-start(bf16[272,128]{1,0:T(8,128)(2,1)S(1)} %collective-permute-done.22.refs_12_), channel_id=1, source_target_pairs={{0,1},{1,0},{2,3},{3,2},{4,5},{5,4},{6,7},{7,6},{8,9},{9,8},{10,11... | collective-permute-start | bytes 208904 | tf_op jit(solution)/shard_map/ppermute | solution.py:514
